TPU v7x, 32 devices: a whole 2x2x4 slice. The times are simulated.
32 devices in a mesh: phi: 16 (over z, y, core), layer: 2 (over x).
Axes of the slice: x: 2, y: 2, z: 4, core: 2. Of those that a mesh axis runs over, the one named last changes fastest.
Arguments:
- node_feats: bfloat16 [64, 1024], P(None, ('phi', 'layer')), may hold values from -6 to 6
- edge_feats: bfloat16 [64, 65536], P(None, ('phi', 'layer')), may hold values from -6 to 6
- edge_source: int32 [65536], P(('phi', 'layer')), may hold values from 0 to 111
- edge_target: int32 [65536], P(('phi', 'layer')), may hold values from 0 to 63
- edge_counts: int32 [16, 2], P('phi', 'layer'), may hold values from 256 to 2048, as said below
- rim_upper: int32 [16, 24], P('phi'), may hold values from 0 to 63, as said below
- rim_lower: int32 [16, 24], P('phi'), may hold values from 0 to 63, as said below
- edge_first: bfloat16 [64, 192], replicated, may hold values from -0.4375 to 0.4375
- edge_second: bfloat16 [64, 64], replicated, may hold values from -0.75 to 0.75
- node_first: bfloat16 [64, 128], replicated, may hold values from -0.1875 to 0.1875
- node_second: bfloat16 [64, 64], replicated, may hold values from -0.75 to 0.75
- biases: float32 [4, 64], replicated, may hold values from -3 to 3
- node_cot: float32 [64, 1024], P(None, ('phi', 'layer')), may hold values from -2 to 2
Outputs:
- node_out: bfloat16 [64, 1024], P(None, ('phi', 'layer'))
- edge_out: bfloat16 [64, 65536], P(None, ('phi', 'layer'))
- node_grad: float32 [64, 1024], P(None, ('phi', 'layer'))
- grad_edge_first: float32 [64, 192], replicated
- grad_edge_second: float32 [64, 64], replicated
- grad_node_first: float32 [64, 128], replicated
- grad_node_second: float32 [64, 64], replicated
- grad_biases: float32 [4, 64], replicated
Inputs may be any that keep to these rules, and one draw needn't show every extreme that they name: `edge_source`: columns 0 to 63 are the slab's own hits, the next 24 come from the slab below in phi and the last 24 from the slab above, on a closed loop; slots past the count hold any index. `edge_target`: a hit of the edge's own slab. `edge_counts`: slots of a device at or past this count are padding; some device is full in every draw. `rim_upper`: distinct hits of the slab within each row. `rim_lower`: distinct hits of the slab within each row.
All inputs are finite; a program needn't handle non-finite values.
Results may differ from a plain program's by a relative error of at most 0.02.
Values may be sent and summed in bfloat16 or wider, within the bound.
No kernel may reach another device: no remote copies, remote signals or barrier semaphores. Data moves between devices by JAX's collectives and lax.ppermute only.
A program may use at most 64 MiB of HBM per device.

v0:
```python
import math

import jax
import jax.numpy as jnp
from jax import lax
from jax.sharding import PartitionSpec as P

ITERS = 2


def from_behind(value, axis, steps):
    count = lax.axis_size(axis)
    pairs = [(source, (source + steps) % count) for source in range(count)]
    return lax.ppermute(value, axis, pairs)


def forward_dot(weight, data):
    return jnp.dot(weight, data, preferred_element_type=jnp.float32)


def back_dot(weight, data):
    return lax.dot_general(
        weight, data, (((0,), (0,)), ((), ())), preferred_element_type=jnp.float32
    )


def exact_back(weight, data):
    return lax.dot_general(
        weight.astype(jnp.float32),
        data,
        (((0,), (0,)), ((), ())),
        precision=lax.Precision.HIGHEST,
        preferred_element_type=jnp.float32,
    )


def outer_dot(left, right):
    return lax.dot_general(
        left, right, (((1,), (1,)), ((), ())), preferred_element_type=jnp.float32
    )


def silu_slope(value):
    logistic = jax.nn.sigmoid(value)
    return logistic * (1.0 + value * (1.0 - logistic))


def column_sums(values, index, width):
    slot_total = values.shape[1]
    block_cols = math.gcd(slot_total, 512)
    block_count = slot_total // block_cols
    positions = jnp.arange(width, dtype=jnp.int32)[:, None]

    def add_block(turn_index, running):
        first_col = turn_index * block_cols
        piece_vals = lax.dynamic_slice_in_dim(values, first_col, block_cols, 1)
        piece_index = lax.dynamic_slice_in_dim(index, first_col, block_cols, 0)
        onehot = (positions == piece_index[None, :]).astype(jnp.bfloat16)
        return running + outer_dot(piece_vals, onehot)

    return lax.fori_loop(
        0, block_count, add_block, jnp.zeros((values.shape[0], width), jnp.float32)
    )


def body(
    node_feats,
    edge_feats,
    edge_source,
    edge_target,
    edge_counts,
    rim_upper,
    rim_lower,
    edge_first,
    edge_second,
    node_first,
    node_second,
    biases,
    node_cot,
):
    latent = node_feats.shape[0]
    groups = lax.axis_size("layer")
    slab_rows = node_feats.shape[1] * groups
    rim_rows = rim_upper.shape[1]
    upper_index = rim_upper[0]
    lower_index = rim_lower[0]
    edge_valid = (jnp.arange(edge_feats.shape[1], dtype=jnp.int32) < edge_counts[0, 0]).astype(
        jnp.float32
    )
    bias_edge = biases[0][:, None]
    bias_message = biases[1][:, None]
    bias_node = biases[2][:, None]
    bias_update = biases[3][:, None]
    first_source = edge_first[:, :latent]
    first_target = edge_first[:, latent : 2 * latent]
    first_self = edge_first[:, 2 * latent :]
    ext_width = slab_rows + 2 * rim_rows
    node_state = node_feats
    edge_state = edge_feats
    stored = []
    for iteration in range(ITERS):
        slab_nodes = lax.all_gather(node_state, "layer", axis=1, tiled=True)
        from_below = from_behind(jnp.take(slab_nodes, upper_index, axis=1), "phi", 1)
        from_above = from_behind(jnp.take(slab_nodes, lower_index, axis=1), "phi", -1)
        slab_nodes, extended = (
            slab_nodes,
            jnp.concatenate([slab_nodes, from_below, from_above], axis=1),
        )
        inputs = jnp.concatenate(
            [
                jnp.take(extended, edge_source, axis=1),
                jnp.take(slab_nodes, edge_target, axis=1),
                edge_state,
            ],
            axis=0,
        )
        hidden_pre = forward_dot(edge_first, inputs) + bias_edge
        hidden = jax.nn.silu(hidden_pre).astype(jnp.bfloat16)
        new_edges = (
            edge_valid
            * (edge_state.astype(jnp.float32) + forward_dot(edge_second, hidden) + bias_message)
        ).astype(jnp.bfloat16)
        partial_value = column_sums(new_edges, edge_target, slab_rows)
        own_messages = lax.psum_scatter(
            partial_value, "layer", scatter_dimension=1, tiled=True
        ).astype(jnp.bfloat16)
        node_in = jnp.concatenate([node_state, own_messages], axis=0)
        node_pre = forward_dot(node_first, node_in) + bias_node
        node_hidden = jax.nn.silu(node_pre).astype(jnp.bfloat16)
        new_nodes = (
            node_state.astype(jnp.float32) + forward_dot(node_second, node_hidden) + bias_update
        ).astype(jnp.bfloat16)
        stored.append((inputs, hidden_pre, hidden, node_in, node_pre, node_hidden))
        node_state = new_nodes
        edge_state = new_edges
    grad_nodes = node_cot
    grad_edges = jnp.zeros(edge_feats.shape, jnp.float32)
    sum_first_edge = jnp.zeros(edge_first.shape, jnp.float32)
    sum_second_edge = jnp.zeros(edge_second.shape, jnp.float32)
    sum_first_node = jnp.zeros(node_first.shape, jnp.float32)
    sum_second_node = jnp.zeros(node_second.shape, jnp.float32)
    edge_bias = jnp.zeros((biases.shape[1],), jnp.float32)
    message_bias = jnp.zeros((biases.shape[1],), jnp.float32)
    node_bias = jnp.zeros((biases.shape[1],), jnp.float32)
    update_bias = jnp.zeros((biases.shape[1],), jnp.float32)
    for iteration in reversed(range(ITERS)):
        inputs, hidden_pre, hidden, node_in, node_pre, node_hidden = stored[iteration]
        nodes_low = grad_nodes.astype(jnp.bfloat16)
        sum_second_node = sum_second_node + outer_dot(nodes_low, node_hidden)
        update_bias = update_bias + jnp.sum(grad_nodes, axis=1)
        node_pre_grad = back_dot(node_second, nodes_low) * silu_slope(node_pre)
        node_pre_low = node_pre_grad.astype(jnp.bfloat16)
        sum_first_node = sum_first_node + outer_dot(node_pre_low, node_in)
        node_bias = node_bias + jnp.sum(node_pre_grad, axis=1)
        node_in_grad = back_dot(node_first, node_pre_low)
        message_grad = node_in_grad[latent:].astype(jnp.bfloat16)
        message_slab = lax.all_gather(message_grad, "layer", axis=1, tiled=True)
        edge_grad = edge_valid * (
            grad_edges + jnp.take(message_slab, edge_target, axis=1).astype(jnp.float32)
        )
        edge_low = edge_grad.astype(jnp.bfloat16)
        sum_second_edge = sum_second_edge + outer_dot(edge_low, hidden)
        message_bias = message_bias + jnp.sum(edge_grad, axis=1)
        pre_grad = back_dot(edge_second, edge_low) * silu_slope(hidden_pre)
        pre_low = pre_grad.astype(jnp.bfloat16)
        sum_first_edge = sum_first_edge + outer_dot(pre_low, inputs)
        edge_bias = edge_bias + jnp.sum(pre_grad, axis=1)
        grad_edges = edge_grad + back_dot(first_self, pre_low)
        source_pre = column_sums(pre_low, edge_source, ext_width)
        target_pre = column_sums(pre_low, edge_target, slab_rows)
        extended_grad = exact_back(first_source, source_pre)
        slab_grad = extended_grad[:, :slab_rows] + exact_back(first_target, target_pre)
        upper_grad = extended_grad[:, slab_rows : slab_rows + rim_rows]
        lower_grad = extended_grad[:, slab_rows + rim_rows :]
        upper_back = from_behind(upper_grad, "phi", -1)
        lower_back = from_behind(lower_grad, "phi", 1)
        slab_grad = slab_grad.at[:, upper_index].add(upper_back).at[:, lower_index].add(lower_back)
        own_grad = lax.psum_scatter(
            slab_grad.astype(jnp.bfloat16), "layer", scatter_dimension=1, tiled=True
        ).astype(jnp.float32)
        grad_nodes = grad_nodes + node_in_grad[:latent] + own_grad
    totals = lax.psum(
        (
            sum_first_edge,
            sum_second_edge,
            sum_first_node,
            sum_second_node,
            jnp.stack([edge_bias, message_bias, node_bias, update_bias]),
        ),
        ("phi", "layer"),
    )
    return (
        node_state,
        edge_state,
        grad_nodes,
        totals[0],
        totals[1],
        totals[2],
        totals[3],
        totals[4],
    )


def solution(mesh):
    return jax.shard_map(
        body,
        mesh=mesh,
        in_specs=(
            P(None, ("phi", "layer")),
            P(None, ("phi", "layer")),
            P(("phi", "layer")),
            P(("phi", "layer")),
            P("phi", "layer"),
            P("phi", None),
            P("phi", None),
            P(),
            P(),
            P(),
            P(),
            P(),
            P(None, ("phi", "layer")),
        ),
        out_specs=(
            P(None, ("phi", "layer")),
            P(None, ("phi", "layer")),
            P(None, ("phi", "layer")),
            P(),
            P(),
            P(),
            P(),
            P(),
        ),
        check_vma=False,
    )
```

profile of v0, /device:TPU:0, one launch (start us, length us, event | category | flops | bytes accessed | tf_op | source)
XLA Modules:
  0.0 309.3 jit_solution(12119545337564932954)
XLA Ops:
  8.5 5.5 %all_gather.12 = bf16[64,64]{0,1:T(8,128)(2,1)S(1)} all-gather(bf16[64,32]{0,1:T(8,128)(2,1)} %param.31), channel_id=1, replica_groups=mesh['phi'=16,'layer'=2] {'layer'}, dimensions={1}, use_global_device_ids=true | all-gather | bytes 12288 | tf_op jit(solution)/shard_map/all_gather | solution.py:102
  16.7 4.4 %collective-permute-start.1 = (bf16[64,24]{0,1:T(8,128)(2,1)S(1)}, bf16[64,24]{0,1:T(8,128)(2,1)S(1)}, u32[]{:S(2)}, u32[]{:S(2)}) collective-permute-start(bf16[64,24]{0,1:T(8,128)(2,1)S(1)} %select_bitcast_fusion.6), channel_id=1, source_target_pairs={{0,30},{2,0},{4,2},{6,4},{8,6},{10,8},{12,10},{14,12},{16,14},{18,... | collective-permute-start | bytes 9224 | tf_op jit(solution)/shard_map/ppermute | solution.py:14
  24.0 6.2 %gather_fusion.3 = bf16[2048,64]{1,0:T(8,128)(2,1)S(1)} fusion(bf16[64,64]{0,1:T(8,128)(2,1)S(1)} %all_gather.12, s32[2048]{0:T(1024)S(1)} %fusion.75), kind=kCustom, calls=%fused_computation.2.clone | custom fusion | bytes 532480 | tf_op jit(solution)/shard_map/jit(_take)/gather | solution.py:112
  32.1 6.2 %gather_fusion.2 = bf16[2048,64]{1,0:T(8,128)(2,1)S(1)} fusion(bf16[64,112]{0,1:T(8,128)(2,1)S(1)} %pad_maximum_fusion.6, s32[2048]{0:T(1024)S(1)} %fusion.74), kind=kCustom, calls=%fused_computation.1.clone | custom fusion | bytes 532480 | tf_op jit(solution)/shard_map/jit(_take)/gather | solution.py:111
  40.6 1.1 while.84
  42.5 8.9 %reduce-scatter.13.cloned.1.call-done = f32[32,64]{1,0:T(8,128)} async-done(((f32[64,64]{1,0:T(8,128)}), f32[32,64]{1,0:T(8,128)}) %reduce-scatter.13.cloned.1.call-update) | async-done | bytes 8208
  52.5 4.4 %all_gather.13 = bf16[64,64]{0,1:T(8,128)(2,1)S(1)} all-gather(bf16[64,32]{0,1:T(8,128)(2,1)S(1)} %fusion.54), channel_id=1, replica_groups=mesh['phi'=16,'layer'=2] {'layer'}, dimensions={1}, use_global_device_ids=true | all-gather | bytes 12288 | tf_op jit(solution)/shard_map/all_gather | solution.py:102
  58.2 4.4 %collective-permute-start.3 = (bf16[64,24]{0,1:T(8,128)(2,1)S(1)}, bf16[64,24]{0,1:T(8,128)(2,1)S(1)}, u32[]{:S(2)}, u32[]{:S(2)}) collective-permute-start(bf16[64,24]{0,1:T(8,128)(2,1)S(1)} %select_bitcast_fusion.4), channel_id=1, source_target_pairs={{0,30},{2,0},{4,2},{6,4},{8,6},{10,8},{12,10},{14,12},{16,14},{18,... | collective-permute-start | bytes 9224 | tf_op jit(solution)/shard_map/ppermute | solution.py:14
  63.2 6.2 %gather_fusion.7 = bf16[2048,64]{1,0:T(8,128)(2,1)S(1)} fusion(bf16[64,64]{0,1:T(8,128)(2,1)S(1)} %all_gather.13, s32[2048]{0:T(1024)S(1)} %fusion.75), kind=kCustom, calls=%fused_computation.7.clone | custom fusion | bytes 532480 | tf_op jit(solution)/shard_map/jit(_take)/gather | solution.py:112
  69.6 6.2 %gather_fusion.6 = bf16[2048,64]{1,0:T(8,128)(2,1)S(1)} fusion(bf16[64,112]{0,1:T(8,128)(2,1)S(1)} %pad_maximum_fusion.7, s32[2048]{0:T(1024)S(1)} %fusion.74), kind=kCustom, calls=%fused_computation.6.clone | custom fusion | bytes 532480 | tf_op jit(solution)/shard_map/jit(_take)/gather | solution.py:111
  76.7 1.1 multiply_convert_fusion
  78.0 1.1 while.85
  80.5 6.7 %reduce-scatter.7.cloned.1.call-done = f32[64,32]{0,1:T(8,128)} async-done(((f32[64,64]{0,1:T(8,128)}), f32[64,32]{0,1:T(8,128)}) %reduce-scatter.7.cloned.1.call-update) | async-done | bytes 8208 | tf_op jit(solution)/shard_map/reduce_scatter | solution.py:124
  88.7 0.8 convolution_bitcast_fusion.5
  89.5 0.7 fusion.55
  91.1 4.4 %all_gather.14 = bf16[64,64]{0,1:T(8,128)(2,1)S(1)} all-gather(bf16[64,32]{0,1:T(8,128)(2,1)S(1)} %slice.125), channel_id=1, replica_groups=mesh['phi'=16,'layer'=2] {'layer'}, dimensions={1}, use_global_device_ids=true | all-gather | bytes 12288 | tf_op jit(solution)/shard_map/all_gather | solution.py:157
  95.4 6.2 %gather_fusion.8 = bf16[2048,64]{1,0:T(8,128)(2,1)S(1)} fusion(bf16[64,64]{0,1:T(8,128)(2,1)S(1)} %all_gather.14, s32[2048]{0:T(1024)S(1)} %fusion.75), kind=kCustom, calls=%fused_computation.8.clone | custom fusion | bytes 532480 | tf_op jit(solution)/shard_map/jit(_take)/gather | solution.py:159
  101.9 1.6 fusion.58
  103.5 1.0 fusion.100
  104.5 1.1 while.86
  106.0 2.1 collective-permute-start.4
  108.1 1.1 while.87
  109.6 0.8 fusion.80
  110.5 5.0 %collective-permute-done.5 = f32[64,24]{1,0:T(8,128)S(1)} collective-permute-done((f32[64,24]{1,0:T(8,128)S(1)}, f32[64,24]{1,0:T(8,128)S(1)}, u32[]{:S(2)}, u32[]{:S(2)}) %collective-permute-start.5) | collective-permute-done | bytes 6176 | tf_op jit(solution)/shard_map/ppermute | solution.py:14
  115.6 0.7 scatter_fusion
  116.4 0.7 scatter_fusion.1
  118.6 5.5 %reduce-scatter.9.cloned.1.call-done = bf16[64,32]{0,1:T(8,128)(2,1)} async-done(((bf16[64,64]{0,1:T(8,128)(2,1)}), bf16[64,32]{0,1:T(8,128)(2,1)}) %reduce-scatter.9.cloned.1.call-update) | async-done | bytes 4112 | tf_op jit(solution)/shard_map/reduce_scatter | solution.py:178
  124.1 1.3 fusion.97
  127.4 4.4 %all_gather.15 = bf16[64,64]{0,1:T(8,128)(2,1)S(1)} all-gather(bf16[64,32]{0,1:T(8,128)(2,1)S(1)} %slice.124), channel_id=1, replica_groups=mesh['phi'=16,'layer'=2] {'layer'}, dimensions={1}, use_global_device_ids=true | all-gather | bytes 12288 | tf_op jit(solution)/shard_map/all_gather | solution.py:157
  131.7 6.2 %gather_fusion.9 = bf16[2048,64]{1,0:T(8,128)(2,1)S(1)} fusion(bf16[64,64]{0,1:T(8,128)(2,1)S(1)} %all_gather.15, s32[2048]{0:T(1024)S(1)} %fusion.75), kind=kCustom, calls=%fused_computation.9.clone | custom fusion | bytes 532480 | tf_op jit(solution)/shard_map/jit(_take)/gather | solution.py:159
  140.4 0.8 convolution_add_fusion.9
  141.3 0.8 convolution_add_fusion.10
  142.1 0.9 convolution_add_fusion.11
  143.9 1.0 convolution_add_fusion.8
  145.0 1.1 while.88
  146.4 2.1 collective-permute-start.6
  148.6 1.1 while.89
  150.2 5.8 %collective-permute-done.7 = f32[64,24]{1,0:T(8,128)S(1)} collective-permute-done((f32[64,24]{1,0:T(8,128)S(1)}, f32[64,24]{1,0:T(8,128)S(1)}, u32[]{:S(2)}, u32[]{:S(2)}) %collective-permute-start.7) | collective-permute-done | bytes 6176 | tf_op jit(solution)/shard_map/ppermute | solution.py:14
  156.1 0.7 scatter_fusion.2
  156.8 0.7 scatter_fusion.3
  158.9 5.6 %reduce-scatter.11.cloned.1.call-done = bf16[64,32]{0,1:T(8,128)(2,1)} async-done(((bf16[64,64]{0,1:T(8,128)(2,1)}), bf16[64,32]{0,1:T(8,128)(2,1)}) %reduce-scatter.11.cloned.1.call-update) | async-done | bytes 4112 | tf_op jit(solution)/shard_map/reduce_scatter | solution.py:178
  164.5 1.3 fusion.66
  165.8 130.0 %all-reduce.3.cloned.1.call-done = (f32[64,192]{1,0:T(8,128)}, f32[64,64]{1,0:T(8,128)}, f32[64,128]{1,0:T(8,128)}, f32[64,64]{0,1:T(8,128)}, f32[4,64]{1,0:T(4,128)}) async-done(((f32[64,192]{1,0:T(8,128)}, f32[64,64]{1,0:T(8,128)}, f32[64,128]{1,0:T(8,128)}, f32[64,64]{0,1:T(8,128)}, f32[4,64]{1,0:T(4,128)}), (f32[64,192]{1,0:T(8,128)}, f32[64,64]{1,0:T(8,128)}, f32[64,128]{1,0:T(8,128)}, ...) | async-done | bytes 115728 | tf_op jit(solution)/shard_map/psum | solution.py:182
  295.8 1.5 copy.71
  297.3 1.5 copy.123
  298.7 1.4 copy.124
  300.1 1.4 copy.125
  301.5 1.3 copy.126
  (273 shorter events, 35.0 us)
Async XLA Ops:
  7.2 32.6 %copy-start = (bf16[64,64]{1,0:T(8,128)(2,1)S(1)}, bf16[64,64]{1,0:T(8,128)(2,1)}, u32[]{:S(2)}) copy-start(bf16[64,64]{1,0:T(8,128)(2,1)} %param.39) | copy-start | bytes 24580
  7.2 44.2 %reduce-scatter.13.cloned.1.call-start = ((), (), s32[]{:S(2)}) async-start(), calls=%async_computation.7 | async-start | bytes 49152
  14.7 17.4 %collective-permute-start = (bf16[64,24]{0,1:T(8,128)(2,1)S(1)}, bf16[64,24]{0,1:T(8,128)(2,1)S(1)}, u32[]{:S(2)}, u32[]{:S(2)}) collective-permute-start(bf16[64,24]{0,1:T(8,128)(2,1)S(1)} %select_bitcast_fusion.7), channel_id=1, source_target_pairs={{0,2},{2,4},{4,6},{6,8},{8,10},{10,12},{12,14},{14,16},{16,18},{18... | collective-permute-start | bytes 9224 | tf_op jit(solution)/shard_map/ppermute | solution.py:14
  16.7 15.4 %collective-permute-start.1 = (bf16[64,24]{0,1:T(8,128)(2,1)S(1)}, bf16[64,24]{0,1:T(8,128)(2,1)S(1)}, u32[]{:S(2)}, u32[]{:S(2)}) collective-permute-start(bf16[64,24]{0,1:T(8,128)(2,1)S(1)} %select_bitcast_fusion.6), channel_id=1, source_target_pairs={{0,30},{2,0},{4,2},{6,4},{8,6},{10,8},{12,10},{14,12},{16,14},{18,... | collective-permute-start | bytes 9224 | tf_op jit(solution)/shard_map/ppermute | solution.py:14
  24.0 52.0 %copy-start.28 = (pred[2048]{0:T(1024)(128)(4,1)}, pred[2048]{0:T(1024)(128)(4,1)S(1)}, u32[]{:S(2)}) copy-start(pred[2048]{0:T(1024)(128)(4,1)S(1)} %compare_and_fusion) | copy-start | bytes 6148
  24.0 6.2 %copy-start.44 = (f32[4,64]{1,0:T(4,128)S(1)}, f32[4,64]{1,0:T(4,128)}, u32[]{:S(2)}) copy-start(f32[4,64]{1,0:T(4,128)} %param.42) | copy-start | bytes 3076
  30.2 8.5 %copy-start.50 = (f32[64]{0:T(128)}, f32[64]{0:T(128)S(1)}, u32[]{:S(2)}) copy-start(f32[64]{0:T(128)S(1)} %get-tuple-element.771) | copy-start | bytes 772
  30.2 22.1 %copy-start.48 = (f32[64]{0:T(128)}, f32[64]{0:T(128)S(1)}, u32[]{:S(2)}) copy-start(f32[64]{0:T(128)S(1)} %get-tuple-element.773) | copy-start | bytes 772
  31.2 46.5 %copy-start.14 = (f32[2048]{0:T(1024)}, f32[2048]{0:T(1024)S(1)}, u32[]{:S(2)}) copy-start(f32[2048]{0:T(1024)S(1)} %fusion.73) | copy-start | bytes 24580
  40.6 11.6 %copy-start.4 = (bf16[64,128]{1,0:T(8,128)(2,1)S(1)}, bf16[64,128]{1,0:T(8,128)(2,1)}, u32[]{:S(2)}) copy-start(bf16[64,128]{1,0:T(8,128)(2,1)} %param.40) | copy-start | bytes 49156
  40.6 11.6 %copy-start.21 = (bf16[64,32]{0,1:T(8,128)(2,1)S(1)}, bf16[64,32]{0,1:T(8,128)(2,1)}, u32[]{:S(2)}) copy-start(bf16[64,32]{0,1:T(8,128)(2,1)} %param.31) | copy-start | bytes 12292
  40.6 11.8 %copy-start.52 = (bf16[64,64]{1,0:T(8,128)(2,1)S(1)}, bf16[64,64]{1,0:T(8,128)(2,1)}, u32[]{:S(2)}) copy-start(bf16[64,64]{1,0:T(8,128)(2,1)} %param.41) | copy-start | bytes 24580
  41.7 20.9 %copy-start.55 = (s32[1,24]{1,0:T(1,128)S(1)}, s32[1,24]{1,0:T(1,128)}, u32[]{:S(2)}) copy-start(s32[1,24]{1,0:T(1,128)} %param.36) | copy-start | bytes 292
  42.4 44.7 %reduce-scatter.7.cloned.1.call-start = ((), (), s32[]{:S(2)}) async-start(), calls=%async_computation.4 | async-start | bytes 49152 | tf_op jit(solution)/shard_map/reduce_scatter | solution.py:124
  52.1 17.2 %copy-start.23 = (bf16[64,32]{0,1:T(8,128)(2,1)}, bf16[64,32]{0,1:T(8,128)(2,1)S(1)}, u32[]{:S(2)}) copy-start(bf16[64,32]{0,1:T(8,128)(2,1)S(1)} %bitcast_convert_fusion) | copy-start | bytes 12292
  52.3 17.0 %copy-start.25 = (f32[64,32]{0,1:T(8,128)}, f32[64,32]{0,1:T(8,128)S(1)}, u32[]{:S(2)}) copy-start(f32[64,32]{0,1:T(8,128)S(1)} %fusion.53) | copy-start | bytes 24580
  52.5 37.0 %copy-start.17 = (bf16[64,32]{0,1:T(8,128)(2,1)}, bf16[64,32]{0,1:T(8,128)(2,1)S(1)}, u32[]{:S(2)}) copy-start(bf16[64,32]{0,1:T(8,128)(2,1)S(1)} %fusion.54) | copy-start | bytes 12292
  58.1 11.5 %collective-permute-start.2 = (bf16[64,24]{0,1:T(8,128)(2,1)S(1)}, bf16[64,24]{0,1:T(8,128)(2,1)S(1)}, u32[]{:S(2)}, u32[]{:S(2)}) collective-permute-start(bf16[64,24]{0,1:T(8,128)(2,1)S(1)} %select_bitcast_fusion.5), channel_id=1, source_target_pairs={{0,2},{2,4},{4,6},{6,8},{8,10},{10,12},{12,14},{14,16},{16,18},{18... | collective-permute-start | bytes 9224 | tf_op jit(solution)/shard_map/ppermute | solution.py:14
  58.2 11.4 %collective-permute-start.3 = (bf16[64,24]{0,1:T(8,128)(2,1)S(1)}, bf16[64,24]{0,1:T(8,128)(2,1)S(1)}, u32[]{:S(2)}, u32[]{:S(2)}) collective-permute-start(bf16[64,24]{0,1:T(8,128)(2,1)S(1)} %select_bitcast_fusion.4), channel_id=1, source_target_pairs={{0,30},{2,0},{4,2},{6,4},{8,6},{10,8},{12,10},{14,12},{16,14},{18,... | collective-permute-start | bytes 9224 | tf_op jit(solution)/shard_map/ppermute | solution.py:14
  78.0 10.1 %copy-start.38 = (f32[64,32]{0,1:T(8,128)S(1)}, f32[64,32]{0,1:T(8,128)}, u32[]{:S(2)}) copy-start(f32[64,32]{0,1:T(8,128)} %param.43) | copy-start | bytes 24580
  78.0 10.1 %copy-start.53 = (bf16[64,64]{1,0:T(8,128)(2,1)S(1)}, bf16[64,64]{1,0:T(8,128)(2,1)}, u32[]{:S(2)}) copy-start(bf16[64,64]{1,0:T(8,128)(2,1)} %param.41) | copy-start | bytes 24580
  78.0 11.5 %copy-start.49 = (f32[64]{0:T(128)S(1)}, f32[64]{0:T(128)}, u32[]{:S(2)}) copy-start(f32[64]{0:T(128)} %copy-done.48) | copy-start | bytes 772
  79.1 22.5 %copy-start.1 = (bf16[64,2048]{1,0:T(8,128)(2,1)}, bf16[64,2048]{1,0:T(8,128)(2,1)S(1)}, u32[]{:S(2)}) copy-start(bf16[64,2048]{1,0:T(8,128)(2,1)S(1)} %get-tuple-element.1109) | copy-start | bytes 786436
  79.9 44.2 %reduce-scatter.9.cloned.1.call-start = ((), (), s32[]{:S(2)}) async-start(), calls=%async_computation.5 | async-start | bytes 24576 | tf_op jit(solution)/shard_map/reduce_scatter | solution.py:178
  106.0 3.6 %copy-start.18 = (bf16[64,32]{0,1:T(8,128)(2,1)S(1)}, bf16[64,32]{0,1:T(8,128)(2,1)}, u32[]{:S(2)}) copy-start(bf16[64,32]{0,1:T(8,128)(2,1)} %copy-done.17) | copy-start | bytes 12292
  106.0 3.6 %copy-start.20 = (bf16[64,32]{0,1:T(8,128)(2,1)S(1)}, bf16[64,32]{0,1:T(8,128)(2,1)}, u32[]{:S(2)}) copy-start(bf16[64,32]{0,1:T(8,128)(2,1)} %copy-done.19) | copy-start | bytes 12292
  106.0 3.6 %copy-start.33 = (bf16[64,32]{0,1:T(8,128)(2,1)S(1)}, bf16[64,32]{0,1:T(8,128)(2,1)}, u32[]{:S(2)}) copy-start(bf16[64,32]{0,1:T(8,128)(2,1)} %copy-done.32) | copy-start | bytes 12292
  106.0 4.5 %collective-permute-start.4 = (f32[64,24]{1,0:T(8,128)S(1)}, f32[64,24]{1,0:T(8,128)S(1)}, u32[]{:S(2)}, u32[]{:S(2)}) collective-permute-start(f32[64,24]{1,0:T(8,128)S(1)} %get-tuple-element.769), channel_id=1, source_target_pairs={{0,30},{2,0},{4,2},{6,4},{8,6},{10,8},{12,10},{14,12},{16,14},{18,... | collective-permute-start | bytes 18440 | tf_op jit(solution)/shard_map/ppermute | solution.py:14
  108.1 7.5 %copy-start.40 = (s32[24]{0:T(128)S(1)}, s32[24]{0:T(128)}, u32[]{:S(2)}) copy-start(s32[24]{0:T(128)} %fusion.85) | copy-start | bytes 292
  109.2 7.2 %copy-start.42 = (s32[24]{0:T(128)S(1)}, s32[24]{0:T(128)}, u32[]{:S(2)}) copy-start(s32[24]{0:T(128)} %fusion.86) | copy-start | bytes 292
  109.5 6.1 %collective-permute-start.5 = (f32[64,24]{1,0:T(8,128)S(1)}, f32[64,24]{1,0:T(8,128)S(1)}, u32[]{:S(2)}, u32[]{:S(2)}) collective-permute-start(f32[64,24]{1,0:T(8,128)S(1)} %get-tuple-element.768), channel_id=1, source_target_pairs={{0,2},{2,4},{4,6},{6,8},{8,10},{10,12},{12,14},{14,16},{16,18},{18... | collective-permute-start | bytes 18440 | tf_op jit(solution)/shard_map/ppermute | solution.py:14
  116.4 7.7 %copy-start.13 = (f32[128,32]{0,1:T(8,128)S(1)}, f32[128,32]{0,1:T(8,128)}, u32[]{:S(2)}) copy-start(f32[128,32]{0,1:T(8,128)} %copy-done.12) | copy-start | bytes 49156
  116.4 7.7 %copy-start.39 = (f32[64,32]{0,1:T(8,128)S(1)}, f32[64,32]{0,1:T(8,128)}, u32[]{:S(2)}) copy-start(f32[64,32]{0,1:T(8,128)} %param.43) | copy-start | bytes 24580
  116.4 8.9 %copy-start.26 = (f32[64,32]{0,1:T(8,128)S(1)}, f32[64,32]{0,1:T(8,128)}, u32[]{:S(2)}) copy-start(f32[64,32]{0,1:T(8,128)} %copy-done.25) | copy-start | bytes 24580
  116.4 8.9 %copy-start.54 = (bf16[64,64]{1,0:T(8,128)(2,1)S(1)}, bf16[64,64]{1,0:T(8,128)(2,1)}, u32[]{:S(2)}) copy-start(bf16[64,64]{1,0:T(8,128)(2,1)} %param.41) | copy-start | bytes 24580
  117.8 46.6 %reduce-scatter.11.cloned.1.call-start = ((), (), s32[]{:S(2)}) async-start(), calls=%async_computation.6 | async-start | bytes 24576 | tf_op jit(solution)/shard_map/reduce_scatter | solution.py:178
  146.4 3.6 %copy-start.58 = (f32[64]{0:T(128)S(1)}, f32[64]{0:T(128)}, u32[]{:S(2)}) copy-start(f32[64]{0:T(128)} %get-tuple-element.764) | copy-start | bytes 772
  146.4 3.6 %copy-start.47 = (f32[64]{0:T(128)S(1)}, f32[64]{0:T(128)}, u32[]{:S(2)}) copy-start(f32[64]{0:T(128)} %fusion.56) | copy-start | bytes 772
  146.4 3.6 %copy-start.57 = (f32[64]{0:T(128)S(1)}, f32[64]{0:T(128)}, u32[]{:S(2)}) copy-start(f32[64]{0:T(128)} %get-tuple-element.779) | copy-start | bytes 772
  146.4 3.6 %copy-start.59 = (f32[64]{0:T(128)S(1)}, f32[64]{0:T(128)}, u32[]{:S(2)}) copy-start(f32[64]{0:T(128)} %get-tuple-element.781) | copy-start | bytes 772
  146.4 3.6 %copy-start.45 = (f32[64]{0:T(128)S(1)}, f32[64]{0:T(128)}, u32[]{:S(2)}) copy-start(f32[64]{0:T(128)} %get-tuple-element.760) | copy-start | bytes 772
  146.4 3.6 %copy-start.46 = (f32[64]{0:T(128)S(1)}, f32[64]{0:T(128)}, u32[]{:S(2)}) copy-start(f32[64]{0:T(128)} %get-tuple-element.770) | copy-start | bytes 772
  146.4 3.7 %collective-permute-start.6 = (f32[64,24]{1,0:T(8,128)S(1)}, f32[64,24]{1,0:T(8,128)S(1)}, u32[]{:S(2)}, u32[]{:S(2)}) collective-permute-start(f32[64,24]{1,0:T(8,128)S(1)} %get-tuple-element.767), channel_id=1, source_target_pairs={{0,30},{2,0},{4,2},{6,4},{8,6},{10,8},{12,10},{14,12},{16,14},{18,... | collective-permute-start | bytes 18440 | tf_op jit(solution)/shard_map/ppermute | solution.py:14
  148.6 7.5 %copy-start.41 = (s32[24]{0:T(128)S(1)}, s32[24]{0:T(128)}, u32[]{:S(2)}) copy-start(s32[24]{0:T(128)} %fusion.85) | copy-start | bytes 292
  149.6 7.2 %copy-start.43 = (s32[24]{0:T(128)S(1)}, s32[24]{0:T(128)}, u32[]{:S(2)}) copy-start(s32[24]{0:T(128)} %fusion.86) | copy-start | bytes 292
  149.9 6.1 %collective-permute-start.7 = (f32[64,24]{1,0:T(8,128)S(1)}, f32[64,24]{1,0:T(8,128)S(1)}, u32[]{:S(2)}, u32[]{:S(2)}) collective-permute-start(f32[64,24]{1,0:T(8,128)S(1)} %get-tuple-element.766), channel_id=1, source_target_pairs={{0,2},{2,4},{4,6},{6,8},{8,10},{10,12},{12,14},{14,16},{16,18},{18... | collective-permute-start | bytes 18440 | tf_op jit(solution)/shard_map/ppermute | solution.py:14
  156.8 7.6 %copy-start.11 = (f32[128,32]{0,1:T(8,128)S(1)}, f32[128,32]{0,1:T(8,128)}, u32[]{:S(2)}) copy-start(f32[128,32]{0,1:T(8,128)} %copy-done.10) | copy-start | bytes 49156
  158.2 137.6 %all-reduce.3.cloned.1.call-start = ((), (), s32[]{:S(2)}) async-start(), calls=%async_computation.8 | async-start | bytes 331776 | tf_op jit(solution)/shard_map/psum | solution.py:182
  (29 other events, 36.5 us)
Sparse Core Ops, SparseCore 0:
  42.6 8.8 reduce-scatter.12
  80.0 7.1 reduce-scatter.6
  118.0 6.0 reduce-scatter.8
  158.3 6.0 reduce-scatter.10
  171.3 124.4 all-reduce.2
where the time goes:
time: 311 us; the launch traced here: 309 us
  waiting for transfers between devices  168 us (54%)
  local copies, waits for them, and re-layouts  57.1 us (18%)
  matrix products  19.5 us (6%)
  blocking collectives  18.6 us (6%)
  other arithmetic  17.1 us (5%)
  between operations  15.4 us (5%)
  starting transfers between devices  13.4 us (4%)
    psum x1, waiting for transfers between devices, body(): lax.psum((sum_first_edge, sum_second_edge, sum_first_node, sum_second_nod...  130 us
    unnamed x135, local copies, waits for them, and re-layouts  13.6 us
    ppermute x8, starting transfers between devices, from_behind(): return lax.ppermute(value, axis, pairs)  13.2 us
    gather x4, local copies, waits for them, and re-layouts, body(): jnp.take(message_slab, edge_target, axis=1).astype(jnp.float32)  12.8 us
    gather x3, local copies, waits for them, and re-layouts, body(): jnp.take(extended, edge_source, axis=1)  12.6 us
    gather x3, local copies, waits for them, and re-layouts, body(): jnp.take(slab_nodes, edge_target, axis=1)  12.6 us
    dot_general x32, matrix products, outer_dot(): lax.dot_general(left, right, (((1,), (1,)), ((), ())), preferred_element_...  11.6 us
    reduce_scatter x2, waiting for transfers between devices, body(): lax.psum_scatter(slab_grad.astype(jnp.bfloat16), 'layer', scatter_dimensi...  11 us
  transfers between devices with their start and end apart: 13, of which 7 were waited for; matrix products, arithmetic and copies ran while one was open for 8% of the time, Pallas kernels for 0%

commit v1 on v0

v1 whole, which is shorter than its diff:
```python
import functools
import math

import jax
import jax.numpy as jnp
from jax import lax
from jax.experimental import pallas as pl
from jax.experimental.pallas import tpu as pltpu
from jax.sharding import PartitionSpec as P

BF = jnp.bfloat16
F32 = jnp.float32
CHUNK = 512
LANES = 128
HBM = pltpu.HBM
VM = pltpu.VMEM


def mm(left, right):
    return jnp.dot(left, right, preferred_element_type=F32)


def mm_nt(left, right):
    return lax.dot_general(left, right, (((1,), (1,)), ((), ())), preferred_element_type=F32)


def flip(weight):
    return weight.astype(F32).T.astype(BF)


def halves(value):
    high = value.astype(BF)
    return high, (value - high.astype(F32)).astype(BF)


def wide_mm(weight, value):
    high, low = halves(value)
    return mm(jnp.concatenate([weight, weight], axis=1), jnp.concatenate([high, low], axis=0))


def gather_mm(table, onehot):
    high, low = halves(table)
    return mm(jnp.concatenate([high, low], axis=1), jnp.concatenate([onehot, onehot], axis=0))


def sigmoid(value):
    return 0.5 + 0.5 * jnp.tanh(0.5 * value)


def add_to(total, value):
    return value if total is None else total + value


def chunks_of(count):
    return [slice(first, first + CHUNK) for first in range(0, count, CHUNK)]


def is_even():
    return lax.rem(lax.axis_index("phi"), 2) == 0


def pick(parts, natural):
    groups = len(parts)
    turn = lax.rem(lax.axis_index("layer") - natural + groups, groups)
    value = parts[0]
    for rank in range(1, groups):
        value = jnp.where(turn == rank, parts[rank], value)
    return value


def own_rows(slab_rows, width):
    layer = lax.axis_index("layer")
    value = slab_rows[:width]
    for rank in range(1, slab_rows.shape[0] // width):
        value = jnp.where(layer == rank, slab_rows[rank * width : (rank + 1) * width], value)
    return value


def rim_payloads(slab16, upper_ref, lower_ref, alpha_ref, beta_ref):
    upper = mm(slab16, upper_ref[...])
    lower = mm(slab16, lower_ref[...])
    even = is_even()
    alpha_ref[...] = jnp.where(even, upper, lower).astype(BF)
    beta_ref[...] = jnp.where(even, lower, upper).astype(BF)


def rim_columns(alpha, beta, room):
    even = is_even()
    below = jnp.where(even, beta, alpha)
    above = jnp.where(even, alpha, beta)
    pad = jnp.zeros((below.shape[0], room - 2 * below.shape[1]), F32)
    return jnp.concatenate([below, above, pad], axis=1).astype(BF)


def placed_rims(alpha, beta, upper_ref, lower_ref):
    even = is_even()
    from_upper = jnp.where(even, alpha, beta).astype(BF)
    from_lower = jnp.where(even, beta, alpha).astype(BF)
    return mm_nt(from_upper, upper_ref[...]) + mm_nt(from_lower, lower_ref[...])


def rim_gradients(ext_grad, slab, rim):
    even = is_even()
    below = ext_grad[:, slab : slab + rim]
    above = ext_grad[:, slab + rim : slab + 2 * rim]
    return jnp.where(even, above, below), jnp.where(even, below, above)


def slope_parts(pre):
    logistic = sigmoid(pre)
    value = pre * logistic
    return value, logistic + value * (1.0 - logistic)


def activate(base_ref, rim_table, onehot_ref, slab, hidden_ref, slope_ref):
    wide = onehot_ref.shape[0] - slab
    high, low = halves(rim_table)
    table = jnp.concatenate([high, low], axis=1)
    total = None
    for cols in chunks_of(base_ref.shape[1]):
        rims = onehot_ref[slab:wide, cols]
        pre = base_ref[:, cols] + mm(table, jnp.concatenate([rims, rims], axis=0))
        value, slope = slope_parts(pre)
        hidden = value.astype(BF)
        hidden_ref[:, cols] = hidden
        slope_ref[:, cols] = slope
        total = add_to(total, mm_nt(hidden, onehot_ref[wide:, cols]))
    return total


def slab_base(first_ref, slab16, bias, onehot_ref, edges_of, base_ref):
    latent, slab = slab16.shape
    wide = onehot_ref.shape[0] - slab
    source = halves(mm(first_ref[:, :latent], slab16))
    target = halves(mm(first_ref[:, latent : 2 * latent], slab16))
    own = first_ref[:, 2 * latent :]
    table = jnp.concatenate([*source, *target, own], axis=1)
    for cols in chunks_of(base_ref.shape[1]):
        near = onehot_ref[:slab, cols]
        hit = onehot_ref[wide:, cols]
        stack = jnp.concatenate([near, near, hit, hit, edges_of(cols)], axis=0)
        base_ref[:, cols] = mm(table, stack) + bias[:, 0:1]


def node_backward(grad, pre, first_back_ref, second_back_ref):
    latent = grad.shape[0]
    pre_grad = mm(second_back_ref[...], grad.astype(BF)) * slope_parts(pre)[1]
    back = mm(first_back_ref[...], pre_grad.astype(BF))
    return pre_grad, back[:latent], back[latent:].astype(BF)


def node_sums(grad, pre_grad, joined, hidden):
    return (
        mm_nt(pre_grad.astype(BF), joined),
        mm_nt(grad.astype(BF), hidden),
        jnp.sum(pre_grad, axis=1, keepdims=True),
        jnp.sum(grad, axis=1, keepdims=True),
    )


def table_grads(first_back_ref, sums, slab, wide):
    latent = sums.shape[0]
    ext_grad = mm(first_back_ref[:latent], sums[:, :wide].astype(BF))
    target = mm(first_back_ref[latent : 2 * latent], sums[:, wide : wide + slab].astype(BF))
    return ext_grad, ext_grad[:, :slab] + target


def first_total(sums, slab16, rims16, slab, wide):
    source = sums[:, :wide].astype(BF)
    target = sums[:, wide : wide + slab].astype(BF)
    ext16 = jnp.concatenate([slab16, rims16], axis=1)
    return jnp.concatenate(
        [mm_nt(source, ext16), mm_nt(target, slab16), sums[:, wide + slab :]], axis=1
    )


def prep_kernel(count_ref, source_hbm, target_hbm, feats_hbm, cot_hbm, upper_hbm, lower_hbm,
                out_ref, upper_ref, lower_ref,
                source, target, feats, cot, upper, lower, sems):
    pairs = ((source_hbm, source), (target_hbm, target), (feats_hbm, feats), (cot_hbm, cot),
             (upper_hbm, upper), (lower_hbm, lower))
    copies = [pltpu.make_async_copy(a, b, sems.at[place]) for place, (a, b) in enumerate(pairs)]
    for copy in copies:
        copy.start()
    for copy in copies:
        copy.wait()
    rows = source.shape[0]
    position = lax.broadcasted_iota(jnp.int32, (rows, LANES), 0) * LANES + lax.broadcasted_iota(
        jnp.int32, (rows, LANES), 1
    )
    valid = position < count_ref[0, 0]
    index = source[...]
    out_ref[:rows] = jnp.where(valid, index // LANES, -1).astype(F32).astype(BF)
    out_ref[rows : 2 * rows] = (index % LANES).astype(F32).astype(BF)
    out_ref[2 * rows : 3 * rows] = jnp.where(valid, target[...], -1).astype(F32).astype(BF)
    out_ref[3 * rows :] = jnp.concatenate([feats[...].astype(F32), cot[...]], axis=1).astype(BF)
    hits = lax.broadcasted_iota(jnp.int32, upper_ref.shape, 0)
    upper_ref[...] = (hits == upper[...]).astype(F32).astype(BF)
    lower_ref[...] = (hits == lower[...]).astype(F32).astype(BF)


def slab_kernel(groups, rows, *refs):
    packs = [ref[3 * rows :].astype(F32) for ref in refs[:groups]]
    upper_ref, lower_ref, slab_ref, cot_ref, alpha_ref, beta_ref = refs[groups:]
    latent = slab_ref.shape[0]
    both = jnp.concatenate([pick(packs, rank) for rank in range(groups)], axis=0).T
    slab16 = both[:latent].astype(BF)
    slab_ref[...] = slab16
    cot_ref[...] = both[latent:]
    rim_payloads(slab16, upper_ref, lower_ref, alpha_ref, beta_ref)


def onehot_kernel(groups, rows, rim, *refs):
    packs = [ref[: 3 * rows].astype(F32) for ref in refs[:groups]]
    parts = refs[groups : 2 * groups]
    (slab_ref, first_ref, second_ref, node_first_ref, node_second_ref, bias_ref,
     onehot_ref, edges_ref, base_ref, message_ref, count_ref,
     first_back, second_back, node_first_back, node_second_back, bias_out) = refs[2 * groups :]
    latent, slab = slab_ref.shape
    wide = onehot_ref.shape[0] - slab
    first_back[...] = flip(first_ref[...])
    second_back[...] = flip(second_ref[...])
    node_first_back[...] = flip(node_first_ref[...])
    node_second_back[...] = flip(node_second_ref[...])
    bias = bias_ref[...].T
    bias_out[...] = bias
    source_rows = lax.broadcasted_iota(jnp.int32, (wide, LANES), 0).astype(F32)
    target_rows = lax.broadcasted_iota(jnp.int32, (slab, LANES), 0).astype(F32)
    ones_row = source_rows == float(slab + 2 * rim)
    for rank in range(groups):
        pack = pick(packs, rank)
        source = jnp.where(pack[:rows] < 0.0, -1.0, pack[:rows] * LANES + pack[rows : 2 * rows])
        target = pack[2 * rows :]
        for row in range(rows):
            cols = slice((rank * rows + row) * LANES, (rank * rows + row + 1) * LANES)
            match = (source_rows == source[row : row + 1]) | ones_row
            onehot_ref[:wide, cols] = jnp.where(match, 1.0, 0.0).astype(BF)
            onehot_ref[wide:, cols] = jnp.where(target_rows == target[row : row + 1], 1.0, 0.0).astype(BF)
        for cols in chunks_of(parts[0].shape[1]):
            first = rank * rows * LANES + cols.start
            edges_ref[:, first : first + CHUNK] = pick([part[:, cols] for part in parts], rank)
    message = None
    count = None
    for cols in chunks_of(edges_ref.shape[1]):
        hit = onehot_ref[wide:, cols]
        message = add_to(message, mm_nt(edges_ref[:, cols], hit))
        count = add_to(count, mm_nt(jnp.ones((16, CHUNK), BF), hit))
    message_ref[...] = message
    count_ref[...] = count[:8]
    slab_base(first_ref, slab_ref[...], bias, onehot_ref, lambda cols: edges_ref[:, cols], base_ref)


def forward_kernel(base_ref, onehot_ref, slab_ref, alpha_in, beta_in, message_in, count_ref,
                   first_ref, second_ref, node_first_ref, node_second_ref, bias_ref, upper_ref, lower_ref,
                   hidden_ref, slope_ref, rims_ref, sums_ref, message_ref, joined_ref, node_pre_ref,
                   node_hidden_ref, state_ref, alpha_ref, beta_ref):
    latent, slab = slab_ref.shape
    wide = onehot_ref.shape[0] - slab
    rims16 = rim_columns(alpha_in[...].astype(F32), beta_in[...].astype(F32), wide - slab)
    rims_ref[...] = rims16
    sums = activate(
        base_ref, mm(first_ref[:, :latent], rims16), onehot_ref, slab, hidden_ref, slope_ref
    )
    sums_ref[...] = sums
    bias = bias_ref[...]
    message = message_in[...] + wide_mm(second_ref[...], sums) + bias[:, 1:2] * count_ref[0:1]
    message_ref[...] = message
    slab16 = slab_ref[...]
    joined = jnp.concatenate([slab16, message.astype(BF)], axis=0)
    joined_ref[...] = joined
    node_pre = mm(node_first_ref[...], joined) + bias[:, 2:3]
    node_pre_ref[...] = node_pre
    node_hidden = slope_parts(node_pre)[0].astype(BF)
    node_hidden_ref[...] = node_hidden
    state = (slab16.astype(F32) + mm(node_second_ref[...], node_hidden) + bias[:, 3:4]).astype(BF)
    state_ref[...] = state
    rim_payloads(state, upper_ref, lower_ref, alpha_ref, beta_ref)


def between_kernel(edges_ref, hidden_ref, onehot_ref, slab_ref, first_ref, second_ref, bias_ref,
                   new_ref, base_ref):
    bias = bias_ref[...]
    second = second_ref[...]
    for cols in chunks_of(edges_ref.shape[1]):
        new_ref[:, cols] = (
            edges_ref[:, cols].astype(F32) + mm(second, hidden_ref[:, cols]) + bias[:, 1:2]
        ).astype(BF)
    slab_base(first_ref, slab_ref[...], bias, onehot_ref, lambda cols: new_ref[:, cols], base_ref)


def edge_gradient(gm_total, extra_ref, slope_ref, onehot_ref, edges_ref, second_back, low_ref):
    slab = gm_total.shape[1]
    wide = onehot_ref.shape[0] - slab
    high, low = halves(wide_mm(second_back[...], gm_total))
    table = jnp.concatenate([high, low], axis=1)
    total = None
    for cols in chunks_of(edges_ref.shape[1]):
        hit = onehot_ref[wide:, cols]
        grad = mm(table, jnp.concatenate([hit, hit], axis=0))
        if extra_ref is not None:
            grad = grad + extra_ref[:, cols]
        pre_low = (grad * slope_ref[:, cols]).astype(BF)
        if low_ref is not None:
            low_ref[:, cols] = pre_low
        total = add_to(
            total, mm_nt(pre_low, jnp.concatenate([onehot_ref[:, cols], edges_ref[:, cols]], axis=0))
        )
    return total


def middle_kernel(base_ref, onehot_ref, edges_ref, slab_ref, alpha_in, beta_in, message_in, count_ref, cot_ref,
                  first_ref, second_ref, node_first_ref, bias_ref, first_back, second_back,
                  node_first_back, node_second_back,
                  hidden_ref, low_ref, rims_ref, sums_ref, joined_ref, node_pre_ref, node_grad_ref, gm_ref,
                  first_sums_ref, back_ref, alpha_ref, beta_ref, slope_ref):
    latent, slab = slab_ref.shape
    wide = onehot_ref.shape[0] - slab
    rims16 = rim_columns(alpha_in[...].astype(F32), beta_in[...].astype(F32), wide - slab)
    rims_ref[...] = rims16
    sums = activate(
        base_ref, mm(first_ref[:, :latent], rims16), onehot_ref, slab, hidden_ref, slope_ref
    )
    sums_ref[...] = sums
    bias = bias_ref[...]
    message = message_in[...] + wide_mm(second_ref[...], sums) + bias[:, 1:2] * count_ref[0:1]
    joined = jnp.concatenate([slab_ref[...], message.astype(BF)], axis=0)
    joined_ref[...] = joined
    node_pre = mm(node_first_ref[...], joined) + bias[:, 2:3]
    node_pre_ref[...] = node_pre
    cot = cot_ref[...]
    pre_grad, through, gm = node_backward(cot, node_pre, node_first_back, node_second_back)
    node_grad_ref[...] = pre_grad
    gm_ref[...] = gm
    first_sums = edge_gradient(
        gm.astype(F32), None, slope_ref, onehot_ref, edges_ref, second_back, low_ref
    )
    first_sums_ref[...] = first_sums
    ext_grad, slab_grad = table_grads(first_back, first_sums, slab, wide)
    back_ref[...] = cot + through + slab_grad
    alpha, beta = rim_gradients(ext_grad, slab, alpha_ref.shape[1])
    alpha_ref[...] = alpha.astype(BF)
    beta_ref[...] = beta.astype(BF)


def carry_kernel(rim, low_ref, hidden_zero_ref, hidden_ref, edges_ref, slab_ref, rims_ref, sums_ref, sums_zero_ref,
                 joined_ref, node_pre_ref, node_grad_ref, gm_ref, first_sums_ref, count_ref, cot_ref,
                 first_back, second_back,
                 extra_ref, total_ref):
    latent, slab = slab_ref.shape
    wide = slab + rims_ref.shape[1]
    self_back = first_back[2 * latent :]
    back = second_back[...]
    cross = None
    for cols in chunks_of(low_ref.shape[1]):
        low = low_ref[:, cols]
        extra_ref[:, cols] = mm(back, mm(self_back, low).astype(BF))
        cross = add_to(cross, mm_nt(low, hidden_zero_ref[:, cols]))
    sums = first_sums_ref[...]
    pre_sum = sums[:, slab + 2 * rim : slab + 2 * rim + 1]
    gm = gm_ref[...]
    edge_two = (
        mm_nt(gm, sums_ref[...].astype(BF))
        + mm_nt(gm, sums_zero_ref[...].astype(BF))
        + mm(self_back, cross.astype(BF))
    )
    gm_sum = 2.0 * jnp.sum(gm.astype(F32) * count_ref[0:1], axis=1, keepdims=True) + wide_mm(
        self_back, jnp.broadcast_to(pre_sum, (latent, LANES))
    )[:, :1]
    cot = cot_ref[...]
    node_pre = node_pre_ref[...]
    node_one, node_two, node_pre_sum, cot_sum = node_sums(
        cot, node_grad_ref[...], joined_ref[...], slope_parts(node_pre)[0].astype(BF)
    )
    edge_one = first_total(sums, slab_ref[...], rims_ref[...], slab, wide)
    used = edge_one.shape[1] + edge_two.shape[1] + node_one.shape[1] + node_two.shape[1]
    pad = jnp.zeros((latent, total_ref.shape[1] - used - 4), F32)
    total_ref[...] = jnp.concatenate(
        [edge_one, edge_two, node_one, node_two, pre_sum, gm_sum, node_pre_sum, cot_sum, pad], axis=1
    )


def output_kernel(count_ref, edges_ref, hidden_ref, joined_ref, node_pre_ref, second_ref, node_second_ref, bias_ref,
                  edge_out, node_out, new_ref):
    bias = bias_ref[...]
    latent = edges_ref.shape[0]
    second = second_ref[...]
    for cols in chunks_of(edges_ref.shape[1]):
        new_ref[:, cols] = (
            edges_ref[:, cols].astype(F32) + mm(second, hidden_ref[:, cols]) + bias[:, 1:2]
        ).astype(BF)
    slots = edge_out.shape[1]
    begin = lax.axis_index("layer") * slots
    for cols in chunks_of(slots):
        position = lax.broadcasted_iota(jnp.int32, (latent, CHUNK), 1) + cols.start
        mine = new_ref[:, pl.ds(pl.multiple_of(begin + cols.start, CHUNK), CHUNK)].astype(F32)
        edge_out[:, cols] = jnp.where(position < count_ref[0, 0], mine, 0.0).astype(BF)
    node_hidden = slope_parts(node_pre_ref[...])[0].astype(BF)
    state = joined_ref[:latent].astype(F32) + mm(node_second_ref[...], node_hidden) + bias[:, 3:4]
    node_out[...] = own_rows(state.T, node_out.shape[0]).astype(BF)


def last_kernel(back_in, alpha_grad, beta_grad, upper_ref, lower_ref, joined_ref, node_pre_ref, node_hidden_ref,
                gm_in, sums_ref, count_ref, extra_ref, slope_ref, onehot_ref, edges_ref, slab_ref, rims_ref,
                total_in, first_back, second_back, node_first_back, node_second_back,
                total_ref, back_ref):
    latent, slab = slab_ref.shape
    wide = onehot_ref.shape[0] - slab
    rim = alpha_grad.shape[1]
    grad = back_in[...] + placed_rims(
        alpha_grad[...].astype(F32), beta_grad[...].astype(F32), upper_ref, lower_ref
    )
    pre_grad, through, gm = node_backward(grad, node_pre_ref[...], node_first_back, node_second_back)
    gm_wide = gm.astype(F32) + gm_in[...].astype(F32)
    sums = edge_gradient(gm_wide, extra_ref, slope_ref, onehot_ref, edges_ref, second_back, None)
    ext_grad, slab_grad = table_grads(first_back, sums, slab, wide)
    back_ref[...] = grad + through + slab_grad
    alpha, beta = rim_gradients(ext_grad, slab, rim)
    node_one, node_two, node_pre_sum, grad_sum = node_sums(grad, pre_grad, joined_ref[...], node_hidden_ref[...])
    edge_one = first_total(sums, slab_ref[...], rims_ref[...], slab, wide)
    edge_two = mm_nt(gm, sums_ref[...].astype(BF))
    pre_sum = sums[:, slab + 2 * rim : slab + 2 * rim + 1]
    gm_sum = jnp.sum(gm.astype(F32) * count_ref[0:1], axis=1, keepdims=True)
    used = edge_one.shape[1] + edge_two.shape[1] + node_one.shape[1] + node_two.shape[1]
    pad = jnp.zeros((latent, total_ref.shape[1] - used - 4 - 2 * rim), F32)
    total_ref[...] = (
        total_in[...]
        + jnp.concatenate(
            [edge_one, edge_two, node_one, node_two, pre_sum, gm_sum, node_pre_sum, grad_sum, alpha, beta, pad],
            axis=1,
        )
    ).astype(BF)


def add_kernel(used, rim, bit, mine_ref, other_ref, out_ref):
    mine = mine_ref[...].astype(F32)
    other = other_ref[...].astype(F32)
    lane = lax.broadcasted_iota(jnp.int32, mine.shape, 1)
    held = other[:, used + rim : used + 2 * rim]
    if bit == 1:
        arrived = jnp.zeros_like(held)
        passing = held
    else:
        place = lax.axis_index("phi")
        home = (lax.rem(place // bit, 2) == 1) == (lax.rem(place, 2) == 0)
        arrived = mine[:, used : used + rim] + jnp.where(home, held, 0.0)
        passing = jnp.where(home, 0.0, held)
    pad = jnp.zeros((mine.shape[0], mine.shape[1] - used - 2 * rim), F32)
    out_ref[...] = jnp.concatenate(
        [(mine + other)[:, :used], arrived, passing, pad], axis=1
    ).astype(BF)


def finish_kernel(used, rim, mine_ref, other_ref, back_ref, alpha_in, upper_ref, lower_ref,
                  node_grad, edge_one, edge_two, node_one, node_two, bias_out):
    mine = mine_ref[...].astype(F32)
    other = other_ref[...].astype(F32)
    total = mine + other
    cut = 0
    for ref in (edge_one, edge_two, node_one, node_two):
        ref[...] = total[:, cut : cut + ref.shape[1]]
        cut += ref.shape[1]
    block = used - 4 - (used - 4) % LANES
    turned = total[:, block : block + LANES].T
    bias_out[...] = turned[used - 4 - block : used - block]
    alpha = alpha_in[...].astype(F32)[:, used : used + rim]
    beta = mine[:, used : used + rim] + other[:, used + rim : used + 2 * rim]
    grad = back_ref[...] + placed_rims(alpha, beta, upper_ref, lower_ref)
    node_grad[...] = own_rows(grad.T, node_grad.shape[0])


def call(kernel, outs, *args, scratch=(), smem=0, hbm=(), cost=1.0):
    args = [
        pltpu.with_memory_space_constraint(arg, HBM) if place in hbm else arg for place, arg in enumerate(args)
    ]
    held = [(arg.shape, arg.dtype) for arg in args] + list(outs)
    held += [(ref.shape, ref.dtype) for ref in scratch if jnp.issubdtype(ref.dtype, jnp.number)]
    room = sum(math.prod(shape) * jnp.dtype(kind).itemsize for shape, kind in held)
    spaces = [pltpu.SMEM if place < smem else HBM if place in hbm else VM for place in range(len(args))]
    specs = [pl.BlockSpec(memory_space=space) for space in spaces]
    return pl.pallas_call(
        kernel,
        out_shape=[jax.ShapeDtypeStruct(shape, kind) for shape, kind in outs],
        in_specs=specs,
        out_specs=[pl.BlockSpec(memory_space=VM) for _ in outs],
        scratch_shapes=list(scratch),
        compiler_params=pltpu.CompilerParams(vmem_limit_bytes=room + 10 * 1024 * 1024),
        cost_estimate=pl.CostEstimate(
            flops=int(cost * 1e9), bytes_accessed=int(cost * 3.6e6), transcendentals=0
        ),
    )(*args)


def swap(value, axis, pairing):
    count = lax.axis_size(axis)
    return lax.ppermute(value, axis, [(source, pairing(source) % count) for source in range(count)])


def by_alpha(value):
    return swap(value, "phi", lambda index: index ^ 1)


def by_beta(value):
    return swap(value, "phi", lambda index: index - 1 if index % 2 == 0 else index + 1)


def layer_parts(value):
    groups = lax.axis_size("layer")
    return [value] + [
        swap(value, "layer", lambda index, turn=turn: index + turn) for turn in range(1, groups)
    ]


def body(node_feats, edge_feats, edge_source, edge_target, edge_counts, rim_upper, rim_lower,
         edge_first, edge_second, node_first, node_second, biases, node_cot):
    groups = lax.axis_size("layer")
    ring = lax.axis_size("phi")
    latent, width = node_feats.shape
    hidden = edge_second.shape[1]
    slots = edge_feats.shape[1]
    slab = width * groups
    rim = rim_upper.shape[1]
    wide = (slab + 2 * rim) // LANES * LANES + LANES
    total_slots = slots * groups
    rows = slots // LANES
    rim_shape = ((latent, rim), BF)
    per_slot = lambda kind: ((latent, total_slots), kind)
    per_hit = lambda kind, depth=1: ((depth * latent, slab), kind)

    packed, upper, lower = call(
        prep_kernel, [((3 * rows + width, LANES), BF), ((slab, rim), BF), ((slab, rim), BF)],
        edge_counts, edge_source.reshape(rows, LANES), edge_target.reshape(rows, LANES),
        node_feats.T, node_cot.T, rim_upper, rim_lower,
        scratch=[VM((rows, LANES), jnp.int32), VM((rows, LANES), jnp.int32),
                 VM((width, latent), BF), VM((width, latent), F32), VM((1, rim), jnp.int32),
                 VM((1, rim), jnp.int32), pltpu.SemaphoreType.DMA((6,))],
        smem=1, hbm=range(1, 7),
    )
    packs = layer_parts(packed)
    parts = layer_parts(edge_feats)
    slab_zero, cot, alpha, beta = call(
        functools.partial(slab_kernel, groups, rows),
        [per_hit(BF), per_hit(F32), rim_shape, rim_shape], *packs, upper, lower, cost=0.3,
    )
    alpha = by_alpha(alpha)
    beta = by_beta(beta)
    (onehot, edges_zero, base, message, count, first_back, second_back, node_first_back, node_second_back,
     bias) = call(
        functools.partial(onehot_kernel, groups, rows, rim),
        [((wide + slab, total_slots), BF), per_slot(BF), per_slot(F32), per_hit(F32), ((8, slab), F32),
         (edge_first.shape[::-1], BF), (edge_second.shape[::-1], BF), (node_first.shape[::-1], BF),
         (node_second.shape[::-1], BF), (biases.shape[::-1], F32)],
        *packs, *parts, slab_zero, edge_first, edge_second, node_first, node_second, biases, cost=2.0,
    )
    (hidden_zero, slope, rims_zero, sums_zero, message, joined_zero, node_pre_zero, node_hidden_zero, slab_one,
     alpha, beta) = call(
        forward_kernel,
        [per_slot(BF), per_slot(F32), ((latent, wide - slab), BF), per_hit(F32), per_hit(F32), per_hit(BF, 2),
         per_hit(F32), per_hit(BF), per_hit(BF), rim_shape, rim_shape],
        base, onehot, slab_zero, alpha, beta, message, count, edge_first, edge_second, node_first, node_second,
        bias, upper, lower, cost=2.0,
    )
    alpha = by_alpha(alpha)
    beta = by_beta(beta)
    edges_one, base = call(
        between_kernel, [per_slot(BF), per_slot(F32)],
        edges_zero, hidden_zero, onehot, slab_one, edge_first, edge_second, bias, cost=2.0,
    )
    total_width = edge_first.shape[1] + hidden + node_first.shape[1] + node_second.shape[1] + 4
    lanes = -(-(total_width + 2 * rim) // LANES) * LANES
    (hidden_one, low, rims_one, sums_one, joined_one, node_pre_one, node_grad_one, gm, first_sums, back,
     alpha, beta) = call(
        middle_kernel,
        [per_slot(BF), per_slot(BF), ((latent, wide - slab), BF), per_hit(F32), per_hit(BF, 2), per_hit(F32),
         per_hit(F32), per_hit(BF), ((hidden, wide + slab + latent), F32), per_hit(F32), rim_shape, rim_shape],
        base, onehot, edges_one, slab_one, alpha, beta, message, count, cot, edge_first, edge_second, node_first,
        bias, first_back, second_back, node_first_back, node_second_back,
        scratch=[VM((hidden, total_slots), F32)], cost=3.0,
    )
    alpha = by_alpha(alpha)
    beta = by_beta(beta)
    extra, total = call(
        functools.partial(carry_kernel, rim), [per_slot(F32), ((latent, lanes), F32)],
        low, hidden_zero, hidden_one, edges_one, slab_one, rims_one, sums_one, sums_zero, joined_one, node_pre_one,
        node_grad_one, gm, first_sums, count, cot, first_back, second_back, cost=2.0,
    )
    edge_out, node_out = call(
        output_kernel, [((latent, slots), BF), ((width, latent), BF)],
        edge_counts, edges_one, hidden_one, joined_one, node_pre_one, edge_second, node_second, bias,
        scratch=[VM((latent, total_slots), BF)], smem=1, cost=2.0,
    )
    total, back = call(
        last_kernel, [((latent, lanes), BF), per_hit(F32)],
        back, alpha, beta, upper, lower, joined_zero, node_pre_zero, node_hidden_zero, gm, sums_zero, count, extra,
        slope, onehot, edges_zero, slab_zero, rims_zero, total, first_back, second_back, node_first_back,
        node_second_back, cost=2.0,
    )
    other = by_alpha(total)
    alpha_last = other
    bit = 1
    while 2 * bit < ring:
        total = call(
            functools.partial(add_kernel, total_width, rim, bit), [((latent, lanes), BF)], total, other, cost=0.1,
        )[0]
        bit *= 2
        other = swap(total, "phi", lambda index, bit=bit: index ^ bit)
    node_grad, edge_one, edge_two, node_one, node_two, bias_out = call(
        functools.partial(finish_kernel, total_width, rim),
        [((width, latent), F32), (edge_first.shape, F32), (edge_second.shape, F32),
         (node_first.shape, F32), (node_second.shape, F32), (biases.shape, F32)],
        total, other, back, alpha_last, upper, lower,
    )
    return node_out.T, edge_out, node_grad.T, edge_one, edge_two, node_one, node_two, bias_out


def solution(mesh):
    split = P(None, ("phi", "layer"))
    return jax.shard_map(
        body,
        mesh=mesh,
        in_specs=(split, split, P(("phi", "layer")), P(("phi", "layer")), P("phi", "layer"),
                  P("phi", None), P("phi", None), P(), P(), P(), P(), P(), split),
        out_specs=(split, split, split, P(), P(), P(), P(), P()),
        check_vma=False,
    )
```

time: 311 us -> 53.7 us (0.17)
  waiting for transfers between devices: 168 us -> 18.7 us
  local copies, waits for them, and re-layouts: 57.1 us -> 0.03 us
  matrix products: 19.5 us -> 0 us
  blocking collectives: 18.6 us -> 0 us
  other arithmetic: 17.1 us -> 0 us
  Pallas kernels: 0 us -> 14.4 us
  between operations: 15.4 us -> 1.52 us
  starting transfers between devices: 13.4 us -> 19 us
    psum x1 -> x0, waiting for transfers between devices: 130 us -> none  [body(): lax.psum((sum_first_edge, sum_second_edge, sum_first_node, sum_second_nod...]
    gather x14 -> x0, local copies, waits for them, and re-layouts: 40.3 us -> none  [the longest x4 12.8 us: body(): jnp.take(message_slab, edge_target, axis=1).astype(jnp.float32)]
    dot_general x51 -> x0, matrix products: 19.5 us -> none  [the longest x32 11.6 us: outer_dot(): lax.dot_general(left, right, (((1,), (1,)), ((), ())), preferred_element_...]
    all_gather x4 -> x0, blocking collectives: 18.6 us -> none  [the longest x2 9.88 us: body(): slab_nodes = lax.all_gather(node_state, 'layer', axis=1, tiled=True)]
    reduce_scatter x3 -> x0, waiting for transfers between devices: 17.7 us -> none  [the longest x2 11 us: body(): lax.psum_scatter(slab_grad.astype(jnp.bfloat16), 'layer', scatter_dimensi...]
    pallas_call x0 -> x13, Pallas kernels: none -> 14.4 us  [call(): pl.pallas_call(kernel, out_shape=[jax.ShapeDtypeStruct(shape, kind) for s...]
    unnamed x135 -> x12, local copies, waits for them, and re-layouts: 13.6 us -> 0.03 us
    unnamed x6 -> x0, waiting for transfers between devices: 9.02 us -> none
  transfers between devices with their start and end apart: 13 -> 12, of which waited for: 7 -> 7; matrix products, arithmetic and copies ran while one was open for 8% -> 0% of each run, Pallas kernels for 0% -> 12%
where the time goes in v1:
time: 53.7 us; the launch traced here: 53.5 us
  starting transfers between devices  19 us (35%)
  waiting for transfers between devices  18.7 us (35%)
  Pallas kernels  14.4 us (27%)
  between operations  1.52 us (3%)
    ppermute x12, starting transfers between devices, swap(): lax.ppermute(value, axis, [(source, pairing(source) % count) for source i...  19 us
    ppermute x12, waiting for transfers between devices, swap(): lax.ppermute(value, axis, [(source, pairing(source) % count) for source i...  18.7 us
    pallas_call x13, Pallas kernels, call(): pl.pallas_call(kernel, out_shape=[jax.ShapeDtypeStruct(shape, kind) for s...  14.4 us
  transfers between devices with their start and end apart: 12, of which 7 were waited for; matrix products, arithmetic and copies ran while one was open for 0% of the time, Pallas kernels for 12%

profile of v1, /device:TPU:0, one launch (start us, length us, event | category | flops | bytes accessed | tf_op | source)
XLA Modules:
  0.0 53.5 jit_solution(8730892103197285396)
XLA Ops:
  0.6 3.0 %collective-permute-start.1 = (bf16[64,2048]{1,0:T(8,128)(2,1)}, bf16[64,2048]{1,0:T(8,128)(2,1)S(1)}, u32[]{:S(2)}, u32[]{:S(2)}) collective-permute-start(bf16[64,2048]{1,0:T(8,128)(2,1)} %refs_2_.1), channel_id=1, source_target_pairs={{0,1},{1,0},{2,3},{3,2},{4,5},{5,4},{6,7},{7,6},{8,9},{9,8},{10,11... | collective-permute-start | bytes 786440 | tf_op jit(solution)/shard_map/ppermute | solution.py:495
  4.3 0.0 copy-start
  4.3 0.0 copy-start.1
  4.3 0.0 copy-start.2
  4.3 0.0 copy-start.3
  4.3 0.0 copy-start.4
  4.3 0.0 copy-start.5
  4.4 1.0 %shard_map.188 = (bf16[80,128]{1,0:T(8,128)(2,1)S(1)}, bf16[64,24]{1,0:T(8,128)(2,1)S(1)}, bf16[64,24]{1,0:T(8,128)(2,1)S(1)}) custom-call(s32[1,1]{1,0:T(1,128)S(6)} %copy.21.count_ref, s32[16,128]{1,0:T(8,128)} %bitcast.7, s32[16,128]{1,0:T(8,128)} %bitcast.8, bf16[32,64]{1,0:T(8,128)(2,1)} %bitcast.9, f32[32,64]{1,0:T(8,128)} %bitcast.6, ...), custom_call_target="tpu_custom_call" | custom-call | flops 1000000000 | bytes 3600000 | tf_op jit(solution)/shard_map/pallas_call | solution.py:480
  5.3 0.1 collective-permute-start
  5.4 5.2 %collective-permute-done.refs_1_ = bf16[80,128]{1,0:T(8,128)(2,1)S(1)} collective-permute-done((bf16[80,128]{1,0:T(8,128)(2,1)S(1)}, bf16[80,128]{1,0:T(8,128)(2,1)S(1)}, u32[]{:S(2)}, u32[]{:S(2)}) %collective-permute-start) | collective-permute-done | bytes 20512 | tf_op jit(solution)/shard_map/ppermute | solution.py:495
  10.6 0.2 shard_map.189
  10.8 0.1 collective-permute-start.2
  10.9 4.9 %collective-permute-start.3 = (bf16[64,24]{1,0:T(8,128)(2,1)S(1)}, bf16[64,24]{1,0:T(8,128)(2,1)S(1)}, u32[]{:S(2)}, u32[]{:S(2)}) collective-permute-start(bf16[64,24]{1,0:T(8,128)(2,1)S(1)} %get-tuple-element.70), channel_id=1, source_target_pairs={{0,30},{2,4},{4,2},{6,8},{8,6},{10,12},{12,10},{14,16},{16,14},{18... | collective-permute-start | bytes 9224 | tf_op jit(solution)/shard_map/ppermute | solution.py:495
  15.8 0.0 collective-permute-done.1.refs_3_
  15.8 0.0 copy-done
  15.8 0.0 copy-done.1
  15.8 0.0 copy-done.2
  15.8 0.0 copy-done.3
  15.8 0.0 copy-done.4
  15.8 0.0 copy-done.5
  15.8 1.3 %shard_map.190 = (bf16[192,4096]{1,0:T(8,128)(2,1)S(1)}, bf16[64,4096]{1,0:T(8,128)(2,1)S(1)}, f32[64,4096]{1,0:T(8,128)S(1)}, f32[64,64]{1,0:T(8,128)S(1)}, f32...) custom-call(bf16[80,128]{1,0:T(8,128)(2,1)S(1)} %get-tuple-element.6, ...), custom_call_target="tpu_custom_call" | custom-call | flops 2000000000 | bytes 7200000 | tf_op jit(solution)/shard_map/pallas_call | solution.py:480
  17.1 0.0 collective-permute-done.2.alpha_in
  17.2 0.1 collective-permute-done.3.beta_in
  17.2 1.5 %shard_map.191 = (bf16[64,4096]{1,0:T(8,128)(2,1)S(1)}, f32[64,4096]{1,0:T(8,128)S(1)}, bf16[64,64]{1,0:T(8,128)(2,1)S(1)}, f32[64,64]{1,0:T(8,128)S(1)}, f32[64...) custom-call(f32[64,4096]{1,0:T(8,128)S(1)} %get-tuple-element.67.bas, ...), custom_call_target="tpu_custom_call" | custom-call | flops 2000000000 | bytes 7200000 | tf_op jit(solution)/shard_map/pallas_call | solution.py:480
  18.7 0.1 collective-permute-start.4
  18.8 4.5 %collective-permute-start.5 = (bf16[64,24]{1,0:T(8,128)(2,1)S(1)}, bf16[64,24]{1,0:T(8,128)(2,1)S(1)}, u32[]{:S(2)}, u32[]{:S(2)}) collective-permute-start(bf16[64,24]{1,0:T(8,128)(2,1)S(1)} %get-tuple-element.79), channel_id=1, source_target_pairs={{0,30},{2,4},{4,2},{6,8},{8,6},{10,12},{12,10},{14,16},{16,14},{18... | collective-permute-start | bytes 9224 | tf_op jit(solution)/shard_map/ppermute | solution.py:495
  23.3 1.0 %shard_map.192 = (bf16[64,4096]{1,0:T(8,128)(2,1)S(1)}, f32[64,4096]{1,0:T(8,128)S(1)}) custom-call(bf16[64,4096]{1,0:T(8,128)(2,1)S(1)} %get-tuple-element.66.edges_ref, bf16[64,4096]{1,0:T(8,128)(2,1)S(1)} %get-tuple-element.74.hidden_ref.hidden_zero_ref, bf16[192,4096]{1,0:T(8,128)(2,1)S(1)} %get-tuple-element.68.onehot_ref, ...), custom_call_target="tpu_custom_call" | custom-call | flops 2000000000 | bytes 7200000 | tf_op jit(solution)/shard_map/pallas_call | solution.py:480
  24.3 0.0 collective-permute-done.4.alpha_in
  24.3 0.4 collective-permute-done.5.beta_in
  24.7 3.2 %shard_map.193 = (bf16[64,4096]{1,0:T(8,128)(2,1)S(1)}, bf16[64,4096]{1,0:T(8,128)(2,1)S(1)}, bf16[64,64]{1,0:T(8,128)(2,1)S(1)}, f32[64,64]{1,0:T(8,128)S(1)}, ...) custom-call(f32[64,4096]{1,0:T(8,128)S(1)} %get-tuple-element.77.bas, ...), custom_call_target="tpu_custom_call" | custom-call | flops 3000000000 | bytes 10800000 | tf_op jit(solution)/shard_map/pallas_call | solution.py:480
  27.9 0.0 collective-permute-start.6
  28.0 4.5 %collective-permute-start.7 = (bf16[64,24]{1,0:T(8,128)(2,1)S(1)}, bf16[64,24]{1,0:T(8,128)(2,1)S(1)}, u32[]{:S(2)}, u32[]{:S(2)}) collective-permute-start(bf16[64,24]{1,0:T(8,128)(2,1)S(1)} %get-tuple-element.93), channel_id=1, source_target_pairs={{0,30},{2,4},{4,2},{6,8},{8,6},{10,12},{12,10},{14,16},{16,14},{18... | collective-permute-start | bytes 9224 | tf_op jit(solution)/shard_map/ppermute | solution.py:495
  32.5 1.7 %shard_map.195 = (f32[64,4096]{1,0:T(8,128)S(1)}, f32[64,512]{1,0:T(8,128)S(1)}) custom-call(bf16[64,4096]{1,0:T(8,128)(2,1)S(1)} %get-tuple-element.99.low_ref, bf16[64,4096]{1,0:T(8,128)(2,1)S(1)} %get-tuple-element.74.hidden_ref.hidden_zero_ref, bf16[64,4096]{1,0:T(8,128)(2,1)S(1)} %get-tuple-element.86.hidden_ref, ...), custom_call_target="tpu_custom_call" | custom-call | flops 2000000000 | bytes 7200000 | tf_op jit(solution)/shard_map/pallas_call | solution.py:480
  34.2 0.0 collective-permute-done.6.alpha_grad
  34.2 0.0 collective-permute-done.7.beta_grad
  34.2 2.3 %shard_map.196 = (bf16[64,512]{1,0:T(8,128)(2,1)S(1)}, f32[64,64]{1,0:T(8,128)S(1)}) custom-call(f32[64,64]{1,0:T(8,128)S(1)} %get-tuple-element.91.back_in, bf16[64,24]{1,0:T(8,128)(2,1)S(1)} %collective-permute-done.6.alpha_grad, bf16[64,24]{1,0:T(8,128)(2,1)S(1)} %collective-permute-done.7.beta_grad, ...), custom_call_target="tpu_custom_call" | custom-call | flops 2000000000 | bytes 7200000 | tf_op jit(solution)/shard_map/pallas_call | solution.py:480
  36.5 0.1 collective-permute-start.8
  36.6 1.2 %collective-permute-done.8.other_ref.alpha_in = bf16[64,512]{1,0:T(8,128)(2,1)S(1)} collective-permute-done((bf16[64,512]{1,0:T(8,128)(2,1)S(1)}, bf16[64,512]{1,0:T(8,128)(2,1)S(1)}, u32[]{:S(2)}, u32[]{:S(2)}) %collective-permute-start.8) | collective-permute-done | bytes 65568 | tf_op jit(solution)/shard_map/ppermute | solution.py:495
  37.9 0.1 collective-permute-start.9
  38.0 4.3 %collective-permute-done.9.other_ref = bf16[64,512]{1,0:T(8,128)(2,1)S(1)} collective-permute-done((bf16[64,512]{1,0:T(8,128)(2,1)S(1)}, bf16[64,512]{1,0:T(8,128)(2,1)S(1)}, u32[]{:S(2)}, u32[]{:S(2)}) %collective-permute-start.9) | collective-permute-done | bytes 65568 | tf_op jit(solution)/shard_map/ppermute | solution.py:495
  42.2 0.1 shard_map.198.mine_ref
  42.3 0.0 collective-permute-start.10
  42.3 4.3 %collective-permute-done.10.other_ref = bf16[64,512]{1,0:T(8,128)(2,1)S(1)} collective-permute-done((bf16[64,512]{1,0:T(8,128)(2,1)S(1)}, bf16[64,512]{1,0:T(8,128)(2,1)S(1)}, u32[]{:S(2)}, u32[]{:S(2)}) %collective-permute-start.10) | collective-permute-done | bytes 65568 | tf_op jit(solution)/shard_map/ppermute | solution.py:495
  46.6 0.1 shard_map.199.mine_ref
  46.7 1.6 %collective-permute-start.11 = (bf16[64,512]{1,0:T(8,128)(2,1)S(1)}, bf16[64,512]{1,0:T(8,128)(2,1)S(1)}, u32[]{:S(2)}, u32[]{:S(2)}) collective-permute-start(bf16[64,512]{1,0:T(8,128)(2,1)S(1)} %shard_map.199.mine_ref), channel_id=1, source_target_pairs={{0,16},{2,18},{4,20},{6,22},{8,24},{10,26},{12,28},{14,30},{16,0},... | collective-permute-start | bytes 196616 | tf_op jit(solution)/shard_map/ppermute | solution.py:495
  48.3 1.1 %shard_map.194 = (bf16[64,2048]{1,0:T(8,128)(2,1)}, bf16[32,64]{1,0:T(8,128)(2,1)}) custom-call(s32[1,1]{1,0:T(1,128)S(6)} %copy.21.count_ref, bf16[64,4096]{1,0:T(8,128)(2,1)S(1)} %get-tuple-element.76.edges_ref, bf16[64,4096]{1,0:T(8,128)(2,1)S(1)} %get-tuple-element.86.hidden_ref, bf16[128,64]{1,0:T(8,128)(2,1)S(1)} %get-tuple-element.87.joined_ref, ...), custom_call_target="tpu_custom_call" | custom-call | flops 2000000000 | bytes 7200000 | tf_op jit(solution)/shard_map/pallas_call | solution.py:480
  49.4 3.2 %collective-permute-done.11.other_ref = bf16[64,512]{1,0:T(8,128)(2,1)S(1)} collective-permute-done((bf16[64,512]{1,0:T(8,128)(2,1)S(1)}, bf16[64,512]{1,0:T(8,128)(2,1)S(1)}, u32[]{:S(2)}, u32[]{:S(2)}) %collective-permute-start.11) | collective-permute-done | bytes 65568 | tf_op jit(solution)/shard_map/ppermute | solution.py:495
  52.6 1.0 %shard_map.200 = (f32[32,64]{1,0:T(8,128)}, f32[64,192]{1,0:T(8,128)}, f32[64,64]{1,0:T(8,128)}, f32[64,128]{1,0:T(8,128)}, f32[64,64]{1,0:T(8,128)}, /*index=5*/f32[4,64]{1,0:T(4,128)}) custom-call(bf16[64,512]{1,0:T(8,128)(2,1)S(1)} %shard_map.199.mine_ref, bf16[64,512]{1,0:T(8,128)(2,1)S(1)} %collective-permute-done.11.other_ref, ...), custom_call_target="tpu_custom_call" | custom-call | flops 1000000000 | bytes 3600000 | tf_op jit(solution)/shard_map/pallas_call | solution.py:480
  (1 shorter events, 0.0 us)
Async XLA Ops:
  0.6 15.2 %collective-permute-start.1 = (bf16[64,2048]{1,0:T(8,128)(2,1)}, bf16[64,2048]{1,0:T(8,128)(2,1)S(1)}, u32[]{:S(2)}, u32[]{:S(2)}) collective-permute-start(bf16[64,2048]{1,0:T(8,128)(2,1)} %refs_2_.1), channel_id=1, source_target_pairs={{0,1},{1,0},{2,3},{3,2},{4,5},{5,4},{6,7},{7,6},{8,9},{9,8},{10,11... | collective-permute-start | bytes 786440 | tf_op jit(solution)/shard_map/ppermute | solution.py:495
  4.3 11.5 %copy-start = (bf16[64,2048]{1,0:T(8,128)(2,1)S(1)}, bf16[64,2048]{1,0:T(8,128)(2,1)}, u32[]{:S(2)}) copy-start(bf16[64,2048]{1,0:T(8,128)(2,1)} %refs_2_.1) | copy-start | bytes 786436
  4.3 11.5 %copy-start.1 = (bf16[64,192]{1,0:T(8,128)(2,1)S(1)}, bf16[64,192]{1,0:T(8,128)(2,1)}, u32[]{:S(2)}) copy-start(bf16[64,192]{1,0:T(8,128)(2,1)} %first_ref.5) | copy-start | bytes 73732
  4.3 11.5 %copy-start.2 = (bf16[64,128]{1,0:T(8,128)(2,1)S(1)}, bf16[64,128]{1,0:T(8,128)(2,1)}, u32[]{:S(2)}) copy-start(bf16[64,128]{1,0:T(8,128)(2,1)} %node_first_ref.3) | copy-start | bytes 49156
  4.3 11.5 %copy-start.3 = (bf16[64,64]{1,0:T(8,128)(2,1)S(1)}, bf16[64,64]{1,0:T(8,128)(2,1)}, u32[]{:S(2)}) copy-start(bf16[64,64]{1,0:T(8,128)(2,1)} %second_ref.7) | copy-start | bytes 24580
  4.3 11.5 %copy-start.4 = (bf16[64,64]{1,0:T(8,128)(2,1)S(1)}, bf16[64,64]{1,0:T(8,128)(2,1)}, u32[]{:S(2)}) copy-start(bf16[64,64]{1,0:T(8,128)(2,1)} %node_second_ref.3) | copy-start | bytes 24580
  4.3 11.5 %copy-start.5 = (f32[4,64]{1,0:T(4,128)S(1)}, f32[4,64]{1,0:T(4,128)}, u32[]{:S(2)}) copy-start(f32[4,64]{1,0:T(4,128)} %refs_9_.1) | copy-start | bytes 3076
  5.3 5.3 %collective-permute-start = (bf16[80,128]{1,0:T(8,128)(2,1)S(1)}, bf16[80,128]{1,0:T(8,128)(2,1)S(1)}, u32[]{:S(2)}, u32[]{:S(2)}) collective-permute-start(bf16[80,128]{1,0:T(8,128)(2,1)S(1)} %get-tuple-element.62.refs_0_), channel_id=1, source_target_pairs={{0,1},{1,0},{2,3},{3,2},{4,5},{5,4},{6,7},{7,6},{8,9},{9,8},{10,11... | collective-permute-start | bytes 61448 | tf_op jit(solution)/shard_map/ppermute | solution.py:495
  10.8 6.4 %collective-permute-start.2 = (bf16[64,24]{1,0:T(8,128)(2,1)S(1)}, bf16[64,24]{1,0:T(8,128)(2,1)S(1)}, u32[]{:S(2)}, u32[]{:S(2)}) collective-permute-start(bf16[64,24]{1,0:T(8,128)(2,1)S(1)} %get-tuple-element.69), channel_id=1, source_target_pairs={{0,2},{2,0},{4,6},{6,4},{8,10},{10,8},{12,14},{14,12},{16,18},{18,... | collective-permute-start | bytes 9224 | tf_op jit(solution)/shard_map/ppermute | solution.py:495
  10.9 6.4 %collective-permute-start.3 = (bf16[64,24]{1,0:T(8,128)(2,1)S(1)}, bf16[64,24]{1,0:T(8,128)(2,1)S(1)}, u32[]{:S(2)}, u32[]{:S(2)}) collective-permute-start(bf16[64,24]{1,0:T(8,128)(2,1)S(1)} %get-tuple-element.70), channel_id=1, source_target_pairs={{0,30},{2,4},{4,2},{6,8},{8,6},{10,12},{12,10},{14,16},{16,14},{18... | collective-permute-start | bytes 9224 | tf_op jit(solution)/shard_map/ppermute | solution.py:495
  18.7 5.6 %collective-permute-start.4 = (bf16[64,24]{1,0:T(8,128)(2,1)S(1)}, bf16[64,24]{1,0:T(8,128)(2,1)S(1)}, u32[]{:S(2)}, u32[]{:S(2)}) collective-permute-start(bf16[64,24]{1,0:T(8,128)(2,1)S(1)} %get-tuple-element.78), channel_id=1, source_target_pairs={{0,2},{2,0},{4,6},{6,4},{8,10},{10,8},{12,14},{14,12},{16,18},{18,... | collective-permute-start | bytes 9224 | tf_op jit(solution)/shard_map/ppermute | solution.py:495
  18.8 5.9 %collective-permute-start.5 = (bf16[64,24]{1,0:T(8,128)(2,1)S(1)}, bf16[64,24]{1,0:T(8,128)(2,1)S(1)}, u32[]{:S(2)}, u32[]{:S(2)}) collective-permute-start(bf16[64,24]{1,0:T(8,128)(2,1)S(1)} %get-tuple-element.79), channel_id=1, source_target_pairs={{0,30},{2,4},{4,2},{6,8},{8,6},{10,12},{12,10},{14,16},{16,14},{18... | collective-permute-start | bytes 9224 | tf_op jit(solution)/shard_map/ppermute | solution.py:495
  27.9 6.3 %collective-permute-start.6 = (bf16[64,24]{1,0:T(8,128)(2,1)S(1)}, bf16[64,24]{1,0:T(8,128)(2,1)S(1)}, u32[]{:S(2)}, u32[]{:S(2)}) collective-permute-start(bf16[64,24]{1,0:T(8,128)(2,1)S(1)} %get-tuple-element.92), channel_id=1, source_target_pairs={{0,2},{2,0},{4,6},{6,4},{8,10},{10,8},{12,14},{14,12},{16,18},{18,... | collective-permute-start | bytes 9224 | tf_op jit(solution)/shard_map/ppermute | solution.py:495
  28.0 6.2 %collective-permute-start.7 = (bf16[64,24]{1,0:T(8,128)(2,1)S(1)}, bf16[64,24]{1,0:T(8,128)(2,1)S(1)}, u32[]{:S(2)}, u32[]{:S(2)}) collective-permute-start(bf16[64,24]{1,0:T(8,128)(2,1)S(1)} %get-tuple-element.93), channel_id=1, source_target_pairs={{0,30},{2,4},{4,2},{6,8},{8,6},{10,12},{12,10},{14,16},{16,14},{18... | collective-permute-start | bytes 9224 | tf_op jit(solution)/shard_map/ppermute | solution.py:495
  36.5 1.3 %collective-permute-start.8 = (bf16[64,512]{1,0:T(8,128)(2,1)S(1)}, bf16[64,512]{1,0:T(8,128)(2,1)S(1)}, u32[]{:S(2)}, u32[]{:S(2)}) collective-permute-start(bf16[64,512]{1,0:T(8,128)(2,1)S(1)} %get-tuple-element.108.mine_ref), channel_id=1, source_target_pairs={{0,2},{2,0},{4,6},{6,4},{8,10},{10,8},{12,14},{14,12},{16,18},{18,... | collective-permute-start | bytes 196616 | tf_op jit(solution)/shard_map/ppermute | solution.py:495
  37.9 4.3 %collective-permute-start.9 = (bf16[64,512]{1,0:T(8,128)(2,1)S(1)}, bf16[64,512]{1,0:T(8,128)(2,1)S(1)}, u32[]{:S(2)}, u32[]{:S(2)}) collective-permute-start(bf16[64,512]{1,0:T(8,128)(2,1)S(1)} %shard_map.197.mine_ref), channel_id=1, source_target_pairs={{0,4},{2,6},{4,0},{6,2},{8,12},{10,14},{12,8},{14,10},{16,20},{18,... | collective-permute-start | bytes 196616 | tf_op jit(solution)/shard_map/ppermute | solution.py:495
  42.3 4.3 %collective-permute-start.10 = (bf16[64,512]{1,0:T(8,128)(2,1)S(1)}, bf16[64,512]{1,0:T(8,128)(2,1)S(1)}, u32[]{:S(2)}, u32[]{:S(2)}) collective-permute-start(bf16[64,512]{1,0:T(8,128)(2,1)S(1)} %shard_map.198.mine_ref), channel_id=1, source_target_pairs={{0,8},{2,10},{4,12},{6,14},{8,0},{10,2},{12,4},{14,6},{16,24},{18,... | collective-permute-start | bytes 196616 | tf_op jit(solution)/shard_map/ppermute | solution.py:495
  46.7 5.9 %collective-permute-start.11 = (bf16[64,512]{1,0:T(8,128)(2,1)S(1)}, bf16[64,512]{1,0:T(8,128)(2,1)S(1)}, u32[]{:S(2)}, u32[]{:S(2)}) collective-permute-start(bf16[64,512]{1,0:T(8,128)(2,1)S(1)} %shard_map.199.mine_ref), channel_id=1, source_target_pairs={{0,16},{2,18},{4,20},{6,22},{8,24},{10,26},{12,28},{14,30},{16,0},... | collective-permute-start | bytes 196616 | tf_op jit(solution)/shard_map/ppermute | solution.py:495

commit v2 on v1

v2 whole, which is shorter than its diff:
```python
import functools
import math

import jax
import jax.numpy as jnp
from jax import lax
from jax.experimental import pallas as pl
from jax.experimental.pallas import tpu as pltpu
from jax.sharding import PartitionSpec as P

BF = jnp.bfloat16
F32 = jnp.float32
CHUNK = 512
LANES = 128
HBM = pltpu.HBM
VM = pltpu.VMEM


def mm(left, right):
    return jnp.dot(left, right, preferred_element_type=F32)


def mm_nt(left, right):
    return lax.dot_general(left, right, (((1,), (1,)), ((), ())), preferred_element_type=F32)


def flip(weight):
    return weight.astype(F32).T.astype(BF)


def halves(value):
    high = value.astype(BF)
    return high, (value - high.astype(F32)).astype(BF)


def wide_mm(weight, value):
    high, low = halves(value)
    return mm(jnp.concatenate([weight, weight], axis=1), jnp.concatenate([high, low], axis=0))


def sigmoid(value):
    return 0.5 + 0.5 * jnp.tanh(0.5 * value)


def add_to(total, value):
    return value if total is None else total + value


def chunks_of(count):
    return [slice(first, first + CHUNK) for first in range(0, count, CHUNK)]


def is_even():
    return lax.rem(lax.axis_index("phi"), 2) == 0


def pick(parts, natural):
    groups = len(parts)
    turn = lax.rem(lax.axis_index("layer") - natural + groups, groups)
    value = parts[0]
    for rank in range(1, groups):
        value = jnp.where(turn == rank, parts[rank], value)
    return value


def own_rows(slab_rows, width):
    layer = lax.axis_index("layer")
    value = slab_rows[:width]
    for rank in range(1, slab_rows.shape[0] // width):
        value = jnp.where(layer == rank, slab_rows[rank * width : (rank + 1) * width], value)
    return value


def split(value):
    high, low = halves(value)
    return jnp.concatenate([high, high, low], axis=1)


def split_mm(table, value):
    high, low = halves(value)
    return mm(table, jnp.concatenate([high, low, high], axis=0))


def pair_mm(table, value):
    return mm(table[:, value.shape[0] :], jnp.concatenate([value, value], axis=0))


def placed_rims(alpha, beta, upper_ref, lower_ref):
    even = is_even()
    from_upper = jnp.where(even, alpha, beta).astype(BF)
    from_lower = jnp.where(even, beta, alpha).astype(BF)
    return mm_nt(from_upper, upper_ref[...]) + mm_nt(from_lower, lower_ref[...])


def rim_gradients(ext_grad, slab, rim):
    even = is_even()
    below = ext_grad[:, slab : slab + rim]
    above = ext_grad[:, slab + rim : slab + 2 * rim]
    return jnp.where(even, above, below), jnp.where(even, below, above)


def slope_parts(pre):
    logistic = sigmoid(pre)
    value = pre * logistic
    return value, logistic + value * (1.0 - logistic)


def activate(base_ref, table, onehot_ref, slab, hidden_ref, slope_ref):
    wide = onehot_ref.shape[0] - slab
    total = None
    for cols in chunks_of(base_ref.shape[1]):
        rims = onehot_ref[slab:wide, cols]
        pre = base_ref[:, cols] + mm(table, jnp.concatenate([rims, rims], axis=0))
        value, slope = slope_parts(pre)
        hidden = value.astype(BF)
        hidden_ref[:, cols] = hidden
        slope_ref[:, cols] = slope
        total = add_to(total, mm_nt(hidden, onehot_ref[wide:, cols]))
    return total


def slab_base(source, target, own, bias, onehot_ref, edges_ref, base_ref):
    slab = source.shape[1]
    wide = onehot_ref.shape[0] - slab
    table = jnp.concatenate([*halves(source), *halves(target), own], axis=1)
    for cols in chunks_of(base_ref.shape[1]):
        near = onehot_ref[:slab, cols]
        hit = onehot_ref[wide:, cols]
        stack = jnp.concatenate([near, near, hit, hit, edges_ref[:, cols]], axis=0)
        base_ref[:, cols] = mm(table, stack) + bias[:, 0:1]


def node_base(state16, message, first_ref, bias):
    latent = state16.shape[0]
    return (
        mm(first_ref[:, :latent], state16)
        + wide_mm(first_ref[:, latent:], message)
        + bias[:, 2:3]
    )


def node_sums(grad, pre_grad, joined, hidden):
    return (
        mm_nt(pre_grad.astype(BF), joined),
        mm_nt(grad.astype(BF), hidden),
        jnp.sum(pre_grad, axis=1, keepdims=True),
        jnp.sum(grad, axis=1, keepdims=True),
    )


def prep_kernel(count_ref, source_hbm, target_hbm, feats_hbm, cot_hbm, upper_hbm, lower_hbm,
                out_ref, upper_ref, lower_ref, source, target, feats, cot, sems):
    pairs = ((source_hbm, source), (target_hbm, target), (feats_hbm, feats), (cot_hbm, cot),
             (upper_hbm, upper_ref), (lower_hbm, lower_ref))
    copies = [pltpu.make_async_copy(a, b, sems.at[place]) for place, (a, b) in enumerate(pairs)]
    for copy in copies:
        copy.start()
    for copy in copies:
        copy.wait()
    rows = source.shape[0]
    position = lax.broadcasted_iota(jnp.int32, (rows, LANES), 0) * LANES + lax.broadcasted_iota(
        jnp.int32, (rows, LANES), 1
    )
    valid = position < count_ref[0, 0]
    index = source[...]
    out_ref[:rows] = jnp.where(valid, index // LANES, -1).astype(F32).astype(BF)
    out_ref[rows : 2 * rows] = (index % LANES).astype(F32).astype(BF)
    out_ref[2 * rows : 3 * rows] = jnp.where(valid, target[...], -1).astype(F32).astype(BF)
    out_ref[3 * rows :] = jnp.concatenate([feats[...].astype(F32), cot[...]], axis=1).astype(BF)


def pick_kernel(packed_ref, upper, lower, upper_ref, lower_ref, alpha_pick, beta_pick):
    hits = lax.broadcasted_iota(jnp.int32, upper_ref.shape, 0)
    upper_ref[...] = (hits == upper[...]).astype(F32).astype(BF)
    lower_ref[...] = (hits == lower[...]).astype(F32).astype(BF)
    slab, room = alpha_pick.shape
    rim = upper.shape[1]
    first = jnp.concatenate([upper[...], jnp.full((1, room - rim), -1, jnp.int32)], axis=1)
    second = jnp.concatenate(
        [jnp.full((1, rim), -1, jnp.int32), lower[...], jnp.full((1, room - 2 * rim), -1, jnp.int32)], axis=1
    )
    even = is_even()
    hits = lax.broadcasted_iota(jnp.int32, (slab, room), 0)
    alpha_pick[...] = (hits == jnp.where(even, first, second)).astype(F32).astype(BF)
    beta_pick[...] = (hits == jnp.where(even, second, first)).astype(F32).astype(BF)


def slab_kernel(groups, rows, *refs):
    packs = [ref[3 * rows :].astype(F32) for ref in refs[:groups]]
    alpha_pick, beta_pick, slab_ref, cot_ref, alpha_ref, beta_ref = refs[groups:]
    latent = slab_ref.shape[0]
    both = jnp.concatenate([pick(packs, rank) for rank in range(groups)], axis=0).T
    slab16 = both[:latent].astype(BF)
    slab_ref[...] = slab16
    cot_ref[...] = both[latent:]
    alpha_ref[...] = mm(slab16, alpha_pick[...]).astype(BF)
    beta_ref[...] = mm(slab16, beta_pick[...]).astype(BF)


def onehot_kernel(groups, rows, rim, *refs):
    packs = [ref[: 3 * rows].astype(F32) for ref in refs[:groups]]
    (first_ref, second_ref, node_first_ref, node_second_ref, bias_ref, alpha_pick, beta_pick,
     onehot_ref, first_back, second_back, node_first_back, node_second_back, bias_out,
     to_node, to_node_back, to_table, to_table_back, to_hidden, alpha_place, beta_place) = refs[groups:]
    latent = first_ref.shape[0]
    slab, room = alpha_pick.shape
    wide = slab + room
    source_rows = lax.broadcasted_iota(jnp.int32, (wide, LANES), 0).astype(F32)
    target_rows = lax.broadcasted_iota(jnp.int32, (slab, LANES), 0).astype(F32)
    ones_row = source_rows == float(slab + 2 * rim)
    for rank in range(groups):
        pack = pick(packs, rank)
        source = jnp.where(pack[:rows] < 0.0, -1.0, pack[:rows] * LANES + pack[rows : 2 * rows])
        target = pack[2 * rows :]
        for row in range(rows):
            cols = slice((rank * rows + row) * LANES, (rank * rows + row + 1) * LANES)
            match = (source_rows == source[row : row + 1]) | ones_row
            onehot_ref[:wide, cols] = jnp.where(match, 1.0, 0.0).astype(BF)
            onehot_ref[wide:, cols] = jnp.where(target_rows == target[row : row + 1], 1.0, 0.0).astype(BF)
    first_back[...] = flip(first_ref[...])
    second_back[...] = flip(second_ref[...])
    node_first_back[...] = flip(node_first_ref[...])
    node_second_back[...] = flip(node_second_ref[...])
    bias_out[...] = bias_ref[...].T
    forward = mm(node_first_ref[:, latent:], second_ref[...])
    to_node[...] = split(forward)
    to_node_back[...] = split(forward.T)
    table = mm(first_ref[:, :latent], node_second_ref[...])
    to_table[...] = split(table)
    to_table_back[...] = split(table.T)
    to_hidden[...] = split(mm(first_ref[:, 2 * latent :], second_ref[...]).T)
    for choose, place in ((alpha_pick, alpha_place), (beta_pick, beta_place)):
        block = choose[...].astype(F32)
        none = jnp.zeros_like(block)
        place[...] = jnp.concatenate(
            [jnp.concatenate([block, none], axis=1), jnp.concatenate([none, block], axis=1)], axis=0
        ).astype(BF)


def start_kernel(groups, *refs):
    parts = refs[:groups]
    (onehot_ref, slab_ref, first_ref, node_first_ref, bias_ref,
     edges_ref, base_ref, message_ref, count_ref, node_base_ref, table_ref) = refs[groups:]
    latent, slab = slab_ref.shape
    wide = onehot_ref.shape[0] - slab
    slots = parts[0].shape[1]
    message = None
    count = None
    for rank in range(groups):
        for cols in chunks_of(slots):
            here = slice(rank * slots + cols.start, rank * slots + cols.stop)
            edges = pick([part[:, cols] for part in parts], rank)
            edges_ref[:, here] = edges
            hit = onehot_ref[wide:, here]
            message = add_to(message, mm_nt(edges, hit))
            count = add_to(count, mm_nt(jnp.ones((16, CHUNK), BF), hit))
    bias = bias_ref[...]
    count_ref[...] = count[:8]
    message = message + bias[:, 1:2] * count[0:1]
    message_ref[...] = message
    slab16 = slab_ref[...]
    source = mm(first_ref[:, :latent], slab16)
    target = mm(first_ref[:, latent : 2 * latent], slab16)
    slab_base(source, target, first_ref[:, 2 * latent :], bias, onehot_ref, edges_ref, base_ref)
    node_base_ref[...] = node_base(slab16, message, node_first_ref, bias)
    shift = wide_mm(first_ref[:, :latent], jnp.broadcast_to(bias[:, 3:4], (latent, LANES)))
    table_ref[...] = source + shift[:, :1]


def forward_kernel(base_ref, onehot_ref, slab_ref, beta_in, alpha_in, node_base_ref, table_in,
                   first_ref, node_second_ref, bias_ref, to_node, to_table, alpha_place, beta_place,
                   hidden_ref, slope_ref, rims_ref, sums_ref, node_pre_ref, node_hidden_ref, state_ref, table_ref,
                   alpha_ref, beta_ref):
    latent, slab = slab_ref.shape
    rims16 = alpha_in[...] + beta_in[...]
    rims_ref[...] = rims16
    table = jnp.concatenate(halves(mm(first_ref[:, :latent], rims16)), axis=1)
    sums = activate(base_ref, table, onehot_ref, slab, hidden_ref, slope_ref)
    sums_ref[...] = sums
    node_pre = node_base_ref[...] + split_mm(to_node[...], sums)
    node_pre_ref[...] = node_pre
    node_hidden = slope_parts(node_pre)[0].astype(BF)
    node_hidden_ref[...] = node_hidden
    table = table_in[...] + pair_mm(to_table[...], node_hidden)
    table_ref[...] = table
    both = jnp.concatenate(halves(table), axis=1)
    alpha_ref[...] = mm(both, alpha_place[...]).astype(BF)
    beta_ref[...] = mm(both, beta_place[...]).astype(BF)
    state = slab_ref[...].astype(F32) + mm(node_second_ref[...], node_hidden) + bias_ref[:, 3:4]
    state_ref[...] = state.astype(BF)


def between_kernel(edges_ref, hidden_ref, onehot_ref, slab_in, state_ref, table_ref, sums_ref, message_in, count_ref,
                   first_ref, second_ref, node_first_ref, bias_ref,
                   new_ref, base_ref, message_ref, joined_ref, node_base_ref):
    latent = edges_ref.shape[0]
    bias = bias_ref[...]
    second = second_ref[...]
    for cols in chunks_of(edges_ref.shape[1]):
        new_ref[:, cols] = (
            edges_ref[:, cols].astype(F32) + mm(second, hidden_ref[:, cols]) + bias[:, 1:2]
        ).astype(BF)
    state16 = state_ref[...]
    target = mm(first_ref[:, latent : 2 * latent], state16)
    slab_base(table_ref[...], target, first_ref[:, 2 * latent :], bias, onehot_ref, new_ref, base_ref)
    message = message_in[...] + wide_mm(second, sums_ref[...])
    joined_ref[...] = jnp.concatenate([slab_in[...], message.astype(BF)], axis=0)
    message = message + bias[:, 1:2] * count_ref[0:1]
    message_ref[...] = message
    node_base_ref[...] = node_base(state16, message, node_first_ref, bias)


def edge_gradient(wanted, extra_ref, slope_ref, onehot_ref, edges_ref, low_ref):
    slab = wanted.shape[1]
    wide = onehot_ref.shape[0] - slab
    table = jnp.concatenate(halves(wanted), axis=1)
    total = None
    for cols in chunks_of(edges_ref.shape[1]):
        hit = onehot_ref[wide:, cols]
        grad = mm(table, jnp.concatenate([hit, hit], axis=0))
        if extra_ref is not None:
            grad = grad + extra_ref[:, cols]
        pre_low = (grad * slope_ref[:, cols]).astype(BF)
        if low_ref is not None:
            low_ref[:, cols] = pre_low
        total = add_to(
            total, mm_nt(jnp.concatenate([onehot_ref[:, cols], edges_ref[:, cols]], axis=0), pre_low)
        )
    return total.T


def middle_kernel(base_ref, onehot_ref, edges_ref, beta_in, alpha_in, node_base_ref, cot_ref,
                  node_second_back, to_node, to_node_back,
                  hidden_ref, low_ref, sums_ref, node_pre_ref, node_grad_ref, wanted_ref, first_sums_ref, rims_ref,
                  slope_ref):
    slab = cot_ref.shape[1]
    wide = onehot_ref.shape[0] - slab
    cot_grad = mm(node_second_back[...], cot_ref[...].astype(BF))
    sums = activate(base_ref, alpha_in[...] + beta_in[...], onehot_ref, slab, hidden_ref, slope_ref)
    sums_ref[...] = sums
    node_pre = node_base_ref[...] + split_mm(to_node[...], sums)
    node_pre_ref[...] = node_pre
    pre_grad = cot_grad * slope_parts(node_pre)[1]
    node_grad_ref[...] = pre_grad
    wanted = split_mm(to_node_back[...], pre_grad)
    wanted_ref[...] = wanted
    first_sums = edge_gradient(wanted, None, slope_ref, onehot_ref, edges_ref, low_ref)
    rims_ref[...] = first_sums[:, slab:wide].astype(BF)
    first_sums_ref[...] = first_sums


def carry_kernel(rim, low_ref, hidden_zero_ref, slab_ref, sums_ref, sums_zero_ref, message_in,
                 node_pre_ref, node_grad_ref, first_sums_ref, count_ref, cot_ref,
                 second_ref, first_back, node_first_back, node_second_back, to_hidden,
                 extra_ref, total_ref, joined_ref, back_ref, back_node_ref):
    latent, slab = slab_ref.shape
    wide = first_sums_ref.shape[1] - slab - latent
    sums = first_sums_ref[...]
    cot = cot_ref[...]
    pre_grad = node_grad_ref[...]
    node_back = mm(node_first_back[...], pre_grad.astype(BF))
    gm = node_back[latent:].astype(BF)
    source = sums[:, :slab].astype(BF)
    target = sums[:, wide : wide + slab].astype(BF)
    back = cot + node_back[:latent] + mm(first_back[:latent], source) + mm(first_back[latent : 2 * latent], target)
    back_ref[...] = back
    back_node_ref[...] = wide_mm(node_second_back[...], back)
    self_back = first_back[2 * latent :]
    cross = None
    for cols in chunks_of(low_ref.shape[1]):
        low = low_ref[:, cols]
        extra_ref[:, cols] = pair_mm(to_hidden[...], low)
        cross = add_to(cross, mm_nt(low, hidden_zero_ref[:, cols]))
    slab16 = slab_ref[...]
    message = message_in[...] + wide_mm(second_ref[...], sums_ref[...])
    joined = jnp.concatenate([slab16, message.astype(BF)], axis=0)
    joined_ref[...] = joined
    pre_sum = sums[:, slab + 2 * rim : slab + 2 * rim + 1]
    edge_two = (
        mm_nt(gm, sums_ref[...].astype(BF))
        + mm_nt(gm, sums_zero_ref[...].astype(BF))
        + mm(self_back, cross.astype(BF))
    )
    gm_sum = 2.0 * jnp.sum(gm.astype(F32) * count_ref[0:1], axis=1, keepdims=True) + wide_mm(
        self_back, jnp.broadcast_to(pre_sum, (latent, LANES))
    )[:, :1]
    node_one, node_two, node_pre_sum, cot_sum = node_sums(
        cot, pre_grad, joined, slope_parts(node_pre_ref[...])[0].astype(BF)
    )
    edge_one = jnp.concatenate(
        [mm_nt(source, slab16), mm_nt(target, slab16), sums[:, wide + slab :]], axis=1
    )
    used = edge_one.shape[1] + edge_two.shape[1] + node_one.shape[1] + node_two.shape[1]
    pad = jnp.zeros((latent, total_ref.shape[1] - used - 4), F32)
    total_ref[...] = jnp.concatenate(
        [edge_one, edge_two, node_one, node_two, pre_sum, gm_sum, node_pre_sum, cot_sum, pad], axis=1
    )


def output_kernel(count_ref, edges_ref, hidden_ref, joined_ref, node_pre_ref, second_ref, node_second_ref, bias_ref,
                  edge_out, node_out, new_ref):
    bias = bias_ref[...]
    latent = edges_ref.shape[0]
    second = second_ref[...]
    for cols in chunks_of(edges_ref.shape[1]):
        new_ref[:, cols] = (
            edges_ref[:, cols].astype(F32) + mm(second, hidden_ref[:, cols]) + bias[:, 1:2]
        ).astype(BF)
    slots = edge_out.shape[1]
    begin = lax.axis_index("layer") * slots
    for cols in chunks_of(slots):
        position = lax.broadcasted_iota(jnp.int32, (latent, CHUNK), 1) + cols.start
        mine = new_ref[:, pl.ds(pl.multiple_of(begin + cols.start, CHUNK), CHUNK)].astype(F32)
        edge_out[:, cols] = jnp.where(position < count_ref[0, 0], mine, 0.0).astype(BF)
    node_hidden = slope_parts(node_pre_ref[...])[0].astype(BF)
    state = joined_ref[:latent].astype(F32) + mm(node_second_ref[...], node_hidden) + bias[:, 3:4]
    node_out[...] = own_rows(state.T, node_out.shape[0]).astype(BF)


def last_kernel(rim, back_in, back_node, beta_in, alpha_in, alpha_pick, beta_pick, joined_ref, node_pre_ref,
                node_hidden_ref, wanted_in, sums_ref, count_ref, extra_ref, slope_ref, onehot_ref, edges_ref,
                slab_ref, rims_ref, slab_one_ref, total_in, first_back, node_first_back, to_node_back, to_table_back,
                total_ref, back_ref):
    latent, slab = slab_ref.shape
    wide = onehot_ref.shape[0] - slab
    placed = mm_nt(alpha_in[...], alpha_pick[...]) + mm_nt(beta_in[...], beta_pick[...])
    pre_grad = (back_node[...] + split_mm(to_table_back[...], placed)) * slope_parts(node_pre_ref[...])[1]
    wanted = wanted_in[...] + split_mm(to_node_back[...], pre_grad)
    sums = edge_gradient(wanted, extra_ref, slope_ref, onehot_ref, edges_ref, None)
    source = sums[:, :wide].astype(BF)
    target = sums[:, wide : wide + slab].astype(BF)
    ext_grad = mm(first_back[:latent], source)
    node_back = mm(node_first_back[...], pre_grad.astype(BF))
    gm = node_back[latent:].astype(BF)
    grad = back_in[...] + wide_mm(first_back[:latent], placed)
    back_ref[...] = (
        grad + node_back[:latent] + ext_grad[:, :slab] + mm(first_back[latent : 2 * latent], target)
    )
    alpha, beta = rim_gradients(ext_grad, slab, rim)
    node_one, node_two, node_pre_sum, grad_sum = node_sums(grad, pre_grad, joined_ref[...], node_hidden_ref[...])
    slab16 = slab_ref[...]
    ext16 = jnp.concatenate([slab16, rims_ref[...]], axis=1)
    edge_one = jnp.concatenate(
        [
            mm_nt(source, ext16) + mm_nt(placed.astype(BF), slab_one_ref[...]),
            mm_nt(target, slab16),
            sums[:, wide + slab :],
        ],
        axis=1,
    )
    edge_two = mm_nt(gm, sums_ref[...].astype(BF))
    pre_sum = sums[:, slab + 2 * rim : slab + 2 * rim + 1]
    gm_sum = jnp.sum(gm.astype(F32) * count_ref[0:1], axis=1, keepdims=True)
    used = edge_one.shape[1] + edge_two.shape[1] + node_one.shape[1] + node_two.shape[1]
    pad = jnp.zeros((latent, total_ref.shape[1] - used - 4 - 2 * rim), F32)
    total_ref[...] = (
        total_in[...]
        + jnp.concatenate(
            [edge_one, edge_two, node_one, node_two, pre_sum, gm_sum, node_pre_sum, grad_sum, alpha, beta, pad],
            axis=1,
        )
    ).astype(BF)


def add_kernel(used, rim, bit, mine_ref, other_ref, out_ref):
    mine = mine_ref[...].astype(F32)
    other = other_ref[...].astype(F32)
    lane = lax.broadcasted_iota(jnp.int32, mine.shape, 1)
    held = other[:, used + rim : used + 2 * rim]
    if bit == 1:
        arrived = jnp.zeros_like(held)
        passing = held
    else:
        place = lax.axis_index("phi")
        home = (lax.rem(place // bit, 2) == 1) == (lax.rem(place, 2) == 0)
        arrived = mine[:, used : used + rim] + jnp.where(home, held, 0.0)
        passing = jnp.where(home, 0.0, held)
    pad = jnp.zeros((mine.shape[0], mine.shape[1] - used - 2 * rim), F32)
    out_ref[...] = jnp.concatenate(
        [(mine + other)[:, :used], arrived, passing, pad], axis=1
    ).astype(BF)


def finish_kernel(used, rim, mine_ref, other_ref, back_ref, alpha_in, upper_ref, lower_ref,
                  node_grad, edge_one, edge_two, node_one, node_two, bias_out):
    mine = mine_ref[...].astype(F32)
    other = other_ref[...].astype(F32)
    total = mine + other
    cut = 0
    for ref in (edge_one, edge_two, node_one, node_two):
        ref[...] = total[:, cut : cut + ref.shape[1]]
        cut += ref.shape[1]
    block = used - 4 - (used - 4) % LANES
    turned = total[:, block : block + LANES].T
    bias_out[...] = turned[used - 4 - block : used - block]
    alpha = alpha_in[...].astype(F32)[:, used : used + rim]
    beta = mine[:, used : used + rim] + other[:, used + rim : used + 2 * rim]
    grad = back_ref[...] + placed_rims(alpha, beta, upper_ref, lower_ref)
    node_grad[...] = own_rows(grad.T, node_grad.shape[0])


def call(kernel, outs, *args, scratch=(), smem=0, hbm=(), cost=1.0):
    args = [
        pltpu.with_memory_space_constraint(arg, HBM) if place in hbm else arg for place, arg in enumerate(args)
    ]
    held = [(arg.shape, arg.dtype) for arg in args] + list(outs)
    held += [(ref.shape, ref.dtype) for ref in scratch if jnp.issubdtype(ref.dtype, jnp.number)]
    room = sum(math.prod(shape) * jnp.dtype(kind).itemsize for shape, kind in held)
    spaces = [pltpu.SMEM if place < smem else HBM if place in hbm else VM for place in range(len(args))]
    specs = [pl.BlockSpec(memory_space=space) for space in spaces]
    return pl.pallas_call(
        kernel,
        out_shape=[jax.ShapeDtypeStruct(shape, kind) for shape, kind in outs],
        in_specs=specs,
        out_specs=[pl.BlockSpec(memory_space=VM) for _ in outs],
        scratch_shapes=list(scratch),
        compiler_params=pltpu.CompilerParams(vmem_limit_bytes=room + 10 * 1024 * 1024),
        cost_estimate=pl.CostEstimate(
            flops=int(cost * 1e9), bytes_accessed=int(cost * 3.6e6), transcendentals=0
        ),
    )(*args)


def swap(value, axis, pairing):
    count = lax.axis_size(axis)
    return lax.ppermute(value, axis, [(source, pairing(source) % count) for source in range(count)])


def by_alpha(value):
    return swap(value, "phi", lambda index: index ^ 1)


def by_beta(value):
    return swap(value, "phi", lambda index: index - 1 if index % 2 == 0 else index + 1)


def layer_parts(value):
    groups = lax.axis_size("layer")
    return [value] + [
        swap(value, "layer", lambda index, turn=turn: index + turn) for turn in range(1, groups)
    ]


def body(node_feats, edge_feats, edge_source, edge_target, edge_counts, rim_upper, rim_lower,
         edge_first, edge_second, node_first, node_second, biases, node_cot):
    groups = lax.axis_size("layer")
    ring = lax.axis_size("phi")
    latent, width = node_feats.shape
    hidden = edge_second.shape[1]
    slots = edge_feats.shape[1]
    slab = width * groups
    rim = rim_upper.shape[1]
    wide = (slab + 2 * rim) // LANES * LANES + LANES
    total_slots = slots * groups
    rows = slots // LANES
    room = wide - slab
    rim_shape = ((latent, room), BF)
    per_slot = lambda kind: ((latent, total_slots), kind)
    per_hit = lambda kind, depth=1: ((depth * latent, slab), kind)

    packed, upper, lower = call(
        prep_kernel,
        [((3 * rows + width, LANES), BF), ((1, rim), jnp.int32), ((1, rim), jnp.int32)],
        edge_counts, edge_source.reshape(rows, LANES), edge_target.reshape(rows, LANES),
        node_feats.T, node_cot.T, rim_upper, rim_lower,
        scratch=[VM((rows, LANES), jnp.int32), VM((rows, LANES), jnp.int32),
                 VM((width, latent), BF), VM((width, latent), F32), pltpu.SemaphoreType.DMA((6,))],
        smem=1, hbm=range(1, 7),
    )
    packs = layer_parts(packed)
    upper, lower, alpha_pick, beta_pick = call(
        pick_kernel,
        [((slab, rim), BF), ((slab, rim), BF), ((slab, room), BF), ((slab, room), BF)],
        packed, upper, lower, cost=0.1,
    )
    later, _ = lax.optimization_barrier((edge_feats, alpha_pick))
    parts = [edge_feats] + layer_parts(later)[1:]
    slab_zero, cot, alpha, beta = call(
        functools.partial(slab_kernel, groups, rows),
        [per_hit(BF), per_hit(F32), rim_shape, rim_shape], *packs, alpha_pick, beta_pick, cost=20.0,
    )
    beta = by_beta(beta)
    alpha = by_alpha(alpha)
    (onehot, first_back, second_back, node_first_back, node_second_back, bias,
     to_node, to_node_back, to_table, to_table_back, to_hidden, alpha_place, beta_place) = call(
        functools.partial(onehot_kernel, groups, rows, rim),
        [((wide + slab, total_slots), BF), (edge_first.shape[::-1], BF), (edge_second.shape[::-1], BF),
         (node_first.shape[::-1], BF), (node_second.shape[::-1], BF), (biases.shape[::-1], F32)]
        + [((hidden, 3 * hidden), BF)] * 5 + [((2 * slab, 2 * room), BF)] * 2,
        *packs, edge_first, edge_second, node_first, node_second, biases, alpha_pick, beta_pick, cost=2.0,
    )
    edges_zero, base, message, count, node_base_zero, table = call(
        functools.partial(start_kernel, groups),
        [per_slot(BF), per_slot(F32), per_hit(F32), ((8, slab), F32), per_hit(F32), per_hit(F32)],
        *parts, onehot, slab_zero, edge_first, node_first, bias, cost=1.0,
    )
    (hidden_zero, slope, rims_zero, sums_zero, node_pre_zero, node_hidden_zero, slab_one, table,
     alpha, beta) = call(
        forward_kernel,
        [per_slot(BF), per_slot(F32), rim_shape, per_hit(F32), per_hit(F32), per_hit(BF), per_hit(BF), per_hit(F32),
         ((latent, 2 * room), BF), ((latent, 2 * room), BF)],
        base, onehot, slab_zero, beta, alpha, node_base_zero, table, edge_first, node_second, bias, to_node, to_table,
        alpha_place, beta_place, cost=2.0,
    )
    beta = by_beta(beta)
    alpha = by_alpha(alpha)
    edges_one, base, message, joined_zero, node_base_one = call(
        between_kernel, [per_slot(BF), per_slot(F32), per_hit(F32), per_hit(BF, 2), per_hit(F32)],
        edges_zero, hidden_zero, onehot, slab_zero, slab_one, table, sums_zero, message, count,
        edge_first, edge_second, node_first, bias, cost=2.0,
    )
    total_width = edge_first.shape[1] + hidden + node_first.shape[1] + node_second.shape[1] + 4
    lanes = -(-(total_width + 2 * rim) // LANES) * LANES
    hidden_one, low, sums_one, node_pre_one, node_grad_one, wanted, first_sums, rims = call(
        middle_kernel,
        [per_slot(BF), per_slot(BF), per_hit(F32), per_hit(F32), per_hit(F32), per_hit(F32),
         ((hidden, wide + slab + latent), F32), rim_shape],
        base, onehot, edges_one, beta, alpha, node_base_one, cot, node_second_back, to_node, to_node_back,
        scratch=[VM((hidden, total_slots), F32)], cost=3.0,
    )
    beta = by_beta(rims)
    alpha = by_alpha(rims)
    extra, total, joined_one, back, back_node = call(
        functools.partial(carry_kernel, rim),
        [per_slot(F32), ((latent, lanes), F32), per_hit(BF, 2), per_hit(F32), per_hit(F32)],
        low, hidden_zero, slab_one, sums_one, sums_zero, message, node_pre_one, node_grad_one, first_sums, count, cot,
        edge_second, first_back, node_first_back, node_second_back, to_hidden, cost=2.0,
    )
    edge_out, node_out = call(
        output_kernel, [((latent, slots), BF), ((width, latent), BF)],
        edge_counts, edges_one, hidden_one, joined_one, node_pre_one, edge_second, node_second, bias,
        scratch=[VM((latent, total_slots), BF)], smem=1, cost=2.0,
    )
    total, back = call(
        functools.partial(last_kernel, rim), [((latent, lanes), BF), per_hit(F32)],
        back, back_node, beta, alpha, alpha_pick, beta_pick, joined_zero, node_pre_zero, node_hidden_zero, wanted,
        sums_zero, count, extra, slope, onehot, edges_zero, slab_zero, rims_zero, slab_one, total,
        first_back, node_first_back, to_node_back, to_table_back, cost=2.0,
    )
    other = by_alpha(total)
    alpha_last = other
    bit = 1
    while 2 * bit < ring:
        total = call(
            functools.partial(add_kernel, total_width, rim, bit), [((latent, lanes), BF)], total, other, cost=0.1,
        )[0]
        bit *= 2
        other = swap(total, "phi", lambda index, bit=bit: index ^ bit)
    node_grad, edge_one, edge_two, node_one, node_two, bias_out = call(
        functools.partial(finish_kernel, total_width, rim),
        [((width, latent), F32), (edge_first.shape, F32), (edge_second.shape, F32),
         (node_first.shape, F32), (node_second.shape, F32), (biases.shape, F32)],
        total, other, back, alpha_last, upper, lower,
    )
    return node_out.T, edge_out, node_grad.T, edge_one, edge_two, node_one, node_two, bias_out


def solution(mesh):
    split = P(None, ("phi", "layer"))
    return jax.shard_map(
        body,
        mesh=mesh,
        in_specs=(split, split, P(("phi", "layer")), P(("phi", "layer")), P("phi", "layer"),
                  P("phi", None), P("phi", None), P(), P(), P(), P(), P(), split),
        out_specs=(split, split, split, P(), P(), P(), P(), P()),
        check_vma=False,
    )
```

time: 53.7 us -> 49.4 us (0.920)
  starting transfers between devices: 19 us -> 12.7 us
  waiting for transfers between devices: 18.7 us -> 20.6 us
    ppermute x12, starting transfers between devices: 19 us -> 12.7 us  [swap(): lax.ppermute(value, axis, [(source, pairing(source) % count) for source i...]
    ppermute x12, waiting for transfers between devices: 18.7 us -> 20.6 us  [swap(): lax.ppermute(value, axis, [(source, pairing(source) % count) for source i...]
    pallas_call x13 -> x15, Pallas kernels: 14.4 us -> 14.5 us  [call(): pl.pallas_call(kernel, out_shape=[jax.ShapeDtypeStruct(shape, kind) for s...]
  transfers between devices with their start and end apart: 12 -> 12, of which waited for: 7 -> 8; matrix products, arithmetic and copies ran while one was open for 0% -> 0% of each run, Pallas kernels for 12% -> 12%
where the time goes in v2:
time: 49.4 us; the launch traced here: 49.3 us
  waiting for transfers between devices  20.6 us (42%)
  Pallas kernels  14.5 us (29%)
  starting transfers between devices  12.7 us (26%)
  between operations  1.43 us (3%)
    ppermute x12, waiting for transfers between devices, swap(): lax.ppermute(value, axis, [(source, pairing(source) % count) for source i...  20.6 us
    pallas_call x15, Pallas kernels, call(): pl.pallas_call(kernel, out_shape=[jax.ShapeDtypeStruct(shape, kind) for s...  14.5 us
    ppermute x12, starting transfers between devices, swap(): lax.ppermute(value, axis, [(source, pairing(source) % count) for source i...  12.7 us
  transfers between devices with their start and end apart: 12, of which 8 were waited for; matrix products, arithmetic and copies ran while one was open for 0% of the time, Pallas kernels for 12%

profile of v2, /device:TPU:0, one launch (start us, length us, event | category | flops | bytes accessed | tf_op | source)
XLA Modules:
  0.0 49.3 jit_solution(15173993097220453593)
XLA Ops:
  1.3 0.0 copy-start
  1.3 0.9 %shard_map.188 = (bf16[80,128]{1,0:T(8,128)(2,1)S(1)}, s32[1,24]{1,0:T(1,128)S(1)}, s32[1,24]{1,0:T(1,128)S(1)}) custom-call(s32[1,1]{1,0:T(1,128)S(6)} %copy.21.count_ref, s32[16,128]{1,0:T(8,128)} %bitcast.7, s32[16,128]{1,0:T(8,128)} %bitcast.8, bf16[32,64]{1,0:T(8,128)(2,1)} %bitcast.9, f32[32,64]{1,0:T(8,128)} %bitcast.6, s32[1,24]{1,0:T(1,128)} %upper_hbm.1, ...), custom_call_target="tpu_custom_call" | custom-call | flops 1000000000 | bytes 3600000 | tf_op jit(solution)/shard_map/pallas_call | solution.py:511
  2.2 3.0 %collective-permute-start.1 = (bf16[80,128]{1,0:T(8,128)(2,1)S(1)}, bf16[80,128]{1,0:T(8,128)(2,1)S(1)}, u32[]{:S(2)}, u32[]{:S(2)}) collective-permute-start(bf16[80,128]{1,0:T(8,128)(2,1)S(1)} %get-tuple-element.76.packed_ref.refs_0_), channel_id=1, source_target_pairs={{0,1},{1,0},{2,3},{3,2},{4,5},{5,4},{6,7},{7,6},{8,9},{9,8},{10,11... | collective-permute-start | bytes 61448 | tf_op jit(solution)/shard_map/ppermute | solution.py:526
  5.2 0.1 shard_map.189
  5.3 0.0 copy-done
  5.3 0.1 collective-permute-start
  5.4 1.6 %collective-permute-done.1.refs_1_ = bf16[80,128]{1,0:T(8,128)(2,1)S(1)} collective-permute-done((bf16[80,128]{1,0:T(8,128)(2,1)S(1)}, bf16[80,128]{1,0:T(8,128)(2,1)S(1)}, u32[]{:S(2)}, u32[]{:S(2)}) %collective-permute-start.1) | collective-permute-done | bytes 20512 | tf_op jit(solution)/shard_map/ppermute | solution.py:526
  7.0 0.0 copy-start.1
  7.0 0.0 copy-start.2
  7.0 0.0 copy-start.5
  7.0 0.2 shard_map.191
  7.2 3.4 %collective-permute-start.2 = (bf16[64,64]{1,0:T(8,128)(2,1)S(1)}, bf16[64,64]{1,0:T(8,128)(2,1)S(1)}, u32[]{:S(2)}, u32[]{:S(2)}) collective-permute-start(bf16[64,64]{1,0:T(8,128)(2,1)S(1)} %get-tuple-element.87), channel_id=1, source_target_pairs={{0,30},{2,4},{4,2},{6,8},{8,6},{10,12},{12,10},{14,16},{16,14},{18... | collective-permute-start | bytes 24584 | tf_op jit(solution)/shard_map/ppermute | solution.py:526
  10.6 0.0 collective-permute-start.3
  10.6 0.0 copy-done.1
  10.6 0.0 copy-done.2
  10.6 0.0 copy-done.3
  10.6 0.0 copy-done.4
  10.7 0.0 copy-done.5
  10.7 1.3 %shard_map.190 = (bf16[192,4096]{1,0:T(8,128)(2,1)S(1)}, bf16[192,64]{1,0:T(8,128)(2,1)S(1)}, bf16[64,64]{1,0:T(8,128)(2,1)}, bf16[128,64]{1,0:T(8,128)(2,1)S(1)...) custom-call(bf16[80,128]{1,0:T(8,128)(2,1)S(1)} %get-tuple-element.7, ...), custom_call_target="tpu_custom_call" | custom-call | flops 2000000000 | bytes 7200000 | tf_op jit(solution)/shard_map/pallas_call | solution.py:511
  12.0 1.2 %collective-permute-done.refs_1_ = bf16[64,2048]{1,0:T(8,128)(2,1)S(1)} collective-permute-done((bf16[64,2048]{1,0:T(8,128)(2,1)S(1)}, bf16[64,2048]{1,0:T(8,128)(2,1)S(1)}, u32[]{:S(2)}, u32[]{:S(2)}) %collective-permute-start) | collective-permute-done | bytes 262176 | tf_op jit(solution)/shard_map/ppermute | solution.py:526
  13.2 1.2 %shard_map.192 = (bf16[64,4096]{1,0:T(8,128)(2,1)S(1)}, f32[64,4096]{1,0:T(8,128)S(1)}, f32[64,64]{1,0:T(8,128)S(1)}, f32[8,64]{1,0:T(8,128)S(1)}, f32[64,64]{1,0:T(8,128)S(1)}, /*index=5*/f32[64,64]{1,0:T(8,128)S(1)}) custom-call(bf16[64,2048]{1,0:T(8,128)(2,1)S(1)} %copy-done, bf16[64,2048]{1,0:T(8,128)(2,1)S(1)} %collective-permute-done.refs_1_, ...), custom_call_target="tpu_custom_call" | custom-call | flops 1000000000 | bytes 3600000 | tf_op jit(solution)/shard_map/pallas_call | solution.py:511
  14.4 0.0 collective-permute-done.2.beta_in
  14.4 0.0 collective-permute-done.3.alpha_in
  14.4 1.4 %shard_map.193 = (bf16[64,4096]{1,0:T(8,128)(2,1)S(1)}, f32[64,4096]{1,0:T(8,128)S(1)}, bf16[64,64]{1,0:T(8,128)(2,1)S(1)}, f32[64,64]{1,0:T(8,128)S(1)}, f32[64...) custom-call(f32[64,4096]{1,0:T(8,128)S(1)} %get-tuple-element.86.bas, ...), custom_call_target="tpu_custom_call" | custom-call | flops 2000000000 | bytes 7200000 | tf_op jit(solution)/shard_map/pallas_call | solution.py:511
  15.8 2.9 %collective-permute-start.4 = (bf16[64,128]{1,0:T(8,128)(2,1)S(1)}, bf16[64,128]{1,0:T(8,128)(2,1)S(1)}, u32[]{:S(2)}, u32[]{:S(2)}) collective-permute-start(bf16[64,128]{1,0:T(8,128)(2,1)S(1)} %get-tuple-element.103), channel_id=1, source_target_pairs={{0,30},{2,4},{4,2},{6,8},{8,6},{10,12},{12,10},{14,16},{16,14},{18... | collective-permute-start | bytes 49160 | tf_op jit(solution)/shard_map/ppermute | solution.py:526
  18.6 0.0 collective-permute-start.5
  18.6 1.1 %shard_map.194 = (bf16[64,4096]{1,0:T(8,128)(2,1)S(1)}, f32[64,4096]{1,0:T(8,128)S(1)}, f32[64,64]{1,0:T(8,128)S(1)}, bf16[128,64]{1,0:T(8,128)(2,1)S(1)}, f32[64,64]{1,0:T(8,128)S(1)}) custom-call(bf16[64,4096]{1,0:T(8,128)(2,1)S(1)} %get-tuple-element.85.edges_ref, bf16[64,4096]{1,0:T(8,128)(2,1)S(1)} %get-tuple-element.95.hidden_ref.hidden_zero_ref, ...), custom_call_target="tpu_custom_call" | custom-call | flops 2000000000 | bytes 7200000 | tf_op jit(solution)/shard_map/pallas_call | solution.py:511
  19.7 2.0 %collective-permute-done.4.beta_in = bf16[64,128]{1,0:T(8,128)(2,1)S(1)} collective-permute-done((bf16[64,128]{1,0:T(8,128)(2,1)S(1)}, bf16[64,128]{1,0:T(8,128)(2,1)S(1)}, u32[]{:S(2)}, u32[]{:S(2)}) %collective-permute-start.4) | collective-permute-done | bytes 16416 | tf_op jit(solution)/shard_map/ppermute | solution.py:526
  21.7 0.0 collective-permute-done.5.alpha_in
  21.7 2.7 %shard_map.195 = (bf16[64,4096]{1,0:T(8,128)(2,1)S(1)}, bf16[64,4096]{1,0:T(8,128)(2,1)S(1)}, f32[64,64]{1,0:T(8,128)S(1)}, f32[64,64]{1,0:T(8,128)S(1)}, f32[64...) custom-call(f32[64,4096]{1,0:T(8,128)S(1)} %get-tuple-element.102.base_ref, ...), custom_call_target="tpu_custom_call" | custom-call | flops 3000000000 | bytes 10800000 | tf_op jit(solution)/shard_map/pallas_call | solution.py:511
  24.4 2.9 %collective-permute-start.6 = (bf16[64,64]{1,0:T(8,128)(2,1)S(1)}, bf16[64,64]{1,0:T(8,128)(2,1)S(1)}, u32[]{:S(2)}, u32[]{:S(2)}) collective-permute-start(bf16[64,64]{1,0:T(8,128)(2,1)S(1)} %get-tuple-element.124), channel_id=1, source_target_pairs={{0,30},{2,4},{4,2},{6,8},{8,6},{10,12},{12,10},{14,16},{16,14},{18... | collective-permute-start | bytes 24584 | tf_op jit(solution)/shard_map/ppermute | solution.py:526
  27.3 0.0 collective-permute-start.7
  27.3 0.9 %shard_map.196 = (f32[64,4096]{1,0:T(8,128)S(1)}, f32[64,512]{1,0:T(8,128)S(1)}, bf16[128,64]{1,0:T(8,128)(2,1)S(1)}, f32[64,64]{1,0:T(8,128)S(1)}, f32[64,64]{1,0:T(8,128)S(1)}) custom-call(bf16[64,4096]{1,0:T(8,128)(2,1)S(1)} %get-tuple-element.110.low_ref, bf16[64,4096]{1,0:T(8,128)(2,1)S(1)} %get-tuple-element.95.hidden_ref.hidden_zero_ref, ...), custom_call_target="tpu_custom_call" | custom-call | flops 2000000000 | bytes 7200000 | tf_op jit(solution)/shard_map/pallas_call | solution.py:511
  28.1 2.2 %collective-permute-done.6.beta_in = bf16[64,64]{1,0:T(8,128)(2,1)S(1)} collective-permute-done((bf16[64,64]{1,0:T(8,128)(2,1)S(1)}, bf16[64,64]{1,0:T(8,128)(2,1)S(1)}, u32[]{:S(2)}, u32[]{:S(2)}) %collective-permute-start.6) | collective-permute-done | bytes 8224 | tf_op jit(solution)/shard_map/ppermute | solution.py:526
  30.3 0.0 collective-permute-done.7.alpha_in
  30.3 2.5 %shard_map.198 = (bf16[64,512]{1,0:T(8,128)(2,1)S(1)}, f32[64,64]{1,0:T(8,128)S(1)}) custom-call(f32[64,64]{1,0:T(8,128)S(1)} %get-tuple-element.122.back_in, f32[64,64]{1,0:T(8,128)S(1)} %get-tuple-element.123.back_node, bf16[64,64]{1,0:T(8,128)(2,1)S(1)} %collective-permute-done.6.beta_in, bf16[64,64]{1,0:T(8,128)(2,1)S(1)} %collective-permute-done.7.alpha_in, ...), custom_call_target="tpu_custom_call" | custom-call | flops 2000000000 | bytes 7200000 | tf_op jit(solution)/shard_map/pallas_call | solution.py:511
  32.8 0.1 collective-permute-start.8
  32.9 1.2 %collective-permute-done.8.other_ref.alpha_in = bf16[64,512]{1,0:T(8,128)(2,1)S(1)} collective-permute-done((bf16[64,512]{1,0:T(8,128)(2,1)S(1)}, bf16[64,512]{1,0:T(8,128)(2,1)S(1)}, u32[]{:S(2)}, u32[]{:S(2)}) %collective-permute-start.8) | collective-permute-done | bytes 65568 | tf_op jit(solution)/shard_map/ppermute | solution.py:526
  34.2 0.1 collective-permute-start.9
  34.2 4.3 %collective-permute-done.9.other_ref = bf16[64,512]{1,0:T(8,128)(2,1)S(1)} collective-permute-done((bf16[64,512]{1,0:T(8,128)(2,1)S(1)}, bf16[64,512]{1,0:T(8,128)(2,1)S(1)}, u32[]{:S(2)}, u32[]{:S(2)}) %collective-permute-start.9) | collective-permute-done | bytes 65568 | tf_op jit(solution)/shard_map/ppermute | solution.py:526
  38.5 0.1 shard_map.200.mine_ref
  38.6 0.0 collective-permute-start.10
  38.6 4.3 %collective-permute-done.10.other_ref = bf16[64,512]{1,0:T(8,128)(2,1)S(1)} collective-permute-done((bf16[64,512]{1,0:T(8,128)(2,1)S(1)}, bf16[64,512]{1,0:T(8,128)(2,1)S(1)}, u32[]{:S(2)}, u32[]{:S(2)}) %collective-permute-start.10) | collective-permute-done | bytes 65568 | tf_op jit(solution)/shard_map/ppermute | solution.py:526
  42.9 0.1 shard_map.201.mine_ref
  43.0 0.3 collective-permute-start.11
  43.3 1.1 %shard_map.197 = (bf16[64,2048]{1,0:T(8,128)(2,1)}, bf16[32,64]{1,0:T(8,128)(2,1)}) custom-call(s32[1,1]{1,0:T(1,128)S(6)} %copy.21.count_ref, bf16[64,4096]{1,0:T(8,128)(2,1)S(1)} %get-tuple-element.101.edges_ref, bf16[64,4096]{1,0:T(8,128)(2,1)S(1)} %get-tuple-element.109.hidden_ref, bf16[128,64]{1,0:T(8,128)(2,1)S(1)} %get-tuple-element.119.joined_ref, ...), custom_call_target="tpu_custom_call" | custom-call | flops 2000000000 | bytes 7200000 | tf_op jit(solution)/shard_map/pallas_call | solution.py:511
  44.4 3.9 %collective-permute-done.11.other_ref = bf16[64,512]{1,0:T(8,128)(2,1)S(1)} collective-permute-done((bf16[64,512]{1,0:T(8,128)(2,1)S(1)}, bf16[64,512]{1,0:T(8,128)(2,1)S(1)}, u32[]{:S(2)}, u32[]{:S(2)}) %collective-permute-start.11) | collective-permute-done | bytes 65568 | tf_op jit(solution)/shard_map/ppermute | solution.py:526
  48.3 1.0 %shard_map.202 = (f32[32,64]{1,0:T(8,128)}, f32[64,192]{1,0:T(8,128)}, f32[64,64]{1,0:T(8,128)}, f32[64,128]{1,0:T(8,128)}, f32[64,64]{1,0:T(8,128)}, /*index=5*/f32[4,64]{1,0:T(4,128)}) custom-call(bf16[64,512]{1,0:T(8,128)(2,1)S(1)} %shard_map.201.mine_ref, bf16[64,512]{1,0:T(8,128)(2,1)S(1)} %collective-permute-done.11.other_ref, ...), custom_call_target="tpu_custom_call" | custom-call | flops 1000000000 | bytes 3600000 | tf_op jit(solution)/shard_map/pallas_call | solution.py:511
  (3 shorter events, 0.0 us)
Async XLA Ops:
  1.3 4.0 %copy-start = (bf16[64,2048]{1,0:T(8,128)(2,1)S(1)}, bf16[64,2048]{1,0:T(8,128)(2,1)}, u32[]{:S(2)}) copy-start(bf16[64,2048]{1,0:T(8,128)(2,1)} %refs_0_.1) | copy-start | bytes 786436
  2.2 4.8 %collective-permute-start.1 = (bf16[80,128]{1,0:T(8,128)(2,1)S(1)}, bf16[80,128]{1,0:T(8,128)(2,1)S(1)}, u32[]{:S(2)}, u32[]{:S(2)}) collective-permute-start(bf16[80,128]{1,0:T(8,128)(2,1)S(1)} %get-tuple-element.76.packed_ref.refs_0_), channel_id=1, source_target_pairs={{0,1},{1,0},{2,3},{3,2},{4,5},{5,4},{6,7},{7,6},{8,9},{9,8},{10,11... | collective-permute-start | bytes 61448 | tf_op jit(solution)/shard_map/ppermute | solution.py:526
  5.3 7.8 %collective-permute-start = (bf16[64,2048]{1,0:T(8,128)(2,1)S(1)}, bf16[64,2048]{1,0:T(8,128)(2,1)S(1)}, u32[]{:S(2)}, u32[]{:S(2)}) collective-permute-start(bf16[64,2048]{1,0:T(8,128)(2,1)S(1)} %copy-done), channel_id=1, source_target_pairs={{0,1},{1,0},{2,3},{3,2},{4,5},{5,4},{6,7},{7,6},{8,9},{9,8},{10,11... | collective-permute-start | bytes 786440 | tf_op jit(solution)/shard_map/ppermute | solution.py:526
  7.0 3.6 %copy-start.1 = (bf16[64,192]{1,0:T(8,128)(2,1)S(1)}, bf16[64,192]{1,0:T(8,128)(2,1)}, u32[]{:S(2)}) copy-start(bf16[64,192]{1,0:T(8,128)(2,1)} %first_ref.3) | copy-start | bytes 73732
  7.0 3.6 %copy-start.2 = (bf16[64,128]{1,0:T(8,128)(2,1)S(1)}, bf16[64,128]{1,0:T(8,128)(2,1)}, u32[]{:S(2)}) copy-start(bf16[64,128]{1,0:T(8,128)(2,1)} %node_first_ref.1) | copy-start | bytes 49156
  7.0 3.6 %copy-start.3 = (bf16[64,64]{1,0:T(8,128)(2,1)S(1)}, bf16[64,64]{1,0:T(8,128)(2,1)}, u32[]{:S(2)}) copy-start(bf16[64,64]{1,0:T(8,128)(2,1)} %second_ref.5) | copy-start | bytes 24580
  7.0 3.6 %copy-start.4 = (bf16[64,64]{1,0:T(8,128)(2,1)S(1)}, bf16[64,64]{1,0:T(8,128)(2,1)}, u32[]{:S(2)}) copy-start(bf16[64,64]{1,0:T(8,128)(2,1)} %node_second_ref.3) | copy-start | bytes 24580
  7.0 3.6 %copy-start.5 = (f32[4,64]{1,0:T(4,128)S(1)}, f32[4,64]{1,0:T(4,128)}, u32[]{:S(2)}) copy-start(f32[4,64]{1,0:T(4,128)} %refs_6_.1) | copy-start | bytes 3076
  7.2 7.1 %collective-permute-start.2 = (bf16[64,64]{1,0:T(8,128)(2,1)S(1)}, bf16[64,64]{1,0:T(8,128)(2,1)S(1)}, u32[]{:S(2)}, u32[]{:S(2)}) collective-permute-start(bf16[64,64]{1,0:T(8,128)(2,1)S(1)} %get-tuple-element.87), channel_id=1, source_target_pairs={{0,30},{2,4},{4,2},{6,8},{8,6},{10,12},{12,10},{14,16},{16,14},{18... | collective-permute-start | bytes 24584 | tf_op jit(solution)/shard_map/ppermute | solution.py:526
  10.6 3.8 %collective-permute-start.3 = (bf16[64,64]{1,0:T(8,128)(2,1)S(1)}, bf16[64,64]{1,0:T(8,128)(2,1)S(1)}, u32[]{:S(2)}, u32[]{:S(2)}) collective-permute-start(bf16[64,64]{1,0:T(8,128)(2,1)S(1)} %get-tuple-element.88), channel_id=1, source_target_pairs={{0,2},{2,0},{4,6},{6,4},{8,10},{10,8},{12,14},{14,12},{16,18},{18,... | collective-permute-start | bytes 24584 | tf_op jit(solution)/shard_map/ppermute | solution.py:526
  15.8 5.9 %collective-permute-start.4 = (bf16[64,128]{1,0:T(8,128)(2,1)S(1)}, bf16[64,128]{1,0:T(8,128)(2,1)S(1)}, u32[]{:S(2)}, u32[]{:S(2)}) collective-permute-start(bf16[64,128]{1,0:T(8,128)(2,1)S(1)} %get-tuple-element.103), channel_id=1, source_target_pairs={{0,30},{2,4},{4,2},{6,8},{8,6},{10,12},{12,10},{14,16},{16,14},{18... | collective-permute-start | bytes 49160 | tf_op jit(solution)/shard_map/ppermute | solution.py:526
  18.6 3.1 %collective-permute-start.5 = (bf16[64,128]{1,0:T(8,128)(2,1)S(1)}, bf16[64,128]{1,0:T(8,128)(2,1)S(1)}, u32[]{:S(2)}, u32[]{:S(2)}) collective-permute-start(bf16[64,128]{1,0:T(8,128)(2,1)S(1)} %get-tuple-element.104), channel_id=1, source_target_pairs={{0,2},{2,0},{4,6},{6,4},{8,10},{10,8},{12,14},{14,12},{16,18},{18,... | collective-permute-start | bytes 49160 | tf_op jit(solution)/shard_map/ppermute | solution.py:526
  24.4 5.9 %collective-permute-start.6 = (bf16[64,64]{1,0:T(8,128)(2,1)S(1)}, bf16[64,64]{1,0:T(8,128)(2,1)S(1)}, u32[]{:S(2)}, u32[]{:S(2)}) collective-permute-start(bf16[64,64]{1,0:T(8,128)(2,1)S(1)} %get-tuple-element.124), channel_id=1, source_target_pairs={{0,30},{2,4},{4,2},{6,8},{8,6},{10,12},{12,10},{14,16},{16,14},{18... | collective-permute-start | bytes 24584 | tf_op jit(solution)/shard_map/ppermute | solution.py:526
  27.3 3.1 %collective-permute-start.7 = (bf16[64,64]{1,0:T(8,128)(2,1)S(1)}, bf16[64,64]{1,0:T(8,128)(2,1)S(1)}, u32[]{:S(2)}, u32[]{:S(2)}) collective-permute-start(bf16[64,64]{1,0:T(8,128)(2,1)S(1)} %get-tuple-element.124), channel_id=1, source_target_pairs={{0,2},{2,0},{4,6},{6,4},{8,10},{10,8},{12,14},{14,12},{16,18},{18,... | collective-permute-start | bytes 24584 | tf_op jit(solution)/shard_map/ppermute | solution.py:526
  32.8 1.3 %collective-permute-start.8 = (bf16[64,512]{1,0:T(8,128)(2,1)S(1)}, bf16[64,512]{1,0:T(8,128)(2,1)S(1)}, u32[]{:S(2)}, u32[]{:S(2)}) collective-permute-start(bf16[64,512]{1,0:T(8,128)(2,1)S(1)} %get-tuple-element.134.mine_ref), channel_id=1, source_target_pairs={{0,2},{2,0},{4,6},{6,4},{8,10},{10,8},{12,14},{14,12},{16,18},{18,... | collective-permute-start | bytes 196616 | tf_op jit(solution)/shard_map/ppermute | solution.py:526
  34.2 4.3 %collective-permute-start.9 = (bf16[64,512]{1,0:T(8,128)(2,1)S(1)}, bf16[64,512]{1,0:T(8,128)(2,1)S(1)}, u32[]{:S(2)}, u32[]{:S(2)}) collective-permute-start(bf16[64,512]{1,0:T(8,128)(2,1)S(1)} %shard_map.199.mine_ref), channel_id=1, source_target_pairs={{0,4},{2,6},{4,0},{6,2},{8,12},{10,14},{12,8},{14,10},{16,20},{18,... | collective-permute-start | bytes 196616 | tf_op jit(solution)/shard_map/ppermute | solution.py:526
  38.6 4.3 %collective-permute-start.10 = (bf16[64,512]{1,0:T(8,128)(2,1)S(1)}, bf16[64,512]{1,0:T(8,128)(2,1)S(1)}, u32[]{:S(2)}, u32[]{:S(2)}) collective-permute-start(bf16[64,512]{1,0:T(8,128)(2,1)S(1)} %shard_map.200.mine_ref), channel_id=1, source_target_pairs={{0,8},{2,10},{4,12},{6,14},{8,0},{10,2},{12,4},{14,6},{16,24},{18,... | collective-permute-start | bytes 196616 | tf_op jit(solution)/shard_map/ppermute | solution.py:526
  43.0 5.3 %collective-permute-start.11 = (bf16[64,512]{1,0:T(8,128)(2,1)S(1)}, bf16[64,512]{1,0:T(8,128)(2,1)S(1)}, u32[]{:S(2)}, u32[]{:S(2)}) collective-permute-start(bf16[64,512]{1,0:T(8,128)(2,1)S(1)} %shard_map.201.mine_ref), channel_id=1, source_target_pairs={{0,16},{2,18},{4,20},{6,22},{8,24},{10,26},{12,28},{14,30},{16,0},... | collective-permute-start | bytes 196616 | tf_op jit(solution)/shard_map/ppermute | solution.py:526

commit v3 on v2

--- a/solution.py
+++ b/solution.py
@@ -10,7 +10,7 @@
 
 BF = jnp.bfloat16
 F32 = jnp.float32
-CHUNK = 512
+CHUNK = 256
 LANES = 128
 HBM = pltpu.HBM
 VM = pltpu.VMEM
@@ -199,8 +199,8 @@
 
 def onehot_kernel(groups, rows, rim, *refs):
     packs = [ref[: 3 * rows].astype(F32) for ref in refs[:groups]]
-    (first_ref, second_ref, node_first_ref, node_second_ref, bias_ref, alpha_pick, beta_pick,
-     onehot_ref, first_back, second_back, node_first_back, node_second_back, bias_out,
+    (slab_ref, first_ref, second_ref, node_first_ref, node_second_ref, bias_ref, alpha_pick, beta_pick,
+     onehot_ref, base_ref, count_ref, table_ref, first_back, second_back, node_first_back, node_second_back, bias_out,
      to_node, to_node_back, to_table, to_table_back, to_hidden, alpha_place, beta_place) = refs[groups:]
     latent = first_ref.shape[0]
     slab, room = alpha_pick.shape
@@ -217,11 +217,25 @@
             match = (source_rows == source[row : row + 1]) | ones_row
             onehot_ref[:wide, cols] = jnp.where(match, 1.0, 0.0).astype(BF)
             onehot_ref[wide:, cols] = jnp.where(target_rows == target[row : row + 1], 1.0, 0.0).astype(BF)
+    bias = bias_ref[...].T
+    bias_out[...] = bias
+    slab16 = slab_ref[...]
+    source = mm(first_ref[:, :latent], slab16)
+    target = mm(first_ref[:, latent : 2 * latent], slab16)
+    shift = wide_mm(first_ref[:, :latent], jnp.broadcast_to(bias[:, 3:4], (latent, LANES)))
+    table_ref[...] = source + shift[:, :1]
+    table = jnp.concatenate([*halves(source), *halves(target)], axis=1)
+    count = None
+    for cols in chunks_of(base_ref.shape[1]):
+        near = onehot_ref[:slab, cols]
+        hit = onehot_ref[wide:, cols]
+        base_ref[:, cols] = mm(table, jnp.concatenate([near, near, hit, hit], axis=0)) + bias[:, 0:1]
+        count = add_to(count, mm_nt(jnp.ones((16, CHUNK), BF), hit))
+    count_ref[...] = count[:8]
     first_back[...] = flip(first_ref[...])
     second_back[...] = flip(second_ref[...])
     node_first_back[...] = flip(node_first_ref[...])
     node_second_back[...] = flip(node_second_ref[...])
-    bias_out[...] = bias_ref[...].T
     forward = mm(node_first_ref[:, latent:], second_ref[...])
     to_node[...] = split(forward)
     to_node_back[...] = split(forward.T)
@@ -239,32 +253,24 @@
 
 def start_kernel(groups, *refs):
     parts = refs[:groups]
-    (onehot_ref, slab_ref, first_ref, node_first_ref, bias_ref,
-     edges_ref, base_ref, message_ref, count_ref, node_base_ref, table_ref) = refs[groups:]
+    (base_in, onehot_ref, slab_ref, count_ref, first_ref, node_first_ref, bias_ref,
+     edges_ref, base_ref, message_ref, node_base_ref) = refs[groups:]
     latent, slab = slab_ref.shape
     wide = onehot_ref.shape[0] - slab
     slots = parts[0].shape[1]
+    own = first_ref[:, 2 * latent :]
     message = None
-    count = None
     for rank in range(groups):
         for cols in chunks_of(slots):
             here = slice(rank * slots + cols.start, rank * slots + cols.stop)
             edges = pick([part[:, cols] for part in parts], rank)
             edges_ref[:, here] = edges
-            hit = onehot_ref[wide:, here]
-            message = add_to(message, mm_nt(edges, hit))
-            count = add_to(count, mm_nt(jnp.ones((16, CHUNK), BF), hit))
+            base_ref[:, here] = base_in[:, here] + mm(own, edges)
+            message = add_to(message, mm_nt(edges, onehot_ref[wide:, here]))
     bias = bias_ref[...]
-    count_ref[...] = count[:8]
-    message = message + bias[:, 1:2] * count[0:1]
+    message = message + bias[:, 1:2] * count_ref[0:1]
     message_ref[...] = message
-    slab16 = slab_ref[...]
-    source = mm(first_ref[:, :latent], slab16)
-    target = mm(first_ref[:, latent : 2 * latent], slab16)
-    slab_base(source, target, first_ref[:, 2 * latent :], bias, onehot_ref, edges_ref, base_ref)
-    node_base_ref[...] = node_base(slab16, message, node_first_ref, bias)
-    shift = wide_mm(first_ref[:, :latent], jnp.broadcast_to(bias[:, 3:4], (latent, LANES)))
-    table_ref[...] = source + shift[:, :1]
+    node_base_ref[...] = node_base(slab_ref[...], message, node_first_ref, bias)
 
 
 def forward_kernel(base_ref, onehot_ref, slab_ref, beta_in, alpha_in, node_base_ref, table_in,
@@ -324,9 +330,9 @@
         if low_ref is not None:
             low_ref[:, cols] = pre_low
         total = add_to(
-            total, mm_nt(jnp.concatenate([onehot_ref[:, cols], edges_ref[:, cols]], axis=0), pre_low)
+            total, mm_nt(pre_low, jnp.concatenate([onehot_ref[:, cols], edges_ref[:, cols]], axis=0))
         )
-    return total.T
+    return total
 
 
 def middle_kernel(base_ref, onehot_ref, edges_ref, beta_in, alpha_in, node_base_ref, cot_ref,
@@ -581,18 +587,19 @@
     )
     beta = by_beta(beta)
     alpha = by_alpha(alpha)
-    (onehot, first_back, second_back, node_first_back, node_second_back, bias,
+    (onehot, base, count, table, first_back, second_back, node_first_back, node_second_back, bias,
      to_node, to_node_back, to_table, to_table_back, to_hidden, alpha_place, beta_place) = call(
         functools.partial(onehot_kernel, groups, rows, rim),
-        [((wide + slab, total_slots), BF), (edge_first.shape[::-1], BF), (edge_second.shape[::-1], BF),
+        [((wide + slab, total_slots), BF), per_slot(F32), ((8, slab), F32), per_hit(F32),
+         (edge_first.shape[::-1], BF), (edge_second.shape[::-1], BF),
          (node_first.shape[::-1], BF), (node_second.shape[::-1], BF), (biases.shape[::-1], F32)]
         + [((hidden, 3 * hidden), BF)] * 5 + [((2 * slab, 2 * room), BF)] * 2,
-        *packs, edge_first, edge_second, node_first, node_second, biases, alpha_pick, beta_pick, cost=2.0,
-    )
-    edges_zero, base, message, count, node_base_zero, table = call(
+        *packs, slab_zero, edge_first, edge_second, node_first, node_second, biases, alpha_pick, beta_pick, cost=2.0,
+    )
+    edges_zero, base, message, node_base_zero = call(
         functools.partial(start_kernel, groups),
-        [per_slot(BF), per_slot(F32), per_hit(F32), ((8, slab), F32), per_hit(F32), per_hit(F32)],
-        *parts, onehot, slab_zero, edge_first, node_first, bias, cost=1.0,
+        [per_slot(BF), per_slot(F32), per_hit(F32), per_hit(F32)],
+        *parts, base, onehot, slab_zero, count, edge_first, node_first, bias, cost=1.0,
     )
     (hidden_zero, slope, rims_zero, sums_zero, node_pre_zero, node_hidden_zero, slab_one, table,
      alpha, beta) = call(

time: 49.4 us -> 48.7 us (0.986)
  Pallas kernels: 14.5 us -> 13.5 us
    pallas_call x15, Pallas kernels: 14.5 us -> 13.5 us  [call(): pl.pallas_call(kernel, out_shape=[jax.ShapeDtypeStruct(shape, kind) for s...]
  transfers between devices with their start and end apart: 12 -> 12, of which waited for: 8 -> 8; matrix products, arithmetic and copies ran while one was open for 0% -> 0% of each run, Pallas kernels for 12% -> 10%
where the time goes in v3:
time: 48.7 us; the launch traced here: 48.5 us
  waiting for transfers between devices  20.8 us (43%)
  Pallas kernels  13.5 us (28%)
  starting transfers between devices  12.7 us (26%)
  between operations  1.43 us (3%)
    ppermute x12, waiting for transfers between devices, swap(): lax.ppermute(value, axis, [(source, pairing(source) % count) for source i...  20.8 us
    pallas_call x15, Pallas kernels, call(): pl.pallas_call(kernel, out_shape=[jax.ShapeDtypeStruct(shape, kind) for s...  13.5 us
    ppermute x12, starting transfers between devices, swap(): lax.ppermute(value, axis, [(source, pairing(source) % count) for source i...  12.7 us
  transfers between devices with their start and end apart: 12, of which 8 were waited for; matrix products, arithmetic and copies ran while one was open for 0% of the time, Pallas kernels for 10%

profile of v3, /device:TPU:0, one launch (start us, length us, event | category | flops | bytes accessed | tf_op | source)
XLA Modules:
  0.0 48.5 jit_solution(17026044537000966598)
XLA Ops:
  1.3 0.0 copy-start
  1.3 0.9 %shard_map.188 = (bf16[80,128]{1,0:T(8,128)(2,1)S(1)}, s32[1,24]{1,0:T(1,128)S(1)}, s32[1,24]{1,0:T(1,128)S(1)}) custom-call(s32[1,1]{1,0:T(1,128)S(6)} %copy.21.count_ref, s32[16,128]{1,0:T(8,128)} %bitcast.7, s32[16,128]{1,0:T(8,128)} %bitcast.8, bf16[32,64]{1,0:T(8,128)(2,1)} %bitcast.9, f32[32,64]{1,0:T(8,128)} %bitcast.6, s32[1,24]{1,0:T(1,128)} %upper_hbm.1, ...), custom_call_target="tpu_custom_call" | custom-call | flops 1000000000 | bytes 3600000 | tf_op jit(solution)/shard_map/pallas_call | solution.py:517
  2.2 3.0 %collective-permute-start.1 = (bf16[80,128]{1,0:T(8,128)(2,1)S(1)}, bf16[80,128]{1,0:T(8,128)(2,1)S(1)}, u32[]{:S(2)}, u32[]{:S(2)}) collective-permute-start(bf16[80,128]{1,0:T(8,128)(2,1)S(1)} %get-tuple-element.77.packed_ref.refs_0_), channel_id=1, source_target_pairs={{0,1},{1,0},{2,3},{3,2},{4,5},{5,4},{6,7},{7,6},{8,9},{9,8},{10,11... | collective-permute-start | bytes 61448 | tf_op jit(solution)/shard_map/ppermute | solution.py:532
  5.2 0.1 shard_map.189
  5.3 0.0 copy-done
  5.3 0.1 collective-permute-start
  5.4 1.6 %collective-permute-done.1.refs_1_ = bf16[80,128]{1,0:T(8,128)(2,1)S(1)} collective-permute-done((bf16[80,128]{1,0:T(8,128)(2,1)S(1)}, bf16[80,128]{1,0:T(8,128)(2,1)S(1)}, u32[]{:S(2)}, u32[]{:S(2)}) %collective-permute-start.1) | collective-permute-done | bytes 20512 | tf_op jit(solution)/shard_map/ppermute | solution.py:532
  7.0 0.0 copy-start.1
  7.0 0.0 copy-start.2
  7.0 0.0 copy-start.5
  7.0 0.2 shard_map.190
  7.2 3.4 %collective-permute-start.2 = (bf16[64,64]{1,0:T(8,128)(2,1)S(1)}, bf16[64,64]{1,0:T(8,128)(2,1)S(1)}, u32[]{:S(2)}, u32[]{:S(2)}) collective-permute-start(bf16[64,64]{1,0:T(8,128)(2,1)S(1)} %get-tuple-element.90), channel_id=1, source_target_pairs={{0,30},{2,4},{4,2},{6,8},{8,6},{10,12},{12,10},{14,16},{16,14},{18... | collective-permute-start | bytes 24584 | tf_op jit(solution)/shard_map/ppermute | solution.py:532
  10.6 0.0 collective-permute-start.3
  10.6 0.0 copy-done.1
  10.6 0.0 copy-done.2
  10.6 0.0 copy-done.3
  10.6 0.0 copy-done.4
  10.7 0.0 copy-done.5
  10.7 1.1 %shard_map.191 = (bf16[192,4096]{1,0:T(8,128)(2,1)S(1)}, f32[64,4096]{1,0:T(8,128)S(1)}, f32[8,64]{1,0:T(8,128)S(1)}, f32[64,64]{1,0:T(8,128)S(1)}, bf16[192,64]...) custom-call(bf16[80,128]{1,0:T(8,128)(2,1)S(1)} %get-tuple-element.7, ...), custom_call_target="tpu_custom_call" | custom-call | flops 2000000000 | bytes 7200000 | tf_op jit(solution)/shard_map/pallas_call | solution.py:517
  11.8 1.4 %collective-permute-done.refs_1_ = bf16[64,2048]{1,0:T(8,128)(2,1)S(1)} collective-permute-done((bf16[64,2048]{1,0:T(8,128)(2,1)S(1)}, bf16[64,2048]{1,0:T(8,128)(2,1)S(1)}, u32[]{:S(2)}, u32[]{:S(2)}) %collective-permute-start) | collective-permute-done | bytes 262176 | tf_op jit(solution)/shard_map/ppermute | solution.py:532
  13.2 0.5 %shard_map.192 = (bf16[64,4096]{1,0:T(8,128)(2,1)S(1)}, f32[64,4096]{1,0:T(8,128)S(1)}, f32[64,64]{1,0:T(8,128)S(1)}, f32[64,64]{1,0:T(8,128)S(1)}) custom-call(bf16[64,2048]{1,0:T(8,128)(2,1)S(1)} %copy-done, bf16[64,2048]{1,0:T(8,128)(2,1)S(1)} %collective-permute-done.refs_1_, f32[64,4096]{1,0:T(8,128)S(1)} %get-tuple-element.84.refs_2_, ...), custom_call_target="tpu_custom_call" | custom-call | flops 1000000000 | bytes 3600000 | tf_op jit(solution)/shard_map/pallas_call | solution.py:517
  13.7 0.0 collective-permute-done.2.beta_in
  13.7 0.0 collective-permute-done.3.alpha_in
  13.8 1.4 %shard_map.193 = (bf16[64,4096]{1,0:T(8,128)(2,1)S(1)}, f32[64,4096]{1,0:T(8,128)S(1)}, bf16[64,64]{1,0:T(8,128)(2,1)S(1)}, f32[64,64]{1,0:T(8,128)S(1)}, f32[64...) custom-call(f32[64,4096]{1,0:T(8,128)S(1)} %get-tuple-element.89.bas, ...), custom_call_target="tpu_custom_call" | custom-call | flops 2000000000 | bytes 7200000 | tf_op jit(solution)/shard_map/pallas_call | solution.py:517
  15.1 2.9 %collective-permute-start.4 = (bf16[64,128]{1,0:T(8,128)(2,1)S(1)}, bf16[64,128]{1,0:T(8,128)(2,1)S(1)}, u32[]{:S(2)}, u32[]{:S(2)}) collective-permute-start(bf16[64,128]{1,0:T(8,128)(2,1)S(1)} %get-tuple-element.105), channel_id=1, source_target_pairs={{0,30},{2,4},{4,2},{6,8},{8,6},{10,12},{12,10},{14,16},{16,14},{18... | collective-permute-start | bytes 49160 | tf_op jit(solution)/shard_map/ppermute | solution.py:532
  18.0 0.0 collective-permute-start.5
  18.0 1.1 %shard_map.194 = (bf16[64,4096]{1,0:T(8,128)(2,1)S(1)}, f32[64,4096]{1,0:T(8,128)S(1)}, f32[64,64]{1,0:T(8,128)S(1)}, bf16[128,64]{1,0:T(8,128)(2,1)S(1)}, f32[64,64]{1,0:T(8,128)S(1)}) custom-call(bf16[64,4096]{1,0:T(8,128)(2,1)S(1)} %get-tuple-element.88.edges_ref, bf16[64,4096]{1,0:T(8,128)(2,1)S(1)} %get-tuple-element.98.hidden_ref.hidden_zero_ref, ...), custom_call_target="tpu_custom_call" | custom-call | flops 2000000000 | bytes 7200000 | tf_op jit(solution)/shard_map/pallas_call | solution.py:517
  19.1 1.9 %collective-permute-done.4.beta_in = bf16[64,128]{1,0:T(8,128)(2,1)S(1)} collective-permute-done((bf16[64,128]{1,0:T(8,128)(2,1)S(1)}, bf16[64,128]{1,0:T(8,128)(2,1)S(1)}, u32[]{:S(2)}, u32[]{:S(2)}) %collective-permute-start.4) | collective-permute-done | bytes 16416 | tf_op jit(solution)/shard_map/ppermute | solution.py:532
  21.0 0.0 collective-permute-done.5.alpha_in
  21.0 2.6 %shard_map.195 = (bf16[64,4096]{1,0:T(8,128)(2,1)S(1)}, bf16[64,4096]{1,0:T(8,128)(2,1)S(1)}, f32[64,64]{1,0:T(8,128)S(1)}, f32[64,64]{1,0:T(8,128)S(1)}, f32[64...) custom-call(f32[64,4096]{1,0:T(8,128)S(1)} %get-tuple-element.104.base_ref, ...), custom_call_target="tpu_custom_call" | custom-call | flops 3000000000 | bytes 10800000 | tf_op jit(solution)/shard_map/pallas_call | solution.py:517
  23.7 2.8 %collective-permute-start.6 = (bf16[64,64]{1,0:T(8,128)(2,1)S(1)}, bf16[64,64]{1,0:T(8,128)(2,1)S(1)}, u32[]{:S(2)}, u32[]{:S(2)}) collective-permute-start(bf16[64,64]{1,0:T(8,128)(2,1)S(1)} %get-tuple-element.126), channel_id=1, source_target_pairs={{0,30},{2,4},{4,2},{6,8},{8,6},{10,12},{12,10},{14,16},{16,14},{18... | collective-permute-start | bytes 24584 | tf_op jit(solution)/shard_map/ppermute | solution.py:532
  26.5 0.0 collective-permute-start.7
  26.5 0.8 %shard_map.196 = (f32[64,4096]{1,0:T(8,128)S(1)}, f32[64,512]{1,0:T(8,128)S(1)}, bf16[128,64]{1,0:T(8,128)(2,1)S(1)}, f32[64,64]{1,0:T(8,128)S(1)}, f32[64,64]{1,0:T(8,128)S(1)}) custom-call(bf16[64,4096]{1,0:T(8,128)(2,1)S(1)} %get-tuple-element.112.low_ref, bf16[64,4096]{1,0:T(8,128)(2,1)S(1)} %get-tuple-element.98.hidden_ref.hidden_zero_ref, ...), custom_call_target="tpu_custom_call" | custom-call | flops 2000000000 | bytes 7200000 | tf_op jit(solution)/shard_map/pallas_call | solution.py:517
  27.4 2.2 %collective-permute-done.6.beta_in = bf16[64,64]{1,0:T(8,128)(2,1)S(1)} collective-permute-done((bf16[64,64]{1,0:T(8,128)(2,1)S(1)}, bf16[64,64]{1,0:T(8,128)(2,1)S(1)}, u32[]{:S(2)}, u32[]{:S(2)}) %collective-permute-start.6) | collective-permute-done | bytes 8224 | tf_op jit(solution)/shard_map/ppermute | solution.py:532
  29.6 0.0 collective-permute-done.7.alpha_in
  29.6 2.5 %shard_map.198 = (bf16[64,512]{1,0:T(8,128)(2,1)S(1)}, f32[64,64]{1,0:T(8,128)S(1)}) custom-call(f32[64,64]{1,0:T(8,128)S(1)} %get-tuple-element.124.back_in, f32[64,64]{1,0:T(8,128)S(1)} %get-tuple-element.125.back_node, bf16[64,64]{1,0:T(8,128)(2,1)S(1)} %collective-permute-done.6.beta_in, bf16[64,64]{1,0:T(8,128)(2,1)S(1)} %collective-permute-done.7.alpha_in, ...), custom_call_target="tpu_custom_call" | custom-call | flops 2000000000 | bytes 7200000 | tf_op jit(solution)/shard_map/pallas_call | solution.py:517
  32.1 0.1 collective-permute-start.8
  32.2 1.2 %collective-permute-done.8.other_ref.alpha_in = bf16[64,512]{1,0:T(8,128)(2,1)S(1)} collective-permute-done((bf16[64,512]{1,0:T(8,128)(2,1)S(1)}, bf16[64,512]{1,0:T(8,128)(2,1)S(1)}, u32[]{:S(2)}, u32[]{:S(2)}) %collective-permute-start.8) | collective-permute-done | bytes 65568 | tf_op jit(solution)/shard_map/ppermute | solution.py:532
  33.4 0.1 collective-permute-start.9
  33.5 4.3 %collective-permute-done.9.other_ref = bf16[64,512]{1,0:T(8,128)(2,1)S(1)} collective-permute-done((bf16[64,512]{1,0:T(8,128)(2,1)S(1)}, bf16[64,512]{1,0:T(8,128)(2,1)S(1)}, u32[]{:S(2)}, u32[]{:S(2)}) %collective-permute-start.9) | collective-permute-done | bytes 65568 | tf_op jit(solution)/shard_map/ppermute | solution.py:532
  37.8 0.1 shard_map.200.mine_ref
  37.8 0.0 collective-permute-start.10
  37.9 4.3 %collective-permute-done.10.other_ref = bf16[64,512]{1,0:T(8,128)(2,1)S(1)} collective-permute-done((bf16[64,512]{1,0:T(8,128)(2,1)S(1)}, bf16[64,512]{1,0:T(8,128)(2,1)S(1)}, u32[]{:S(2)}, u32[]{:S(2)}) %collective-permute-start.10) | collective-permute-done | bytes 65568 | tf_op jit(solution)/shard_map/ppermute | solution.py:532
  42.1 0.1 shard_map.201.mine_ref
  42.2 0.3 collective-permute-start.11
  42.6 1.1 %shard_map.197 = (bf16[64,2048]{1,0:T(8,128)(2,1)}, bf16[32,64]{1,0:T(8,128)(2,1)}) custom-call(s32[1,1]{1,0:T(1,128)S(6)} %copy.21.count_ref, bf16[64,4096]{1,0:T(8,128)(2,1)S(1)} %get-tuple-element.103.edges_ref, bf16[64,4096]{1,0:T(8,128)(2,1)S(1)} %get-tuple-element.111.hidden_ref, bf16[128,64]{1,0:T(8,128)(2,1)S(1)} %get-tuple-element.121.joined_ref, ...), custom_call_target="tpu_custom_call" | custom-call | flops 2000000000 | bytes 7200000 | tf_op jit(solution)/shard_map/pallas_call | solution.py:517
  43.7 3.9 %collective-permute-done.11.other_ref = bf16[64,512]{1,0:T(8,128)(2,1)S(1)} collective-permute-done((bf16[64,512]{1,0:T(8,128)(2,1)S(1)}, bf16[64,512]{1,0:T(8,128)(2,1)S(1)}, u32[]{:S(2)}, u32[]{:S(2)}) %collective-permute-start.11) | collective-permute-done | bytes 65568 | tf_op jit(solution)/shard_map/ppermute | solution.py:532
  47.6 1.0 %shard_map.202 = (f32[32,64]{1,0:T(8,128)}, f32[64,192]{1,0:T(8,128)}, f32[64,64]{1,0:T(8,128)}, f32[64,128]{1,0:T(8,128)}, f32[64,64]{1,0:T(8,128)}, /*index=5*/f32[4,64]{1,0:T(4,128)}) custom-call(bf16[64,512]{1,0:T(8,128)(2,1)S(1)} %shard_map.201.mine_ref, bf16[64,512]{1,0:T(8,128)(2,1)S(1)} %collective-permute-done.11.other_ref, ...), custom_call_target="tpu_custom_call" | custom-call | flops 1000000000 | bytes 3600000 | tf_op jit(solution)/shard_map/pallas_call | solution.py:517
  (3 shorter events, 0.0 us)
Async XLA Ops:
  1.3 4.0 %copy-start = (bf16[64,2048]{1,0:T(8,128)(2,1)S(1)}, bf16[64,2048]{1,0:T(8,128)(2,1)}, u32[]{:S(2)}) copy-start(bf16[64,2048]{1,0:T(8,128)(2,1)} %refs_0_.1) | copy-start | bytes 786436
  2.2 4.8 %collective-permute-start.1 = (bf16[80,128]{1,0:T(8,128)(2,1)S(1)}, bf16[80,128]{1,0:T(8,128)(2,1)S(1)}, u32[]{:S(2)}, u32[]{:S(2)}) collective-permute-start(bf16[80,128]{1,0:T(8,128)(2,1)S(1)} %get-tuple-element.77.packed_ref.refs_0_), channel_id=1, source_target_pairs={{0,1},{1,0},{2,3},{3,2},{4,5},{5,4},{6,7},{7,6},{8,9},{9,8},{10,11... | collective-permute-start | bytes 61448 | tf_op jit(solution)/shard_map/ppermute | solution.py:532
  5.3 7.8 %collective-permute-start = (bf16[64,2048]{1,0:T(8,128)(2,1)S(1)}, bf16[64,2048]{1,0:T(8,128)(2,1)S(1)}, u32[]{:S(2)}, u32[]{:S(2)}) collective-permute-start(bf16[64,2048]{1,0:T(8,128)(2,1)S(1)} %copy-done), channel_id=1, source_target_pairs={{0,1},{1,0},{2,3},{3,2},{4,5},{5,4},{6,7},{7,6},{8,9},{9,8},{10,11... | collective-permute-start | bytes 786440 | tf_op jit(solution)/shard_map/ppermute | solution.py:532
  7.0 3.6 %copy-start.1 = (bf16[64,192]{1,0:T(8,128)(2,1)S(1)}, bf16[64,192]{1,0:T(8,128)(2,1)}, u32[]{:S(2)}) copy-start(bf16[64,192]{1,0:T(8,128)(2,1)} %first_ref.3) | copy-start | bytes 73732
  7.0 3.6 %copy-start.2 = (bf16[64,128]{1,0:T(8,128)(2,1)S(1)}, bf16[64,128]{1,0:T(8,128)(2,1)}, u32[]{:S(2)}) copy-start(bf16[64,128]{1,0:T(8,128)(2,1)} %node_first_ref.1) | copy-start | bytes 49156
  7.0 3.6 %copy-start.3 = (bf16[64,64]{1,0:T(8,128)(2,1)S(1)}, bf16[64,64]{1,0:T(8,128)(2,1)}, u32[]{:S(2)}) copy-start(bf16[64,64]{1,0:T(8,128)(2,1)} %second_ref.5) | copy-start | bytes 24580
  7.0 3.6 %copy-start.4 = (bf16[64,64]{1,0:T(8,128)(2,1)S(1)}, bf16[64,64]{1,0:T(8,128)(2,1)}, u32[]{:S(2)}) copy-start(bf16[64,64]{1,0:T(8,128)(2,1)} %node_second_ref.3) | copy-start | bytes 24580
  7.0 3.6 %copy-start.5 = (f32[4,64]{1,0:T(4,128)S(1)}, f32[4,64]{1,0:T(4,128)}, u32[]{:S(2)}) copy-start(f32[4,64]{1,0:T(4,128)} %refs_7_.2) | copy-start | bytes 3076
  7.2 6.5 %collective-permute-start.2 = (bf16[64,64]{1,0:T(8,128)(2,1)S(1)}, bf16[64,64]{1,0:T(8,128)(2,1)S(1)}, u32[]{:S(2)}, u32[]{:S(2)}) collective-permute-start(bf16[64,64]{1,0:T(8,128)(2,1)S(1)} %get-tuple-element.90), channel_id=1, source_target_pairs={{0,30},{2,4},{4,2},{6,8},{8,6},{10,12},{12,10},{14,16},{16,14},{18... | collective-permute-start | bytes 24584 | tf_op jit(solution)/shard_map/ppermute | solution.py:532
  10.6 3.1 %collective-permute-start.3 = (bf16[64,64]{1,0:T(8,128)(2,1)S(1)}, bf16[64,64]{1,0:T(8,128)(2,1)S(1)}, u32[]{:S(2)}, u32[]{:S(2)}) collective-permute-start(bf16[64,64]{1,0:T(8,128)(2,1)S(1)} %get-tuple-element.91), channel_id=1, source_target_pairs={{0,2},{2,0},{4,6},{6,4},{8,10},{10,8},{12,14},{14,12},{16,18},{18,... | collective-permute-start | bytes 24584 | tf_op jit(solution)/shard_map/ppermute | solution.py:532
  15.1 5.9 %collective-permute-start.4 = (bf16[64,128]{1,0:T(8,128)(2,1)S(1)}, bf16[64,128]{1,0:T(8,128)(2,1)S(1)}, u32[]{:S(2)}, u32[]{:S(2)}) collective-permute-start(bf16[64,128]{1,0:T(8,128)(2,1)S(1)} %get-tuple-element.105), channel_id=1, source_target_pairs={{0,30},{2,4},{4,2},{6,8},{8,6},{10,12},{12,10},{14,16},{16,14},{18... | collective-permute-start | bytes 49160 | tf_op jit(solution)/shard_map/ppermute | solution.py:532
  18.0 3.1 %collective-permute-start.5 = (bf16[64,128]{1,0:T(8,128)(2,1)S(1)}, bf16[64,128]{1,0:T(8,128)(2,1)S(1)}, u32[]{:S(2)}, u32[]{:S(2)}) collective-permute-start(bf16[64,128]{1,0:T(8,128)(2,1)S(1)} %get-tuple-element.106), channel_id=1, source_target_pairs={{0,2},{2,0},{4,6},{6,4},{8,10},{10,8},{12,14},{14,12},{16,18},{18,... | collective-permute-start | bytes 49160 | tf_op jit(solution)/shard_map/ppermute | solution.py:532
  23.7 5.9 %collective-permute-start.6 = (bf16[64,64]{1,0:T(8,128)(2,1)S(1)}, bf16[64,64]{1,0:T(8,128)(2,1)S(1)}, u32[]{:S(2)}, u32[]{:S(2)}) collective-permute-start(bf16[64,64]{1,0:T(8,128)(2,1)S(1)} %get-tuple-element.126), channel_id=1, source_target_pairs={{0,30},{2,4},{4,2},{6,8},{8,6},{10,12},{12,10},{14,16},{16,14},{18... | collective-permute-start | bytes 24584 | tf_op jit(solution)/shard_map/ppermute | solution.py:532
  26.5 3.1 %collective-permute-start.7 = (bf16[64,64]{1,0:T(8,128)(2,1)S(1)}, bf16[64,64]{1,0:T(8,128)(2,1)S(1)}, u32[]{:S(2)}, u32[]{:S(2)}) collective-permute-start(bf16[64,64]{1,0:T(8,128)(2,1)S(1)} %get-tuple-element.126), channel_id=1, source_target_pairs={{0,2},{2,0},{4,6},{6,4},{8,10},{10,8},{12,14},{14,12},{16,18},{18,... | collective-permute-start | bytes 24584 | tf_op jit(solution)/shard_map/ppermute | solution.py:532
  32.1 1.3 %collective-permute-start.8 = (bf16[64,512]{1,0:T(8,128)(2,1)S(1)}, bf16[64,512]{1,0:T(8,128)(2,1)S(1)}, u32[]{:S(2)}, u32[]{:S(2)}) collective-permute-start(bf16[64,512]{1,0:T(8,128)(2,1)S(1)} %get-tuple-element.136.mine_ref), channel_id=1, source_target_pairs={{0,2},{2,0},{4,6},{6,4},{8,10},{10,8},{12,14},{14,12},{16,18},{18,... | collective-permute-start | bytes 196616 | tf_op jit(solution)/shard_map/ppermute | solution.py:532
  33.4 4.3 %collective-permute-start.9 = (bf16[64,512]{1,0:T(8,128)(2,1)S(1)}, bf16[64,512]{1,0:T(8,128)(2,1)S(1)}, u32[]{:S(2)}, u32[]{:S(2)}) collective-permute-start(bf16[64,512]{1,0:T(8,128)(2,1)S(1)} %shard_map.199.mine_ref), channel_id=1, source_target_pairs={{0,4},{2,6},{4,0},{6,2},{8,12},{10,14},{12,8},{14,10},{16,20},{18,... | collective-permute-start | bytes 196616 | tf_op jit(solution)/shard_map/ppermute | solution.py:532
  37.8 4.3 %collective-permute-start.10 = (bf16[64,512]{1,0:T(8,128)(2,1)S(1)}, bf16[64,512]{1,0:T(8,128)(2,1)S(1)}, u32[]{:S(2)}, u32[]{:S(2)}) collective-permute-start(bf16[64,512]{1,0:T(8,128)(2,1)S(1)} %shard_map.200.mine_ref), channel_id=1, source_target_pairs={{0,8},{2,10},{4,12},{6,14},{8,0},{10,2},{12,4},{14,6},{16,24},{18,... | collective-permute-start | bytes 196616 | tf_op jit(solution)/shard_map/ppermute | solution.py:532
  42.2 5.3 %collective-permute-start.11 = (bf16[64,512]{1,0:T(8,128)(2,1)S(1)}, bf16[64,512]{1,0:T(8,128)(2,1)S(1)}, u32[]{:S(2)}, u32[]{:S(2)}) collective-permute-start(bf16[64,512]{1,0:T(8,128)(2,1)S(1)} %shard_map.201.mine_ref), channel_id=1, source_target_pairs={{0,16},{2,18},{4,20},{6,22},{8,24},{10,26},{12,28},{14,30},{16,0},... | collective-permute-start | bytes 196616 | tf_op jit(solution)/shard_map/ppermute | solution.py:532

commit v4 on v3

--- a/solution.py
+++ b/solution.py
@@ -10,7 +10,7 @@
 
 BF = jnp.bfloat16
 F32 = jnp.float32
-CHUNK = 256
+CHUNK = 512
 LANES = 128
 HBM = pltpu.HBM
 VM = pltpu.VMEM
@@ -107,7 +107,6 @@
 
 def activate(base_ref, table, onehot_ref, slab, hidden_ref, slope_ref):
     wide = onehot_ref.shape[0] - slab
-    total = None
     for cols in chunks_of(base_ref.shape[1]):
         rims = onehot_ref[slab:wide, cols]
         pre = base_ref[:, cols] + mm(table, jnp.concatenate([rims, rims], axis=0))
@@ -115,8 +114,7 @@
         hidden = value.astype(BF)
         hidden_ref[:, cols] = hidden
         slope_ref[:, cols] = slope
-        total = add_to(total, mm_nt(hidden, onehot_ref[wide:, cols]))
-    return total
+    return mm_nt(hidden_ref[...], onehot_ref[wide:])
 
 
 def slab_base(source, target, own, bias, onehot_ref, edges_ref, base_ref):
@@ -320,19 +318,13 @@
     slab = wanted.shape[1]
     wide = onehot_ref.shape[0] - slab
     table = jnp.concatenate(halves(wanted), axis=1)
-    total = None
     for cols in chunks_of(edges_ref.shape[1]):
         hit = onehot_ref[wide:, cols]
         grad = mm(table, jnp.concatenate([hit, hit], axis=0))
         if extra_ref is not None:
             grad = grad + extra_ref[:, cols]
-        pre_low = (grad * slope_ref[:, cols]).astype(BF)
-        if low_ref is not None:
-            low_ref[:, cols] = pre_low
-        total = add_to(
-            total, mm_nt(pre_low, jnp.concatenate([onehot_ref[:, cols], edges_ref[:, cols]], axis=0))
-        )
-    return total
+        low_ref[:, cols] = (grad * slope_ref[:, cols]).astype(BF)
+    return mm_nt(low_ref[...], jnp.concatenate([onehot_ref[...], edges_ref[...]], axis=0))
 
 
 def middle_kernel(base_ref, onehot_ref, edges_ref, beta_in, alpha_in, node_base_ref, cot_ref,
@@ -396,15 +388,13 @@
     edge_one = jnp.concatenate(
         [mm_nt(source, slab16), mm_nt(target, slab16), sums[:, wide + slab :]], axis=1
     )
-    used = edge_one.shape[1] + edge_two.shape[1] + node_one.shape[1] + node_two.shape[1]
-    pad = jnp.zeros((latent, total_ref.shape[1] - used - 4), F32)
     total_ref[...] = jnp.concatenate(
-        [edge_one, edge_two, node_one, node_two, pre_sum, gm_sum, node_pre_sum, cot_sum, pad], axis=1
+        [edge_one, edge_two, node_one, node_two, pre_sum, gm_sum, node_pre_sum, cot_sum], axis=1
     )
 
 
 def output_kernel(count_ref, edges_ref, hidden_ref, joined_ref, node_pre_ref, second_ref, node_second_ref, bias_ref,
-                  edge_out, node_out, new_ref):
+                  edge_out, node_out, done_ref, new_ref):
     bias = bias_ref[...]
     latent = edges_ref.shape[0]
     second = second_ref[...]
@@ -421,18 +411,19 @@
     node_hidden = slope_parts(node_pre_ref[...])[0].astype(BF)
     state = joined_ref[:latent].astype(F32) + mm(node_second_ref[...], node_hidden) + bias[:, 3:4]
     node_out[...] = own_rows(state.T, node_out.shape[0]).astype(BF)
+    done_ref[...] = jnp.zeros_like(done_ref)
 
 
 def last_kernel(rim, back_in, back_node, beta_in, alpha_in, alpha_pick, beta_pick, joined_ref, node_pre_ref,
                 node_hidden_ref, wanted_in, sums_ref, count_ref, extra_ref, slope_ref, onehot_ref, edges_ref,
                 slab_ref, rims_ref, slab_one_ref, total_in, first_back, node_first_back, to_node_back, to_table_back,
-                total_ref, back_ref):
+                total_ref, back_ref, low_ref):
     latent, slab = slab_ref.shape
     wide = onehot_ref.shape[0] - slab
     placed = mm_nt(alpha_in[...], alpha_pick[...]) + mm_nt(beta_in[...], beta_pick[...])
     pre_grad = (back_node[...] + split_mm(to_table_back[...], placed)) * slope_parts(node_pre_ref[...])[1]
     wanted = wanted_in[...] + split_mm(to_node_back[...], pre_grad)
-    sums = edge_gradient(wanted, extra_ref, slope_ref, onehot_ref, edges_ref, None)
+    sums = edge_gradient(wanted, extra_ref, slope_ref, onehot_ref, edges_ref, low_ref)
     source = sums[:, :wide].astype(BF)
     target = sums[:, wide : wide + slab].astype(BF)
     ext_grad = mm(first_back[:latent], source)
@@ -457,41 +448,70 @@
     edge_two = mm_nt(gm, sums_ref[...].astype(BF))
     pre_sum = sums[:, slab + 2 * rim : slab + 2 * rim + 1]
     gm_sum = jnp.sum(gm.astype(F32) * count_ref[0:1], axis=1, keepdims=True)
-    used = edge_one.shape[1] + edge_two.shape[1] + node_one.shape[1] + node_two.shape[1]
-    pad = jnp.zeros((latent, total_ref.shape[1] - used - 4 - 2 * rim), F32)
-    total_ref[...] = (
-        total_in[...]
-        + jnp.concatenate(
-            [edge_one, edge_two, node_one, node_two, pre_sum, gm_sum, node_pre_sum, grad_sum, alpha, beta, pad],
-            axis=1,
-        )
-    ).astype(BF)
-
-
-def add_kernel(used, rim, bit, mine_ref, other_ref, out_ref):
+    total = total_in[...] + jnp.concatenate(
+        [edge_one, edge_two, node_one, node_two, pre_sum, gm_sum, node_pre_sum, grad_sum], axis=1
+    )
+    total_ref[...] = padded([total, alpha, beta], total_ref.shape[1]).astype(BF)
+
+
+def padded(pieces, width):
+    spare = width - sum(piece.shape[1] for piece in pieces)
+    if spare:
+        pieces = pieces + [jnp.zeros((pieces[0].shape[0], spare), F32)]
+    return jnp.concatenate(pieces, axis=1)
+
+
+def even_chip():
+    return lax.rem(lax.axis_index("phi") // 2, 2) == 0
+
+
+def open_kernel(used, rim, mine_ref, other_ref, out_ref):
     mine = mine_ref[...].astype(F32)
     other = other_ref[...].astype(F32)
-    lane = lax.broadcasted_iota(jnp.int32, mine.shape, 1)
-    held = other[:, used + rim : used + 2 * rim]
-    if bit == 1:
-        arrived = jnp.zeros_like(held)
-        passing = held
-    else:
-        place = lax.axis_index("phi")
-        home = (lax.rem(place // bit, 2) == 1) == (lax.rem(place, 2) == 0)
-        arrived = mine[:, used : used + rim] + jnp.where(home, held, 0.0)
-        passing = jnp.where(home, 0.0, held)
-    pad = jnp.zeros((mine.shape[0], mine.shape[1] - used - 2 * rim), F32)
-    out_ref[...] = jnp.concatenate(
-        [(mine + other)[:, :used], arrived, passing, pad], axis=1
-    ).astype(BF)
-
-
-def finish_kernel(used, rim, mine_ref, other_ref, back_ref, alpha_in, upper_ref, lower_ref,
-                  node_grad, edge_one, edge_two, node_one, node_two, bias_out):
+    up = mine[:, used + rim : used + 2 * rim]
+    down = other[:, used + rim : used + 2 * rim]
+    near = jnp.where(even_chip(), up, down)
+    far = jnp.where(even_chip(), down, up)
+    out_ref[...] = padded([mine[:, :used] + other[:, :used], near, far], out_ref.shape[1]).astype(BF)
+
+
+def pass_kernel(used, rim, mine_ref, other_ref, out_ref, near_ref):
     mine = mine_ref[...].astype(F32)
     other = other_ref[...].astype(F32)
-    total = mine + other
+    near_ref[...] = other[:, used : used + rim]
+    out_ref[...] = padded(
+        [mine[:, :used] + other[:, :used], other[:, used + rim : used + 2 * rim]], out_ref.shape[1]
+    ).astype(BF)
+
+
+def add_kernel(used, rim, bit, mine_ref, other_ref, out_ref, far_ref):
+    mine = mine_ref[...].astype(F32)
+    other = other_ref[...].astype(F32)
+    place = lax.axis_index("phi")
+    home = (lax.rem(place // bit, 2) == 1) == even_chip()
+    lane = lax.broadcasted_iota(jnp.int32, other.shape, 1)
+    far_ref[...] = jnp.where(home, other[:, used : used + rim], 0.0)
+    out_ref[...] = jnp.where(lane < used, mine + other, jnp.where(home, 0.0, other)).astype(BF)
+
+
+def close_kernel(used, rim, mine_ref, other_ref, near_ref, done_ref, *refs):
+    mine = mine_ref[...].astype(F32)
+    other = other_ref[...].astype(F32)
+    far = other[:, used : used + rim]
+    for ref in refs[:-2]:
+        far = far + ref[...]
+    out_ref, down_ref = refs[-2:]
+    near = near_ref[...]
+    down_ref[...] = jnp.where(even_chip(), near, far)
+    up = jnp.where(even_chip(), far, near)
+    out_ref[...] = padded([mine[:, :used] + other[:, :used], up], out_ref.shape[1]).astype(BF)
+
+
+def finish_kernel(used, rim, mine_ref, sent_ref, down_ref, first_ref, back_ref, upper_ref, lower_ref,
+                  node_grad, edge_one, edge_two, node_one, node_two, bias_out):
+    even = is_even()
+    sent = sent_ref[...].astype(F32)
+    total = jnp.where(even, sent, mine_ref[...].astype(F32))
     cut = 0
     for ref in (edge_one, edge_two, node_one, node_two):
         ref[...] = total[:, cut : cut + ref.shape[1]]
@@ -499,8 +519,8 @@
     block = used - 4 - (used - 4) % LANES
     turned = total[:, block : block + LANES].T
     bias_out[...] = turned[used - 4 - block : used - block]
-    alpha = alpha_in[...].astype(F32)[:, used : used + rim]
-    beta = mine[:, used : used + rim] + other[:, used + rim : used + 2 * rim]
+    alpha = first_ref[...].astype(F32)[:, used : used + rim]
+    beta = jnp.where(even, sent[:, used : used + rim], down_ref[...])
     grad = back_ref[...] + placed_rims(alpha, beta, upper_ref, lower_ref)
     node_grad[...] = own_rows(grad.T, node_grad.shape[0])
 
@@ -540,6 +560,10 @@
     return swap(value, "phi", lambda index: index - 1 if index % 2 == 0 else index + 1)
 
 
+def by_chips(value, bit):
+    return swap(value, "phi", lambda index: index ^ bit if index % 2 else index)
+
+
 def layer_parts(value):
     groups = lax.axis_size("layer")
     return [value] + [
@@ -617,7 +641,6 @@
         edge_first, edge_second, node_first, bias, cost=2.0,
     )
     total_width = edge_first.shape[1] + hidden + node_first.shape[1] + node_second.shape[1] + 4
-    lanes = -(-(total_width + 2 * rim) // LANES) * LANES
     hidden_one, low, sums_one, node_pre_one, node_grad_one, wanted, first_sums, rims = call(
         middle_kernel,
         [per_slot(BF), per_slot(BF), per_hit(F32), per_hit(F32), per_hit(F32), per_hit(F32),
@@ -629,35 +652,50 @@
     alpha = by_alpha(rims)
     extra, total, joined_one, back, back_node = call(
         functools.partial(carry_kernel, rim),
-        [per_slot(F32), ((latent, lanes), F32), per_hit(BF, 2), per_hit(F32), per_hit(F32)],
+        [per_slot(F32), ((latent, total_width), F32), per_hit(BF, 2), per_hit(F32), per_hit(F32)],
         low, hidden_zero, slab_one, sums_one, sums_zero, message, node_pre_one, node_grad_one, first_sums, count, cot,
         edge_second, first_back, node_first_back, node_second_back, to_hidden, cost=2.0,
     )
-    edge_out, node_out = call(
-        output_kernel, [((latent, slots), BF), ((width, latent), BF)],
+    edge_out, node_out, done = call(
+        output_kernel, [((latent, slots), BF), ((width, latent), BF), ((8, LANES), F32)],
         edge_counts, edges_one, hidden_one, joined_one, node_pre_one, edge_second, node_second, bias,
         scratch=[VM((latent, total_slots), BF)], smem=1, cost=2.0,
     )
+    lanes = -(-(total_width + 2 * rim) // LANES) * LANES
     total, back = call(
         functools.partial(last_kernel, rim), [((latent, lanes), BF), per_hit(F32)],
         back, back_node, beta, alpha, alpha_pick, beta_pick, joined_zero, node_pre_zero, node_hidden_zero, wanted,
         sums_zero, count, extra, slope, onehot, edges_zero, slab_zero, rims_zero, slab_one, total,
-        first_back, node_first_back, to_node_back, to_table_back, cost=2.0,
-    )
-    other = by_alpha(total)
-    alpha_last = other
-    bit = 1
+        first_back, node_first_back, to_node_back, to_table_back,
+        scratch=[VM((hidden, total_slots), BF)], cost=2.0,
+    )
+    payload = ((latent, lanes), BF)
+    rim_block = ((latent, rim), F32)
+    first = by_alpha(total)
+    mine = call(functools.partial(open_kernel, total_width, rim), [payload], total, first, cost=0.1)[0]
+    other = by_chips(mine, 2)
+    mine, near = call(
+        functools.partial(pass_kernel, total_width, rim), [payload, rim_block], mine, other, cost=0.1,
+    )
+    far = []
+    bit = 4
     while 2 * bit < ring:
-        total = call(
-            functools.partial(add_kernel, total_width, rim, bit), [((latent, lanes), BF)], total, other, cost=0.1,
-        )[0]
+        other = by_chips(mine, bit)
+        mine, block = call(
+            functools.partial(add_kernel, total_width, rim, bit), [payload, rim_block], mine, other, cost=0.1,
+        )
+        far.append(block)
         bit *= 2
-        other = swap(total, "phi", lambda index, bit=bit: index ^ bit)
+    other = by_chips(mine, bit)
+    mine, down = call(
+        functools.partial(close_kernel, total_width, rim), [payload, rim_block], mine, other, near, done, *far, cost=0.1,
+    )
+    sent = by_alpha(mine)
     node_grad, edge_one, edge_two, node_one, node_two, bias_out = call(
         functools.partial(finish_kernel, total_width, rim),
         [((width, latent), F32), (edge_first.shape, F32), (edge_second.shape, F32),
          (node_first.shape, F32), (node_second.shape, F32), (biases.shape, F32)],
-        total, other, back, alpha_last, upper, lower,
+        mine, sent, down, first, back, upper, lower,
     )
     return node_out.T, edge_out, node_grad.T, edge_one, edge_two, node_one, node_two, bias_out
 

time: 48.7 us -> 51.3 us (1.053)
  starting transfers between devices: 12.7 us -> 27.7 us
  waiting for transfers between devices: 20.8 us -> 8.77 us
    ppermute x12 -> x13, starting transfers between devices: 12.7 us -> 27.7 us  [swap(): lax.ppermute(value, axis, [(source, pairing(source) % count) for source i...]
    ppermute x12 -> x13, waiting for transfers between devices: 20.8 us -> 8.77 us  [swap(): lax.ppermute(value, axis, [(source, pairing(source) % count) for source i...]
    pallas_call x15 -> x16, Pallas kernels: 13.5 us -> 13.2 us  [call(): pl.pallas_call(kernel, out_shape=[jax.ShapeDtypeStruct(shape, kind) for s...]
  transfers between devices with their start and end apart: 12 -> 13, of which waited for: 8 -> 6; matrix products, arithmetic and copies ran while one was open for 0% -> 0% of each run, Pallas kernels for 10% -> 11%
where the time goes in v4:
time: 51.3 us; the launch traced here: 51.1 us
  starting transfers between devices  27.7 us (54%)
  Pallas kernels  13.2 us (26%)
  waiting for transfers between devices  8.77 us (17%)
  between operations  1.45 us (3%)
    ppermute x13, starting transfers between devices, swap(): lax.ppermute(value, axis, [(source, pairing(source) % count) for source i...  27.7 us
    pallas_call x16, Pallas kernels, call(): pl.pallas_call(kernel, out_shape=[jax.ShapeDtypeStruct(shape, kind) for s...  13.2 us
    ppermute x13, waiting for transfers between devices, swap(): lax.ppermute(value, axis, [(source, pairing(source) % count) for source i...  8.77 us
  transfers between devices with their start and end apart: 13, of which 6 were waited for; matrix products, arithmetic and copies ran while one was open for 0% of the time, Pallas kernels for 11%

profile of v4, /device:TPU:0, one launch (start us, length us, event | category | flops | bytes accessed | tf_op | source)
XLA Modules:
  0.0 51.1 jit_solution(6980305752025861046)
XLA Ops:
  1.3 0.0 copy-start
  1.3 0.9 %shard_map.188 = (bf16[80,128]{1,0:T(8,128)(2,1)S(1)}, s32[1,24]{1,0:T(1,128)S(1)}, s32[1,24]{1,0:T(1,128)S(1)}) custom-call(s32[1,1]{1,0:T(1,128)S(6)} %copy.21.count_ref, s32[16,128]{1,0:T(8,128)} %bitcast.7, s32[16,128]{1,0:T(8,128)} %bitcast.8, bf16[32,64]{1,0:T(8,128)(2,1)} %bitcast.9, f32[32,64]{1,0:T(8,128)} %bitcast.6, s32[1,24]{1,0:T(1,128)} %upper_hbm.1, ...), custom_call_target="tpu_custom_call" | custom-call | flops 1000000000 | bytes 3600000 | tf_op jit(solution)/shard_map/pallas_call | solution.py:537
  2.2 3.0 %collective-permute-start.1 = (bf16[80,128]{1,0:T(8,128)(2,1)S(1)}, bf16[80,128]{1,0:T(8,128)(2,1)S(1)}, u32[]{:S(2)}, u32[]{:S(2)}) collective-permute-start(bf16[80,128]{1,0:T(8,128)(2,1)S(1)} %get-tuple-element.84.packed_ref.refs_0_), channel_id=1, source_target_pairs={{0,1},{1,0},{2,3},{3,2},{4,5},{5,4},{6,7},{7,6},{8,9},{9,8},{10,11... | collective-permute-start | bytes 61448 | tf_op jit(solution)/shard_map/ppermute | solution.py:552
  5.2 0.1 shard_map.189
  5.3 0.0 copy-done
  5.3 0.1 collective-permute-start
  5.4 1.6 %collective-permute-done.1.refs_1_ = bf16[80,128]{1,0:T(8,128)(2,1)S(1)} collective-permute-done((bf16[80,128]{1,0:T(8,128)(2,1)S(1)}, bf16[80,128]{1,0:T(8,128)(2,1)S(1)}, u32[]{:S(2)}, u32[]{:S(2)}) %collective-permute-start.1) | collective-permute-done | bytes 20512 | tf_op jit(solution)/shard_map/ppermute | solution.py:552
  7.0 0.0 copy-start.5
  7.0 0.2 shard_map.190
  7.2 3.4 %collective-permute-start.2 = (bf16[64,64]{1,0:T(8,128)(2,1)S(1)}, bf16[64,64]{1,0:T(8,128)(2,1)S(1)}, u32[]{:S(2)}, u32[]{:S(2)}) collective-permute-start(bf16[64,64]{1,0:T(8,128)(2,1)S(1)} %get-tuple-element.97), channel_id=1, source_target_pairs={{0,30},{2,4},{4,2},{6,8},{8,6},{10,12},{12,10},{14,16},{16,14},{18... | collective-permute-start | bytes 24584 | tf_op jit(solution)/shard_map/ppermute | solution.py:552
  10.6 0.0 collective-permute-start.3
  10.6 0.0 copy-done.1
  10.6 0.0 copy-done.2
  10.6 0.0 copy-done.3
  10.7 1.6 %shard_map.191 = (bf16[192,4096]{1,0:T(8,128)(2,1)S(1)}, f32[64,4096]{1,0:T(8,128)S(1)}, f32[8,64]{1,0:T(8,128)S(1)}, f32[64,64]{1,0:T(8,128)S(1)}, bf16[192,64]...) custom-call(bf16[80,128]{1,0:T(8,128)(2,1)S(1)} %get-tuple-element.8, ...), custom_call_target="tpu_custom_call" | custom-call | flops 2000000000 | bytes 7200000 | tf_op jit(solution)/shard_map/pallas_call | solution.py:537
  12.3 0.9 %collective-permute-done.refs_1_ = bf16[64,2048]{1,0:T(8,128)(2,1)S(1)} collective-permute-done((bf16[64,2048]{1,0:T(8,128)(2,1)S(1)}, bf16[64,2048]{1,0:T(8,128)(2,1)S(1)}, u32[]{:S(2)}, u32[]{:S(2)}) %collective-permute-start) | collective-permute-done | bytes 262176 | tf_op jit(solution)/shard_map/ppermute | solution.py:552
  13.2 0.6 %shard_map.192 = (bf16[64,4096]{1,0:T(8,128)(2,1)S(1)}, f32[64,4096]{1,0:T(8,128)S(1)}, f32[64,64]{1,0:T(8,128)S(1)}, f32[64,64]{1,0:T(8,128)S(1)}) custom-call(bf16[64,2048]{1,0:T(8,128)(2,1)S(1)} %copy-done, bf16[64,2048]{1,0:T(8,128)(2,1)S(1)} %collective-permute-done.refs_1_, f32[64,4096]{1,0:T(8,128)S(1)} %get-tuple-element.91.refs_2_, ...), custom_call_target="tpu_custom_call" | custom-call | flops 1000000000 | bytes 3600000 | tf_op jit(solution)/shard_map/pallas_call | solution.py:537
  13.7 0.0 collective-permute-done.2.beta_in
  13.8 0.0 collective-permute-done.3.alpha_in
  13.8 1.4 %shard_map.193 = (bf16[64,4096]{1,0:T(8,128)(2,1)S(1)}, f32[64,4096]{1,0:T(8,128)S(1)}, bf16[64,64]{1,0:T(8,128)(2,1)S(1)}, f32[64,64]{1,0:T(8,128)S(1)}, f32[64...) custom-call(f32[64,4096]{1,0:T(8,128)S(1)} %get-tuple-element.96.bas, ...), custom_call_target="tpu_custom_call" | custom-call | flops 2000000000 | bytes 7200000 | tf_op jit(solution)/shard_map/pallas_call | solution.py:537
  15.2 2.9 %collective-permute-start.4 = (bf16[64,128]{1,0:T(8,128)(2,1)S(1)}, bf16[64,128]{1,0:T(8,128)(2,1)S(1)}, u32[]{:S(2)}, u32[]{:S(2)}) collective-permute-start(bf16[64,128]{1,0:T(8,128)(2,1)S(1)} %get-tuple-element.112), channel_id=1, source_target_pairs={{0,30},{2,4},{4,2},{6,8},{8,6},{10,12},{12,10},{14,16},{16,14},{18... | collective-permute-start | bytes 49160 | tf_op jit(solution)/shard_map/ppermute | solution.py:552
  18.1 0.0 collective-permute-start.5
  18.1 1.1 %shard_map.194 = (bf16[64,4096]{1,0:T(8,128)(2,1)S(1)}, f32[64,4096]{1,0:T(8,128)S(1)}, f32[64,64]{1,0:T(8,128)S(1)}, bf16[128,64]{1,0:T(8,128)(2,1)S(1)}, f32[64,64]{1,0:T(8,128)S(1)}) custom-call(bf16[64,4096]{1,0:T(8,128)(2,1)S(1)} %get-tuple-element.95.edges_ref, bf16[64,4096]{1,0:T(8,128)(2,1)S(1)} %get-tuple-element.105.hidden_ref.hidden_zero_ref, ...), custom_call_target="tpu_custom_call" | custom-call | flops 2000000000 | bytes 7200000 | tf_op jit(solution)/shard_map/pallas_call | solution.py:537
  19.2 1.9 %collective-permute-done.4.beta_in = bf16[64,128]{1,0:T(8,128)(2,1)S(1)} collective-permute-done((bf16[64,128]{1,0:T(8,128)(2,1)S(1)}, bf16[64,128]{1,0:T(8,128)(2,1)S(1)}, u32[]{:S(2)}, u32[]{:S(2)}) %collective-permute-start.4) | collective-permute-done | bytes 16416 | tf_op jit(solution)/shard_map/ppermute | solution.py:552
  21.1 0.0 collective-permute-done.5.alpha_in
  21.1 2.0 %shard_map.195 = (bf16[64,4096]{1,0:T(8,128)(2,1)S(1)}, bf16[64,4096]{1,0:T(8,128)(2,1)S(1)}, f32[64,64]{1,0:T(8,128)S(1)}, f32[64,64]{1,0:T(8,128)S(1)}, f32[64...) custom-call(f32[64,4096]{1,0:T(8,128)S(1)} %get-tuple-element.111.base_ref, ...), custom_call_target="tpu_custom_call" | custom-call | flops 3000000000 | bytes 10800000 | tf_op jit(solution)/shard_map/pallas_call | solution.py:537
  23.2 2.8 %collective-permute-start.6 = (bf16[64,64]{1,0:T(8,128)(2,1)S(1)}, bf16[64,64]{1,0:T(8,128)(2,1)S(1)}, u32[]{:S(2)}, u32[]{:S(2)}) collective-permute-start(bf16[64,64]{1,0:T(8,128)(2,1)S(1)} %get-tuple-element.133), channel_id=1, source_target_pairs={{0,30},{2,4},{4,2},{6,8},{8,6},{10,12},{12,10},{14,16},{16,14},{18... | collective-permute-start | bytes 24584 | tf_op jit(solution)/shard_map/ppermute | solution.py:552
  26.0 0.0 collective-permute-start.7
  26.0 0.9 %shard_map.196 = (f32[64,4096]{1,0:T(8,128)S(1)}, f32[64,452]{1,0:T(8,128)S(1)}, bf16[128,64]{1,0:T(8,128)(2,1)S(1)}, f32[64,64]{1,0:T(8,128)S(1)}, f32[64,64]{1,0:T(8,128)S(1)}) custom-call(bf16[64,4096]{1,0:T(8,128)(2,1)S(1)} %get-tuple-element.119.low_ref, bf16[64,4096]{1,0:T(8,128)(2,1)S(1)} %get-tuple-element.105.hidden_ref.hidden_zero_ref, ...), custom_call_target="tpu_custom_call" | custom-call | flops 2000000000 | bytes 7200000 | tf_op jit(solution)/shard_map/pallas_call | solution.py:537
  26.9 2.2 %collective-permute-done.6.beta_in = bf16[64,64]{1,0:T(8,128)(2,1)S(1)} collective-permute-done((bf16[64,64]{1,0:T(8,128)(2,1)S(1)}, bf16[64,64]{1,0:T(8,128)(2,1)S(1)}, u32[]{:S(2)}, u32[]{:S(2)}) %collective-permute-start.6) | collective-permute-done | bytes 8224 | tf_op jit(solution)/shard_map/ppermute | solution.py:552
  29.1 0.0 collective-permute-done.7.alpha_in
  29.1 1.9 %shard_map.198 = (bf16[64,512]{1,0:T(8,128)(2,1)S(1)}, f32[64,64]{1,0:T(8,128)S(1)}) custom-call(f32[64,64]{1,0:T(8,128)S(1)} %get-tuple-element.131.back_in, f32[64,64]{1,0:T(8,128)S(1)} %get-tuple-element.132.back_node, bf16[64,64]{1,0:T(8,128)(2,1)S(1)} %collective-permute-done.6.beta_in, bf16[64,64]{1,0:T(8,128)(2,1)S(1)} %collective-permute-done.7.alpha_in, ...), custom_call_target="tpu_custom_call" | custom-call | flops 2000000000 | bytes 7200000 | tf_op jit(solution)/shard_map/pallas_call | solution.py:537
  31.0 0.1 collective-permute-start.8
  31.0 1.2 %collective-permute-done.8.other_ref.first_ref = bf16[64,512]{1,0:T(8,128)(2,1)S(1)} collective-permute-done((bf16[64,512]{1,0:T(8,128)(2,1)S(1)}, bf16[64,512]{1,0:T(8,128)(2,1)S(1)}, u32[]{:S(2)}, u32[]{:S(2)}) %collective-permute-start.8) | collective-permute-done | bytes 65568 | tf_op jit(solution)/shard_map/ppermute | solution.py:552
  32.3 0.1 shard_map.199.mine_ref
  32.4 0.7 %collective-permute-start.9 = (bf16[64,512]{1,0:T(8,128)(2,1)S(1)}, bf16[64,512]{1,0:T(8,128)(2,1)S(1)}, u32[]{:S(2)}, u32[]{:S(2)}) collective-permute-start(bf16[64,512]{1,0:T(8,128)(2,1)S(1)} %shard_map.199.mine_ref), channel_id=1, source_target_pairs={{0,0},{2,6},{4,4},{6,2},{8,8},{10,14},{12,12},{14,10},{16,16},{18,... | collective-permute-start | bytes 196616 | tf_op jit(solution)/shard_map/ppermute | solution.py:552
  33.0 0.0 collective-permute-done.9.other_ref
  33.0 0.1 shard_map.200
  33.1 0.7 %collective-permute-start.10 = (bf16[64,512]{1,0:T(8,128)(2,1)S(1)}, bf16[64,512]{1,0:T(8,128)(2,1)S(1)}, u32[]{:S(2)}, u32[]{:S(2)}) collective-permute-start(bf16[64,512]{1,0:T(8,128)(2,1)S(1)} %get-tuple-element.144.mine_ref), channel_id=1, source_target_pairs={{0,0},{2,10},{4,4},{6,14},{8,8},{10,2},{12,12},{14,6},{16,16},{18,... | collective-permute-start | bytes 196616 | tf_op jit(solution)/shard_map/ppermute | solution.py:552
  33.8 0.0 collective-permute-done.10.other_ref
  33.8 0.1 shard_map.201
  33.9 0.7 %collective-permute-start.11 = (bf16[64,512]{1,0:T(8,128)(2,1)S(1)}, bf16[64,512]{1,0:T(8,128)(2,1)S(1)}, u32[]{:S(2)}, u32[]{:S(2)}) collective-permute-start(bf16[64,512]{1,0:T(8,128)(2,1)S(1)} %get-tuple-element.145.mine_ref), channel_id=1, source_target_pairs={{0,0},{2,18},{4,4},{6,22},{8,8},{10,26},{12,12},{14,30},{16,16},{1... | collective-permute-start | bytes 196616 | tf_op jit(solution)/shard_map/ppermute | solution.py:552
  34.6 1.1 %shard_map.197 = (bf16[64,2048]{1,0:T(8,128)(2,1)}, bf16[32,64]{1,0:T(8,128)(2,1)}, f32[8,128]{1,0:T(8,128)S(1)}) custom-call(s32[1,1]{1,0:T(1,128)S(6)} %copy.21.count_ref, bf16[64,4096]{1,0:T(8,128)(2,1)S(1)} %get-tuple-element.110.edges_ref, bf16[64,4096]{1,0:T(8,128)(2,1)S(1)} %get-tuple-element.118.hidden_ref, ...), custom_call_target="tpu_custom_call" | custom-call | flops 2000000000 | bytes 7200000 | tf_op jit(solution)/shard_map/pallas_call | solution.py:537
  35.7 0.0 collective-permute-done.11.other_ref
  35.7 0.1 shard_map.202
  35.8 13.4 %collective-permute-start.12 = (bf16[64,512]{1,0:T(8,128)(2,1)S(1)}, bf16[64,512]{1,0:T(8,128)(2,1)S(1)}, u32[]{:S(2)}, u32[]{:S(2)}) collective-permute-start(bf16[64,512]{1,0:T(8,128)(2,1)S(1)} %get-tuple-element.149.mine_ref), channel_id=1, source_target_pairs={{0,2},{2,0},{4,6},{6,4},{8,10},{10,8},{12,14},{14,12},{16,18},{18,... | collective-permute-start | bytes 196616 | tf_op jit(solution)/shard_map/ppermute | solution.py:552
  49.2 0.9 %collective-permute-done.12.sent_ref = bf16[64,512]{1,0:T(8,128)(2,1)S(1)} collective-permute-done((bf16[64,512]{1,0:T(8,128)(2,1)S(1)}, bf16[64,512]{1,0:T(8,128)(2,1)S(1)}, u32[]{:S(2)}, u32[]{:S(2)}) %collective-permute-start.12) | collective-permute-done | bytes 65568 | tf_op jit(solution)/shard_map/ppermute | solution.py:552
  50.1 1.0 %shard_map.203 = (f32[32,64]{1,0:T(8,128)}, f32[64,192]{1,0:T(8,128)}, f32[64,64]{1,0:T(8,128)}, f32[64,128]{1,0:T(8,128)}, f32[64,64]{1,0:T(8,128)}, /*index=5*/f32[4,64]{1,0:T(4,128)}) custom-call(bf16[64,512]{1,0:T(8,128)(2,1)S(1)} %get-tuple-element.149.mine_ref, bf16[64,512]{1,0:T(8,128)(2,1)S(1)} %collective-permute-done.12.sent_ref, ...), custom_call_target="tpu_custom_call" | custom-call | flops 1000000000 | bytes 3600000 | tf_op jit(solution)/shard_map/pallas_call | solution.py:537
  (6 shorter events, 0.0 us)
Async XLA Ops:
  1.3 4.0 %copy-start = (bf16[64,2048]{1,0:T(8,128)(2,1)S(1)}, bf16[64,2048]{1,0:T(8,128)(2,1)}, u32[]{:S(2)}) copy-start(bf16[64,2048]{1,0:T(8,128)(2,1)} %refs_0_.1) | copy-start | bytes 786436
  2.2 4.8 %collective-permute-start.1 = (bf16[80,128]{1,0:T(8,128)(2,1)S(1)}, bf16[80,128]{1,0:T(8,128)(2,1)S(1)}, u32[]{:S(2)}, u32[]{:S(2)}) collective-permute-start(bf16[80,128]{1,0:T(8,128)(2,1)S(1)} %get-tuple-element.84.packed_ref.refs_0_), channel_id=1, source_target_pairs={{0,1},{1,0},{2,3},{3,2},{4,5},{5,4},{6,7},{7,6},{8,9},{9,8},{10,11... | collective-permute-start | bytes 61448 | tf_op jit(solution)/shard_map/ppermute | solution.py:552
  5.3 7.8 %collective-permute-start = (bf16[64,2048]{1,0:T(8,128)(2,1)S(1)}, bf16[64,2048]{1,0:T(8,128)(2,1)S(1)}, u32[]{:S(2)}, u32[]{:S(2)}) collective-permute-start(bf16[64,2048]{1,0:T(8,128)(2,1)S(1)} %copy-done), channel_id=1, source_target_pairs={{0,1},{1,0},{2,3},{3,2},{4,5},{5,4},{6,7},{7,6},{8,9},{9,8},{10,11... | collective-permute-start | bytes 786440 | tf_op jit(solution)/shard_map/ppermute | solution.py:552
  7.0 3.6 %copy-start.1 = (bf16[64,192]{1,0:T(8,128)(2,1)S(1)}, bf16[64,192]{1,0:T(8,128)(2,1)}, u32[]{:S(2)}) copy-start(bf16[64,192]{1,0:T(8,128)(2,1)} %first_ref.3) | copy-start | bytes 73732
  7.0 3.6 %copy-start.2 = (bf16[64,128]{1,0:T(8,128)(2,1)S(1)}, bf16[64,128]{1,0:T(8,128)(2,1)}, u32[]{:S(2)}) copy-start(bf16[64,128]{1,0:T(8,128)(2,1)} %node_first_ref.1) | copy-start | bytes 49156
  7.0 3.6 %copy-start.3 = (bf16[64,64]{1,0:T(8,128)(2,1)S(1)}, bf16[64,64]{1,0:T(8,128)(2,1)}, u32[]{:S(2)}) copy-start(bf16[64,64]{1,0:T(8,128)(2,1)} %second_ref.5) | copy-start | bytes 24580
  7.0 3.6 %copy-start.4 = (bf16[64,64]{1,0:T(8,128)(2,1)S(1)}, bf16[64,64]{1,0:T(8,128)(2,1)}, u32[]{:S(2)}) copy-start(bf16[64,64]{1,0:T(8,128)(2,1)} %node_second_ref.3) | copy-start | bytes 24580
  7.0 3.6 %copy-start.5 = (f32[4,64]{1,0:T(4,128)S(1)}, f32[4,64]{1,0:T(4,128)}, u32[]{:S(2)}) copy-start(f32[4,64]{1,0:T(4,128)} %refs_7_.2) | copy-start | bytes 3076
  7.2 6.5 %collective-permute-start.2 = (bf16[64,64]{1,0:T(8,128)(2,1)S(1)}, bf16[64,64]{1,0:T(8,128)(2,1)S(1)}, u32[]{:S(2)}, u32[]{:S(2)}) collective-permute-start(bf16[64,64]{1,0:T(8,128)(2,1)S(1)} %get-tuple-element.97), channel_id=1, source_target_pairs={{0,30},{2,4},{4,2},{6,8},{8,6},{10,12},{12,10},{14,16},{16,14},{18... | collective-permute-start | bytes 24584 | tf_op jit(solution)/shard_map/ppermute | solution.py:552
  10.6 3.1 %collective-permute-start.3 = (bf16[64,64]{1,0:T(8,128)(2,1)S(1)}, bf16[64,64]{1,0:T(8,128)(2,1)S(1)}, u32[]{:S(2)}, u32[]{:S(2)}) collective-permute-start(bf16[64,64]{1,0:T(8,128)(2,1)S(1)} %get-tuple-element.98), channel_id=1, source_target_pairs={{0,2},{2,0},{4,6},{6,4},{8,10},{10,8},{12,14},{14,12},{16,18},{18,... | collective-permute-start | bytes 24584 | tf_op jit(solution)/shard_map/ppermute | solution.py:552
  15.2 5.9 %collective-permute-start.4 = (bf16[64,128]{1,0:T(8,128)(2,1)S(1)}, bf16[64,128]{1,0:T(8,128)(2,1)S(1)}, u32[]{:S(2)}, u32[]{:S(2)}) collective-permute-start(bf16[64,128]{1,0:T(8,128)(2,1)S(1)} %get-tuple-element.112), channel_id=1, source_target_pairs={{0,30},{2,4},{4,2},{6,8},{8,6},{10,12},{12,10},{14,16},{16,14},{18... | collective-permute-start | bytes 49160 | tf_op jit(solution)/shard_map/ppermute | solution.py:552
  18.1 3.1 %collective-permute-start.5 = (bf16[64,128]{1,0:T(8,128)(2,1)S(1)}, bf16[64,128]{1,0:T(8,128)(2,1)S(1)}, u32[]{:S(2)}, u32[]{:S(2)}) collective-permute-start(bf16[64,128]{1,0:T(8,128)(2,1)S(1)} %get-tuple-element.113), channel_id=1, source_target_pairs={{0,2},{2,0},{4,6},{6,4},{8,10},{10,8},{12,14},{14,12},{16,18},{18,... | collective-permute-start | bytes 49160 | tf_op jit(solution)/shard_map/ppermute | solution.py:552
  23.2 5.9 %collective-permute-start.6 = (bf16[64,64]{1,0:T(8,128)(2,1)S(1)}, bf16[64,64]{1,0:T(8,128)(2,1)S(1)}, u32[]{:S(2)}, u32[]{:S(2)}) collective-permute-start(bf16[64,64]{1,0:T(8,128)(2,1)S(1)} %get-tuple-element.133), channel_id=1, source_target_pairs={{0,30},{2,4},{4,2},{6,8},{8,6},{10,12},{12,10},{14,16},{16,14},{18... | collective-permute-start | bytes 24584 | tf_op jit(solution)/shard_map/ppermute | solution.py:552
  26.0 3.1 %collective-permute-start.7 = (bf16[64,64]{1,0:T(8,128)(2,1)S(1)}, bf16[64,64]{1,0:T(8,128)(2,1)S(1)}, u32[]{:S(2)}, u32[]{:S(2)}) collective-permute-start(bf16[64,64]{1,0:T(8,128)(2,1)S(1)} %get-tuple-element.133), channel_id=1, source_target_pairs={{0,2},{2,0},{4,6},{6,4},{8,10},{10,8},{12,14},{14,12},{16,18},{18,... | collective-permute-start | bytes 24584 | tf_op jit(solution)/shard_map/ppermute | solution.py:552
  31.0 1.3 %collective-permute-start.8 = (bf16[64,512]{1,0:T(8,128)(2,1)S(1)}, bf16[64,512]{1,0:T(8,128)(2,1)S(1)}, u32[]{:S(2)}, u32[]{:S(2)}) collective-permute-start(bf16[64,512]{1,0:T(8,128)(2,1)S(1)} %get-tuple-element.143.mine_ref), channel_id=1, source_target_pairs={{0,2},{2,0},{4,6},{6,4},{8,10},{10,8},{12,14},{14,12},{16,18},{18,... | collective-permute-start | bytes 196616 | tf_op jit(solution)/shard_map/ppermute | solution.py:552
  32.4 0.7 %collective-permute-start.9 = (bf16[64,512]{1,0:T(8,128)(2,1)S(1)}, bf16[64,512]{1,0:T(8,128)(2,1)S(1)}, u32[]{:S(2)}, u32[]{:S(2)}) collective-permute-start(bf16[64,512]{1,0:T(8,128)(2,1)S(1)} %shard_map.199.mine_ref), channel_id=1, source_target_pairs={{0,0},{2,6},{4,4},{6,2},{8,8},{10,14},{12,12},{14,10},{16,16},{18,... | collective-permute-start | bytes 196616 | tf_op jit(solution)/shard_map/ppermute | solution.py:552
  33.1 0.7 %collective-permute-start.10 = (bf16[64,512]{1,0:T(8,128)(2,1)S(1)}, bf16[64,512]{1,0:T(8,128)(2,1)S(1)}, u32[]{:S(2)}, u32[]{:S(2)}) collective-permute-start(bf16[64,512]{1,0:T(8,128)(2,1)S(1)} %get-tuple-element.144.mine_ref), channel_id=1, source_target_pairs={{0,0},{2,10},{4,4},{6,14},{8,8},{10,2},{12,12},{14,6},{16,16},{18,... | collective-permute-start | bytes 196616 | tf_op jit(solution)/shard_map/ppermute | solution.py:552
  33.9 1.8 %collective-permute-start.11 = (bf16[64,512]{1,0:T(8,128)(2,1)S(1)}, bf16[64,512]{1,0:T(8,128)(2,1)S(1)}, u32[]{:S(2)}, u32[]{:S(2)}) collective-permute-start(bf16[64,512]{1,0:T(8,128)(2,1)S(1)} %get-tuple-element.145.mine_ref), channel_id=1, source_target_pairs={{0,0},{2,18},{4,4},{6,22},{8,8},{10,26},{12,12},{14,30},{16,16},{1... | collective-permute-start | bytes 196616 | tf_op jit(solution)/shard_map/ppermute | solution.py:552
  35.8 14.3 %collective-permute-start.12 = (bf16[64,512]{1,0:T(8,128)(2,1)S(1)}, bf16[64,512]{1,0:T(8,128)(2,1)S(1)}, u32[]{:S(2)}, u32[]{:S(2)}) collective-permute-start(bf16[64,512]{1,0:T(8,128)(2,1)S(1)} %get-tuple-element.149.mine_ref), channel_id=1, source_target_pairs={{0,2},{2,0},{4,6},{6,4},{8,10},{10,8},{12,14},{14,12},{16,18},{18,... | collective-permute-start | bytes 196616 | tf_op jit(solution)/shard_map/ppermute | solution.py:552

commit v5 on v4

--- a/solution.py
+++ b/solution.py
@@ -394,7 +394,7 @@
 
 
 def output_kernel(count_ref, edges_ref, hidden_ref, joined_ref, node_pre_ref, second_ref, node_second_ref, bias_ref,
-                  edge_out, node_out, done_ref, new_ref):
+                  edge_out, node_out, new_ref):
     bias = bias_ref[...]
     latent = edges_ref.shape[0]
     second = second_ref[...]
@@ -411,13 +411,12 @@
     node_hidden = slope_parts(node_pre_ref[...])[0].astype(BF)
     state = joined_ref[:latent].astype(F32) + mm(node_second_ref[...], node_hidden) + bias[:, 3:4]
     node_out[...] = own_rows(state.T, node_out.shape[0]).astype(BF)
-    done_ref[...] = jnp.zeros_like(done_ref)
 
 
 def last_kernel(rim, back_in, back_node, beta_in, alpha_in, alpha_pick, beta_pick, joined_ref, node_pre_ref,
                 node_hidden_ref, wanted_in, sums_ref, count_ref, extra_ref, slope_ref, onehot_ref, edges_ref,
                 slab_ref, rims_ref, slab_one_ref, total_in, first_back, node_first_back, to_node_back, to_table_back,
-                total_ref, back_ref, low_ref):
+                keep_ref, send_ref, back_ref, low_ref):
     latent, slab = slab_ref.shape
     wide = onehot_ref.shape[0] - slab
     placed = mm_nt(alpha_in[...], alpha_pick[...]) + mm_nt(beta_in[...], beta_pick[...])
@@ -451,67 +450,76 @@
     total = total_in[...] + jnp.concatenate(
         [edge_one, edge_two, node_one, node_two, pre_sum, gm_sum, node_pre_sum, grad_sum], axis=1
     )
-    total_ref[...] = padded([total, alpha, beta], total_ref.shape[1]).astype(BF)
-
-
-def padded(pieces, width):
-    spare = width - sum(piece.shape[1] for piece in pieces)
+    even = is_even()
+    half, used = keep_ref.shape
+    keep_ref[...] = jnp.where(even, total[:half], total[half:])
+    pieces = [jnp.where(even, total[half:], total[:half]), alpha[:half], alpha[half:], beta[:half], beta[half:]]
+    spare = send_ref.shape[1] - used - 4 * rim
     if spare:
-        pieces = pieces + [jnp.zeros((pieces[0].shape[0], spare), F32)]
-    return jnp.concatenate(pieces, axis=1)
-
-
-def even_chip():
-    return lax.rem(lax.axis_index("phi") // 2, 2) == 0
-
-
-def open_kernel(used, rim, mine_ref, other_ref, out_ref):
-    mine = mine_ref[...].astype(F32)
+        pieces.append(jnp.zeros((half, spare), F32))
+    send_ref[...] = jnp.concatenate(pieces, axis=1).astype(BF)
+
+
+def open_kernel(rim, keep_ref, other_ref, out_ref):
+    half, used = keep_ref.shape
     other = other_ref[...].astype(F32)
-    up = mine[:, used + rim : used + 2 * rim]
-    down = other[:, used + rim : used + 2 * rim]
-    near = jnp.where(even_chip(), up, down)
-    far = jnp.where(even_chip(), down, up)
-    out_ref[...] = padded([mine[:, :used] + other[:, :used], near, far], out_ref.shape[1]).astype(BF)
+    pieces = [keep_ref[...] + other[:, :used], other[:, used + 2 * rim : used + 4 * rim]]
+    spare = out_ref.shape[1] - used - 2 * rim
+    if spare:
+        pieces.append(jnp.zeros((half, spare), F32))
+    out_ref[...] = jnp.concatenate(pieces, axis=1).astype(BF)
 
 
 def pass_kernel(used, rim, mine_ref, other_ref, out_ref, near_ref):
-    mine = mine_ref[...].astype(F32)
     other = other_ref[...].astype(F32)
-    near_ref[...] = other[:, used : used + rim]
-    out_ref[...] = padded(
-        [mine[:, :used] + other[:, :used], other[:, used + rim : used + 2 * rim]], out_ref.shape[1]
-    ).astype(BF)
-
-
-def add_kernel(used, rim, bit, mine_ref, other_ref, out_ref, far_ref):
-    mine = mine_ref[...].astype(F32)
-    other = other_ref[...].astype(F32)
+    total = mine_ref[...].astype(F32)[:, :used] + other[:, :used]
     place = lax.axis_index("phi")
-    home = (lax.rem(place // bit, 2) == 1) == even_chip()
-    lane = lax.broadcasted_iota(jnp.int32, other.shape, 1)
-    far_ref[...] = jnp.where(home, other[:, used : used + rim], 0.0)
-    out_ref[...] = jnp.where(lane < used, mine + other, jnp.where(home, 0.0, other)).astype(BF)
-
-
-def close_kernel(used, rim, mine_ref, other_ref, near_ref, done_ref, *refs):
-    mine = mine_ref[...].astype(F32)
-    other = other_ref[...].astype(F32)
-    far = other[:, used : used + rim]
-    for ref in refs[:-2]:
-        far = far + ref[...]
-    out_ref, down_ref = refs[-2:]
-    near = near_ref[...]
-    down_ref[...] = jnp.where(even_chip(), near, far)
-    up = jnp.where(even_chip(), far, near)
-    out_ref[...] = padded([mine[:, :used] + other[:, :used], up], out_ref.shape[1]).astype(BF)
-
-
-def finish_kernel(used, rim, mine_ref, sent_ref, down_ref, first_ref, back_ref, upper_ref, lower_ref,
-                  node_grad, edge_one, edge_two, node_one, node_two, bias_out):
+    home = (lax.rem(place // 2, 2) == 1) == (lax.rem(place, 2) == 0)
+    held = other[:, used : used + 2 * rim]
+    near_ref[...] = jnp.where(home, held, 0.0)
+    pieces = [total, jnp.where(home, 0.0, held)]
+    spare = out_ref.shape[1] - used - 2 * rim
+    if spare:
+        pieces.append(jnp.zeros((total.shape[0], spare), F32))
+    block = jnp.concatenate(pieces, axis=1).astype(BF)
+    half = block.shape[0]
+    for first in range(0, out_ref.shape[0], half):
+        out_ref[first : first + half] = block
+
+
+def close_kernel(used, rim, count, all_ref, near_ref, half_ref, beta_ref):
+    half = half_ref.shape[0]
+    blocks = [all_ref[rank * half : (rank + 1) * half].astype(F32) for rank in range(count)]
+    total = blocks[0]
+    for block in blocks[1:]:
+        total = total + block
+    half_ref[...] = total
+    place = lax.axis_index("phi")
+    here = place // 4
+    step = jnp.where(lax.rem(place, 2) == 0, count - 1, 1)
+    source = lax.rem(here + step, count)
+    held = blocks[0]
+    for rank in range(1, count):
+        held = jnp.where(source == rank, blocks[rank], held)
+    beta_ref[...] = near_ref[...] + held[:, used : used + 2 * rim]
+
+
+def rims_of(value, used, rim):
+    return jnp.concatenate([value[:, used : used + rim], value[:, used + rim : used + 2 * rim]], axis=0)
+
+
+def node_kernel(used, rim, first_ref, beta_ref, back_ref, upper_ref, lower_ref, node_grad):
+    alpha = rims_of(first_ref[...].astype(F32), used, rim)
+    beta = rims_of(beta_ref[...], 0, rim)
+    grad = back_ref[...] + placed_rims(alpha, beta, upper_ref, lower_ref)
+    node_grad[...] = own_rows(grad.T, node_grad.shape[0])
+
+
+def finish_kernel(used, half_ref, other_ref, edge_one, edge_two, node_one, node_two, bias_out):
     even = is_even()
-    sent = sent_ref[...].astype(F32)
-    total = jnp.where(even, sent, mine_ref[...].astype(F32))
+    mine = half_ref[...]
+    other = other_ref[...]
+    total = jnp.concatenate([jnp.where(even, mine, other), jnp.where(even, other, mine)], axis=0)
     cut = 0
     for ref in (edge_one, edge_two, node_one, node_two):
         ref[...] = total[:, cut : cut + ref.shape[1]]
@@ -519,10 +527,6 @@
     block = used - 4 - (used - 4) % LANES
     turned = total[:, block : block + LANES].T
     bias_out[...] = turned[used - 4 - block : used - block]
-    alpha = first_ref[...].astype(F32)[:, used : used + rim]
-    beta = jnp.where(even, sent[:, used : used + rim], down_ref[...])
-    grad = back_ref[...] + placed_rims(alpha, beta, upper_ref, lower_ref)
-    node_grad[...] = own_rows(grad.T, node_grad.shape[0])
 
 
 def call(kernel, outs, *args, scratch=(), smem=0, hbm=(), cost=1.0):
@@ -560,10 +564,6 @@
     return swap(value, "phi", lambda index: index - 1 if index % 2 == 0 else index + 1)
 
 
-def by_chips(value, bit):
-    return swap(value, "phi", lambda index: index ^ bit if index % 2 else index)
-
-
 def layer_parts(value):
     groups = lax.axis_size("layer")
     return [value] + [
@@ -656,46 +656,48 @@
         low, hidden_zero, slab_one, sums_one, sums_zero, message, node_pre_one, node_grad_one, first_sums, count, cot,
         edge_second, first_back, node_first_back, node_second_back, to_hidden, cost=2.0,
     )
-    edge_out, node_out, done = call(
-        output_kernel, [((latent, slots), BF), ((width, latent), BF), ((8, LANES), F32)],
+    edge_out, node_out = call(
+        output_kernel, [((latent, slots), BF), ((width, latent), BF)],
         edge_counts, edges_one, hidden_one, joined_one, node_pre_one, edge_second, node_second, bias,
         scratch=[VM((latent, total_slots), BF)], smem=1, cost=2.0,
     )
-    lanes = -(-(total_width + 2 * rim) // LANES) * LANES
-    total, back = call(
-        functools.partial(last_kernel, rim), [((latent, lanes), BF), per_hit(F32)],
+    half = hidden // 2
+    up = lambda count: -(-count // LANES) * LANES
+    keep, send, back = call(
+        functools.partial(last_kernel, rim),
+        [((half, total_width), F32), ((half, up(total_width + 4 * rim)), BF), per_hit(F32)],
         back, back_node, beta, alpha, alpha_pick, beta_pick, joined_zero, node_pre_zero, node_hidden_zero, wanted,
         sums_zero, count, extra, slope, onehot, edges_zero, slab_zero, rims_zero, slab_one, total,
         first_back, node_first_back, to_node_back, to_table_back,
         scratch=[VM((hidden, total_slots), BF)], cost=2.0,
     )
-    payload = ((latent, lanes), BF)
-    rim_block = ((latent, rim), F32)
-    first = by_alpha(total)
-    mine = call(functools.partial(open_kernel, total_width, rim), [payload], total, first, cost=0.1)[0]
-    other = by_chips(mine, 2)
+    first = by_alpha(send)
+    width_now = up(total_width + 2 * rim)
+    mine = call(
+        functools.partial(open_kernel, rim), [((half, width_now), BF)], keep, first, cost=0.1,
+    )[0]
+    other = swap(mine, "phi", lambda index: index ^ 2)
     mine, near = call(
-        functools.partial(pass_kernel, total_width, rim), [payload, rim_block], mine, other, cost=0.1,
-    )
-    far = []
-    bit = 4
-    while 2 * bit < ring:
-        other = by_chips(mine, bit)
-        mine, block = call(
-            functools.partial(add_kernel, total_width, rim, bit), [payload, rim_block], mine, other, cost=0.1,
-        )
-        far.append(block)
-        bit *= 2
-    other = by_chips(mine, bit)
-    mine, down = call(
-        functools.partial(close_kernel, total_width, rim), [payload, rim_block], mine, other, near, done, *far, cost=0.1,
-    )
-    sent = by_alpha(mine)
-    node_grad, edge_one, edge_two, node_one, node_two, bias_out = call(
-        functools.partial(finish_kernel, total_width, rim),
-        [((width, latent), F32), (edge_first.shape, F32), (edge_second.shape, F32),
-         (node_first.shape, F32), (node_second.shape, F32), (biases.shape, F32)],
-        mine, sent, down, first, back, upper, lower,
+        functools.partial(pass_kernel, total_width, rim),
+        [((ring // 4 * half, width_now), BF), ((half, 2 * rim), F32)], mine, other, cost=0.1,
+    )
+    count = ring // 4
+    lines = [[place + 4 * rank for rank in range(count)] for place in range(4)]
+    every = lax.all_to_all(mine, "phi", 0, 0, axis_index_groups=lines, tiled=True)
+    mine, beta = call(
+        functools.partial(close_kernel, total_width, rim, count),
+        [((half, width_now), F32), ((half, 2 * rim), F32)], every, near, cost=0.1,
+    )
+    whole = by_alpha(mine)
+    node_grad = call(
+        functools.partial(node_kernel, total_width, rim), [((width, latent), F32)],
+        first, beta, back, upper, lower, cost=1.0,
+    )[0]
+    edge_one, edge_two, node_one, node_two, bias_out = call(
+        functools.partial(finish_kernel, total_width),
+        [(edge_first.shape, F32), (edge_second.shape, F32), (node_first.shape, F32), (node_second.shape, F32),
+         (biases.shape, F32)],
+        mine, whole,
     )
     return node_out.T, edge_out, node_grad.T, edge_one, edge_two, node_one, node_two, bias_out
 

time: 51.3 us -> 48.5 us (0.945)
  starting transfers between devices: 27.7 us -> 15.6 us
  waiting for transfers between devices: 8.77 us -> 16.8 us
  Pallas kernels: 13.2 us -> 14.4 us
    ppermute x13 -> x11, starting transfers between devices: 27.7 us -> 12.3 us  [swap(): lax.ppermute(value, axis, [(source, pairing(source) % count) for source i...]
    all_to_all x0 -> x1, waiting for transfers between devices: none -> 4.8 us  [body(): lax.all_to_all(mine, 'phi', 0, 0, axis_index_groups=lines, tiled=True)]
    all_to_all x0 -> x1, starting transfers between devices: none -> 3.32 us  [body(): lax.all_to_all(mine, 'phi', 0, 0, axis_index_groups=lines, tiled=True)]
    ppermute x13 -> x11, waiting for transfers between devices: 8.77 us -> 12 us  [swap(): lax.ppermute(value, axis, [(source, pairing(source) % count) for source i...]
    pallas_call x16, Pallas kernels: 13.2 us -> 14.4 us  [call(): pl.pallas_call(kernel, out_shape=[jax.ShapeDtypeStruct(shape, kind) for s...]
  transfers between devices with their start and end apart: 13 -> 12, of which waited for: 6 -> 8; matrix products, arithmetic and copies ran while one was open for 0% -> 0% of each run, Pallas kernels for 11% -> 14%
where the time goes in v5:
time: 48.5 us; the launch traced here: 48.2 us
  waiting for transfers between devices  16.8 us (35%)
  starting transfers between devices  15.6 us (32%)
  Pallas kernels  14.4 us (30%)
  between operations  1.43 us (3%)
    pallas_call x16, Pallas kernels, call(): pl.pallas_call(kernel, out_shape=[jax.ShapeDtypeStruct(shape, kind) for s...  14.4 us
    ppermute x11, starting transfers between devices, swap(): lax.ppermute(value, axis, [(source, pairing(source) % count) for source i...  12.3 us
    ppermute x11, waiting for transfers between devices, swap(): lax.ppermute(value, axis, [(source, pairing(source) % count) for source i...  12 us
    all_to_all x1, waiting for transfers between devices, body(): lax.all_to_all(mine, 'phi', 0, 0, axis_index_groups=lines, tiled=True)  4.8 us
    all_to_all x1, starting transfers between devices, body(): lax.all_to_all(mine, 'phi', 0, 0, axis_index_groups=lines, tiled=True)  3.32 us
  transfers between devices with their start and end apart: 12, of which 8 were waited for; matrix products, arithmetic and copies ran while one was open for 0% of the time, Pallas kernels for 14%

profile of v5, /device:TPU:0, one launch (start us, length us, event | category | flops | bytes accessed | tf_op | source)
XLA Modules:
  0.0 48.2 jit_solution(12670136850851358627)
XLA Ops:
  1.3 0.0 copy-start
  1.3 0.9 %shard_map.188 = (bf16[80,128]{1,0:T(8,128)(2,1)S(1)}, s32[1,24]{1,0:T(1,128)S(1)}, s32[1,24]{1,0:T(1,128)S(1)}) custom-call(s32[1,1]{1,0:T(1,128)S(6)} %copy.21.count_ref, s32[16,128]{1,0:T(8,128)} %bitcast.10, s32[16,128]{1,0:T(8,128)} %bitcast.11, bf16[32,64]{1,0:T(8,128)(2,1)} %bitcast.12, f32[32,64]{1,0:T(8,128)} %bitcast.9, s32[1,24]{1,0:T(1,128)} %upper_hbm.1, ...), custom_call_target="tpu_custom_call" | custom-call | flops 1000000000 | bytes 3600000 | tf_op jit(solution)/shard_map/pallas_call | solution.py:541
  2.2 3.0 %collective-permute-start.1 = (bf16[80,128]{1,0:T(8,128)(2,1)S(1)}, bf16[80,128]{1,0:T(8,128)(2,1)S(1)}, u32[]{:S(2)}, u32[]{:S(2)}) collective-permute-start(bf16[80,128]{1,0:T(8,128)(2,1)S(1)} %get-tuple-element.81.packed_ref.refs_0_), channel_id=1, source_target_pairs={{0,1},{1,0},{2,3},{3,2},{4,5},{5,4},{6,7},{7,6},{8,9},{9,8},{10,11... | collective-permute-start | bytes 61448 | tf_op jit(solution)/shard_map/ppermute | solution.py:556
  5.2 0.1 shard_map.189
  5.3 0.0 copy-done
  5.3 0.1 collective-permute-start
  5.4 1.6 %collective-permute-done.1.refs_1_ = bf16[80,128]{1,0:T(8,128)(2,1)S(1)} collective-permute-done((bf16[80,128]{1,0:T(8,128)(2,1)S(1)}, bf16[80,128]{1,0:T(8,128)(2,1)S(1)}, u32[]{:S(2)}, u32[]{:S(2)}) %collective-permute-start.1) | collective-permute-done | bytes 20512 | tf_op jit(solution)/shard_map/ppermute | solution.py:556
  7.0 0.0 copy-start.5
  7.0 0.2 shard_map.190
  7.2 3.4 %collective-permute-start.2 = (bf16[64,64]{1,0:T(8,128)(2,1)S(1)}, bf16[64,64]{1,0:T(8,128)(2,1)S(1)}, u32[]{:S(2)}, u32[]{:S(2)}) collective-permute-start(bf16[64,64]{1,0:T(8,128)(2,1)S(1)} %get-tuple-element.94), channel_id=1, source_target_pairs={{0,30},{2,4},{4,2},{6,8},{8,6},{10,12},{12,10},{14,16},{16,14},{18... | collective-permute-start | bytes 24584 | tf_op jit(solution)/shard_map/ppermute | solution.py:556
  10.6 0.0 collective-permute-start.3
  10.6 0.0 copy-done.1
  10.6 0.0 copy-done.2
  10.6 0.0 copy-done.3
  10.6 0.0 copy-done.4
  10.7 0.0 copy-done.5
  10.7 1.6 %shard_map.191 = (bf16[192,4096]{1,0:T(8,128)(2,1)S(1)}, f32[64,4096]{1,0:T(8,128)S(1)}, f32[8,64]{1,0:T(8,128)S(1)}, f32[64,64]{1,0:T(8,128)S(1)}, bf16[192,64]...) custom-call(bf16[80,128]{1,0:T(8,128)(2,1)S(1)} %get-tuple-element.8, ...), custom_call_target="tpu_custom_call" | custom-call | flops 2000000000 | bytes 7200000 | tf_op jit(solution)/shard_map/pallas_call | solution.py:541
  12.3 0.9 %collective-permute-done.refs_1_ = bf16[64,2048]{1,0:T(8,128)(2,1)S(1)} collective-permute-done((bf16[64,2048]{1,0:T(8,128)(2,1)S(1)}, bf16[64,2048]{1,0:T(8,128)(2,1)S(1)}, u32[]{:S(2)}, u32[]{:S(2)}) %collective-permute-start) | collective-permute-done | bytes 262176 | tf_op jit(solution)/shard_map/ppermute | solution.py:556
  13.2 0.6 %shard_map.192 = (bf16[64,4096]{1,0:T(8,128)(2,1)S(1)}, f32[64,4096]{1,0:T(8,128)S(1)}, f32[64,64]{1,0:T(8,128)S(1)}, f32[64,64]{1,0:T(8,128)S(1)}) custom-call(bf16[64,2048]{1,0:T(8,128)(2,1)S(1)} %copy-done, bf16[64,2048]{1,0:T(8,128)(2,1)S(1)} %collective-permute-done.refs_1_, f32[64,4096]{1,0:T(8,128)S(1)} %get-tuple-element.88.refs_2_, ...), custom_call_target="tpu_custom_call" | custom-call | flops 1000000000 | bytes 3600000 | tf_op jit(solution)/shard_map/pallas_call | solution.py:541
  13.7 0.0 collective-permute-done.2.beta_in
  13.8 0.0 collective-permute-done.3.alpha_in
  13.8 1.4 %shard_map.193 = (bf16[64,4096]{1,0:T(8,128)(2,1)S(1)}, f32[64,4096]{1,0:T(8,128)S(1)}, bf16[64,64]{1,0:T(8,128)(2,1)S(1)}, f32[64,64]{1,0:T(8,128)S(1)}, f32[64...) custom-call(f32[64,4096]{1,0:T(8,128)S(1)} %get-tuple-element.93.bas, ...), custom_call_target="tpu_custom_call" | custom-call | flops 2000000000 | bytes 7200000 | tf_op jit(solution)/shard_map/pallas_call | solution.py:541
  15.2 2.9 %collective-permute-start.4 = (bf16[64,128]{1,0:T(8,128)(2,1)S(1)}, bf16[64,128]{1,0:T(8,128)(2,1)S(1)}, u32[]{:S(2)}, u32[]{:S(2)}) collective-permute-start(bf16[64,128]{1,0:T(8,128)(2,1)S(1)} %get-tuple-element.109), channel_id=1, source_target_pairs={{0,30},{2,4},{4,2},{6,8},{8,6},{10,12},{12,10},{14,16},{16,14},{18... | collective-permute-start | bytes 49160 | tf_op jit(solution)/shard_map/ppermute | solution.py:556
  18.1 0.0 collective-permute-start.5
  18.1 1.1 %shard_map.194 = (bf16[64,4096]{1,0:T(8,128)(2,1)S(1)}, f32[64,4096]{1,0:T(8,128)S(1)}, f32[64,64]{1,0:T(8,128)S(1)}, bf16[128,64]{1,0:T(8,128)(2,1)S(1)}, f32[64,64]{1,0:T(8,128)S(1)}) custom-call(bf16[64,4096]{1,0:T(8,128)(2,1)S(1)} %get-tuple-element.92.edges_ref, bf16[64,4096]{1,0:T(8,128)(2,1)S(1)} %get-tuple-element.102.hidden_ref.hidden_zero_ref, ...), custom_call_target="tpu_custom_call" | custom-call | flops 2000000000 | bytes 7200000 | tf_op jit(solution)/shard_map/pallas_call | solution.py:541
  19.2 1.9 %collective-permute-done.4.beta_in = bf16[64,128]{1,0:T(8,128)(2,1)S(1)} collective-permute-done((bf16[64,128]{1,0:T(8,128)(2,1)S(1)}, bf16[64,128]{1,0:T(8,128)(2,1)S(1)}, u32[]{:S(2)}, u32[]{:S(2)}) %collective-permute-start.4) | collective-permute-done | bytes 16416 | tf_op jit(solution)/shard_map/ppermute | solution.py:556
  21.1 0.0 collective-permute-done.5.alpha_in
  21.1 2.0 %shard_map.195 = (bf16[64,4096]{1,0:T(8,128)(2,1)S(1)}, bf16[64,4096]{1,0:T(8,128)(2,1)S(1)}, f32[64,64]{1,0:T(8,128)S(1)}, f32[64,64]{1,0:T(8,128)S(1)}, f32[64...) custom-call(f32[64,4096]{1,0:T(8,128)S(1)} %get-tuple-element.108.base_ref, ...), custom_call_target="tpu_custom_call" | custom-call | flops 3000000000 | bytes 10800000 | tf_op jit(solution)/shard_map/pallas_call | solution.py:541
  23.2 2.8 %collective-permute-start.6 = (bf16[64,64]{1,0:T(8,128)(2,1)S(1)}, bf16[64,64]{1,0:T(8,128)(2,1)S(1)}, u32[]{:S(2)}, u32[]{:S(2)}) collective-permute-start(bf16[64,64]{1,0:T(8,128)(2,1)S(1)} %get-tuple-element.130), channel_id=1, source_target_pairs={{0,30},{2,4},{4,2},{6,8},{8,6},{10,12},{12,10},{14,16},{16,14},{18... | collective-permute-start | bytes 24584 | tf_op jit(solution)/shard_map/ppermute | solution.py:556
  26.0 0.0 collective-permute-start.7
  26.0 0.9 %shard_map.196 = (f32[64,4096]{1,0:T(8,128)S(1)}, f32[64,452]{1,0:T(8,128)S(1)}, bf16[128,64]{1,0:T(8,128)(2,1)S(1)}, f32[64,64]{1,0:T(8,128)S(1)}, f32[64,64]{1,0:T(8,128)S(1)}) custom-call(bf16[64,4096]{1,0:T(8,128)(2,1)S(1)} %get-tuple-element.116.low_ref, bf16[64,4096]{1,0:T(8,128)(2,1)S(1)} %get-tuple-element.102.hidden_ref.hidden_zero_ref, ...), custom_call_target="tpu_custom_call" | custom-call | flops 2000000000 | bytes 7200000 | tf_op jit(solution)/shard_map/pallas_call | solution.py:541
  26.9 2.2 %collective-permute-done.6.beta_in = bf16[64,64]{1,0:T(8,128)(2,1)S(1)} collective-permute-done((bf16[64,64]{1,0:T(8,128)(2,1)S(1)}, bf16[64,64]{1,0:T(8,128)(2,1)S(1)}, u32[]{:S(2)}, u32[]{:S(2)}) %collective-permute-start.6) | collective-permute-done | bytes 8224 | tf_op jit(solution)/shard_map/ppermute | solution.py:556
  29.1 0.0 collective-permute-done.7.alpha_in
  29.1 1.9 %shard_map.198 = (f32[32,452]{1,0:T(8,128)S(1)}, bf16[32,640]{1,0:T(8,128)(2,1)S(1)}, f32[64,64]{1,0:T(8,128)S(1)}) custom-call(f32[64,64]{1,0:T(8,128)S(1)} %get-tuple-element.128.back_in, f32[64,64]{1,0:T(8,128)S(1)} %get-tuple-element.129.back_node, bf16[64,64]{1,0:T(8,128)(2,1)S(1)} %collective-permute-done.6.beta_in, ...), custom_call_target="tpu_custom_call" | custom-call | flops 2000000000 | bytes 7200000 | tf_op jit(solution)/shard_map/pallas_call | solution.py:541
  31.0 0.1 collective-permute-start.8
  31.1 1.2 %collective-permute-done.8.other_ref.first_ref = bf16[32,640]{1,0:T(8,128)(2,1)S(1)} collective-permute-done((bf16[32,640]{1,0:T(8,128)(2,1)S(1)}, bf16[32,640]{1,0:T(8,128)(2,1)S(1)}, u32[]{:S(2)}, u32[]{:S(2)}) %collective-permute-start.8) | collective-permute-done | bytes 40992 | tf_op jit(solution)/shard_map/ppermute | solution.py:556
  32.3 0.1 shard_map.199.mine_ref
  32.4 0.0 collective-permute-start.9
  32.4 3.9 %collective-permute-done.9.other_ref = bf16[32,512]{1,0:T(8,128)(2,1)S(1)} collective-permute-done((bf16[32,512]{1,0:T(8,128)(2,1)S(1)}, bf16[32,512]{1,0:T(8,128)(2,1)S(1)}, u32[]{:S(2)}, u32[]{:S(2)}) %collective-permute-start.9) | collective-permute-done | bytes 32800 | tf_op jit(solution)/shard_map/ppermute | solution.py:556
  36.3 0.7 %shard_map.200 = (bf16[128,512]{1,0:T(8,128)(2,1)}, f32[32,48]{1,0:T(8,128)S(1)}) custom-call(bf16[32,512]{1,0:T(8,128)(2,1)S(1)} %shard_map.199.mine_ref, bf16[32,512]{1,0:T(8,128)(2,1)S(1)} %collective-permute-done.9.other_ref), custom_call_target="tpu_custom_call" | custom-call | flops 100000000 | bytes 360000 | tf_op jit(solution)/shard_map/pallas_call | solution.py:541
  37.0 3.3 %all-to-all-start = ((bf16[4,32,512]{2,1,0:T(8,128)(2,1)}), bf16[4,32,512]{2,1,0:T(8,128)(2,1)S(1)}, u32[]{:S(2)}, u32[]{:S(2)}) async-start(bf16[4,32,512]{2,1,0:T(8,128)(2,1)} %bitcast.5), calls=%async_computation | async-start | bytes 262144 | tf_op jit(solution)/shard_map/all_to_all | solution.py:686
  40.3 1.1 %shard_map.197 = (bf16[64,2048]{1,0:T(8,128)(2,1)}, bf16[32,64]{1,0:T(8,128)(2,1)}) custom-call(s32[1,1]{1,0:T(1,128)S(6)} %copy.21.count_ref, bf16[64,4096]{1,0:T(8,128)(2,1)S(1)} %get-tuple-element.107.edges_ref, bf16[64,4096]{1,0:T(8,128)(2,1)S(1)} %get-tuple-element.115.hidden_ref, bf16[128,64]{1,0:T(8,128)(2,1)S(1)} %get-tuple-element.125.joined_ref, ...), custom_call_target="tpu_custom_call" | custom-call | flops 2000000000 | bytes 7200000 | tf_op jit(solution)/shard_map/pallas_call | solution.py:541
  41.4 4.8 %all-to-all-done = bf16[4,32,512]{2,1,0:T(8,128)(2,1)S(1)} async-done(((bf16[4,32,512]{2,1,0:T(8,128)(2,1)}), bf16[4,32,512]{2,1,0:T(8,128)(2,1)S(1)}, u32[]{:S(2)}, u32[]{:S(2)}) %all-to-all-start) | async-done | bytes 131104 | tf_op jit(solution)/shard_map/all_to_all | solution.py:686
  46.2 0.1 shard_map.201
  46.3 0.0 collective-permute-start.10
  46.3 1.0 %shard_map.202 = f32[32,64]{1,0:T(8,128)} custom-call(bf16[32,640]{1,0:T(8,128)(2,1)S(1)} %collective-permute-done.8.other_ref.first_ref, f32[32,48]{1,0:T(8,128)S(1)} %get-tuple-element.144.beta_ref, f32[64,64]{1,0:T(8,128)S(1)} %get-tuple-element.145.back_ref, bf16[64,24]{1,0:T(8,128)(2,1)S(1)} %get-tuple-element.146.upper_ref, ...), custom_call_target="tpu_custom_call" | custom-call | flops 1000000000 | bytes 3600000 | tf_op jit(solution)/shard_map/pallas_call | solution.py:541
  47.3 0.2 collective-permute-done.10.other_ref
  47.5 0.7 %shard_map.203 = (f32[64,192]{1,0:T(8,128)}, f32[64,64]{1,0:T(8,128)}, f32[64,128]{1,0:T(8,128)}, f32[64,64]{1,0:T(8,128)}, f32[4,64]{1,0:T(4,128)}) custom-call(f32[32,512]{1,0:T(8,128)S(1)} %get-tuple-element.148.half_ref, f32[32,512]{1,0:T(8,128)S(1)} %collective-permute-done.10.other_ref), custom_call_target="tpu_custom_call" | custom-call | flops 1000000000 | bytes 3600000 | tf_op jit(solution)/shard_map/pallas_call | solution.py:541
  (4 shorter events, 0.0 us)
Async XLA Ops:
  1.3 4.0 %copy-start = (bf16[64,2048]{1,0:T(8,128)(2,1)S(1)}, bf16[64,2048]{1,0:T(8,128)(2,1)}, u32[]{:S(2)}) copy-start(bf16[64,2048]{1,0:T(8,128)(2,1)} %refs_0_.1) | copy-start | bytes 786436
  2.2 4.8 %collective-permute-start.1 = (bf16[80,128]{1,0:T(8,128)(2,1)S(1)}, bf16[80,128]{1,0:T(8,128)(2,1)S(1)}, u32[]{:S(2)}, u32[]{:S(2)}) collective-permute-start(bf16[80,128]{1,0:T(8,128)(2,1)S(1)} %get-tuple-element.81.packed_ref.refs_0_), channel_id=1, source_target_pairs={{0,1},{1,0},{2,3},{3,2},{4,5},{5,4},{6,7},{7,6},{8,9},{9,8},{10,11... | collective-permute-start | bytes 61448 | tf_op jit(solution)/shard_map/ppermute | solution.py:556
  5.3 7.8 %collective-permute-start = (bf16[64,2048]{1,0:T(8,128)(2,1)S(1)}, bf16[64,2048]{1,0:T(8,128)(2,1)S(1)}, u32[]{:S(2)}, u32[]{:S(2)}) collective-permute-start(bf16[64,2048]{1,0:T(8,128)(2,1)S(1)} %copy-done), channel_id=1, source_target_pairs={{0,1},{1,0},{2,3},{3,2},{4,5},{5,4},{6,7},{7,6},{8,9},{9,8},{10,11... | collective-permute-start | bytes 786440 | tf_op jit(solution)/shard_map/ppermute | solution.py:556
  7.0 3.6 %copy-start.1 = (bf16[64,192]{1,0:T(8,128)(2,1)S(1)}, bf16[64,192]{1,0:T(8,128)(2,1)}, u32[]{:S(2)}) copy-start(bf16[64,192]{1,0:T(8,128)(2,1)} %first_ref.3) | copy-start | bytes 73732
  7.0 3.6 %copy-start.2 = (bf16[64,128]{1,0:T(8,128)(2,1)S(1)}, bf16[64,128]{1,0:T(8,128)(2,1)}, u32[]{:S(2)}) copy-start(bf16[64,128]{1,0:T(8,128)(2,1)} %node_first_ref.1) | copy-start | bytes 49156
  7.0 3.6 %copy-start.3 = (bf16[64,64]{1,0:T(8,128)(2,1)S(1)}, bf16[64,64]{1,0:T(8,128)(2,1)}, u32[]{:S(2)}) copy-start(bf16[64,64]{1,0:T(8,128)(2,1)} %second_ref.5) | copy-start | bytes 24580
  7.0 3.6 %copy-start.4 = (bf16[64,64]{1,0:T(8,128)(2,1)S(1)}, bf16[64,64]{1,0:T(8,128)(2,1)}, u32[]{:S(2)}) copy-start(bf16[64,64]{1,0:T(8,128)(2,1)} %node_second_ref.3) | copy-start | bytes 24580
  7.0 3.6 %copy-start.5 = (f32[4,64]{1,0:T(4,128)S(1)}, f32[4,64]{1,0:T(4,128)}, u32[]{:S(2)}) copy-start(f32[4,64]{1,0:T(4,128)} %refs_7_.2) | copy-start | bytes 3076
  7.2 6.5 %collective-permute-start.2 = (bf16[64,64]{1,0:T(8,128)(2,1)S(1)}, bf16[64,64]{1,0:T(8,128)(2,1)S(1)}, u32[]{:S(2)}, u32[]{:S(2)}) collective-permute-start(bf16[64,64]{1,0:T(8,128)(2,1)S(1)} %get-tuple-element.94), channel_id=1, source_target_pairs={{0,30},{2,4},{4,2},{6,8},{8,6},{10,12},{12,10},{14,16},{16,14},{18... | collective-permute-start | bytes 24584 | tf_op jit(solution)/shard_map/ppermute | solution.py:556
  10.6 3.1 %collective-permute-start.3 = (bf16[64,64]{1,0:T(8,128)(2,1)S(1)}, bf16[64,64]{1,0:T(8,128)(2,1)S(1)}, u32[]{:S(2)}, u32[]{:S(2)}) collective-permute-start(bf16[64,64]{1,0:T(8,128)(2,1)S(1)} %get-tuple-element.95), channel_id=1, source_target_pairs={{0,2},{2,0},{4,6},{6,4},{8,10},{10,8},{12,14},{14,12},{16,18},{18,... | collective-permute-start | bytes 24584 | tf_op jit(solution)/shard_map/ppermute | solution.py:556
  15.2 5.9 %collective-permute-start.4 = (bf16[64,128]{1,0:T(8,128)(2,1)S(1)}, bf16[64,128]{1,0:T(8,128)(2,1)S(1)}, u32[]{:S(2)}, u32[]{:S(2)}) collective-permute-start(bf16[64,128]{1,0:T(8,128)(2,1)S(1)} %get-tuple-element.109), channel_id=1, source_target_pairs={{0,30},{2,4},{4,2},{6,8},{8,6},{10,12},{12,10},{14,16},{16,14},{18... | collective-permute-start | bytes 49160 | tf_op jit(solution)/shard_map/ppermute | solution.py:556
  18.1 3.1 %collective-permute-start.5 = (bf16[64,128]{1,0:T(8,128)(2,1)S(1)}, bf16[64,128]{1,0:T(8,128)(2,1)S(1)}, u32[]{:S(2)}, u32[]{:S(2)}) collective-permute-start(bf16[64,128]{1,0:T(8,128)(2,1)S(1)} %get-tuple-element.110), channel_id=1, source_target_pairs={{0,2},{2,0},{4,6},{6,4},{8,10},{10,8},{12,14},{14,12},{16,18},{18,... | collective-permute-start | bytes 49160 | tf_op jit(solution)/shard_map/ppermute | solution.py:556
  23.2 5.9 %collective-permute-start.6 = (bf16[64,64]{1,0:T(8,128)(2,1)S(1)}, bf16[64,64]{1,0:T(8,128)(2,1)S(1)}, u32[]{:S(2)}, u32[]{:S(2)}) collective-permute-start(bf16[64,64]{1,0:T(8,128)(2,1)S(1)} %get-tuple-element.130), channel_id=1, source_target_pairs={{0,30},{2,4},{4,2},{6,8},{8,6},{10,12},{12,10},{14,16},{16,14},{18... | collective-permute-start | bytes 24584 | tf_op jit(solution)/shard_map/ppermute | solution.py:556
  26.0 3.1 %collective-permute-start.7 = (bf16[64,64]{1,0:T(8,128)(2,1)S(1)}, bf16[64,64]{1,0:T(8,128)(2,1)S(1)}, u32[]{:S(2)}, u32[]{:S(2)}) collective-permute-start(bf16[64,64]{1,0:T(8,128)(2,1)S(1)} %get-tuple-element.130), channel_id=1, source_target_pairs={{0,2},{2,0},{4,6},{6,4},{8,10},{10,8},{12,14},{14,12},{16,18},{18,... | collective-permute-start | bytes 24584 | tf_op jit(solution)/shard_map/ppermute | solution.py:556
  31.0 1.3 %collective-permute-start.8 = (bf16[32,640]{1,0:T(8,128)(2,1)S(1)}, bf16[32,640]{1,0:T(8,128)(2,1)S(1)}, u32[]{:S(2)}, u32[]{:S(2)}) collective-permute-start(bf16[32,640]{1,0:T(8,128)(2,1)S(1)} %get-tuple-element.140), channel_id=1, source_target_pairs={{0,2},{2,0},{4,6},{6,4},{8,10},{10,8},{12,14},{14,12},{16,18},{18,... | collective-permute-start | bytes 122888 | tf_op jit(solution)/shard_map/ppermute | solution.py:556
  32.4 3.9 %collective-permute-start.9 = (bf16[32,512]{1,0:T(8,128)(2,1)S(1)}, bf16[32,512]{1,0:T(8,128)(2,1)S(1)}, u32[]{:S(2)}, u32[]{:S(2)}) collective-permute-start(bf16[32,512]{1,0:T(8,128)(2,1)S(1)} %shard_map.199.mine_ref), channel_id=1, source_target_pairs={{0,4},{2,6},{4,0},{6,2},{8,12},{10,14},{12,8},{14,10},{16,20},{18,... | collective-permute-start | bytes 98312 | tf_op jit(solution)/shard_map/ppermute | solution.py:556
  37.0 9.2 %all-to-all-start = ((bf16[4,32,512]{2,1,0:T(8,128)(2,1)}), bf16[4,32,512]{2,1,0:T(8,128)(2,1)S(1)}, u32[]{:S(2)}, u32[]{:S(2)}) async-start(bf16[4,32,512]{2,1,0:T(8,128)(2,1)} %bitcast.5), calls=%async_computation | async-start | bytes 262144 | tf_op jit(solution)/shard_map/all_to_all | solution.py:686
  46.3 1.3 %collective-permute-start.10 = (f32[32,512]{1,0:T(8,128)S(1)}, f32[32,512]{1,0:T(8,128)S(1)}, u32[]{:S(2)}, u32[]{:S(2)}) collective-permute-start(f32[32,512]{1,0:T(8,128)S(1)} %get-tuple-element.148.half_ref), channel_id=1, source_target_pairs={{0,2},{2,0},{4,6},{6,4},{8,10},{10,8},{12,14},{14,12},{16,18},{18,... | collective-permute-start | bytes 196616 | tf_op jit(solution)/shard_map/ppermute | solution.py:556

commit v6 on v5

--- a/solution.py
+++ b/solution.py
@@ -109,11 +109,11 @@
     wide = onehot_ref.shape[0] - slab
     for cols in chunks_of(base_ref.shape[1]):
         rims = onehot_ref[slab:wide, cols]
-        pre = base_ref[:, cols] + mm(table, jnp.concatenate([rims, rims], axis=0))
+        pre = base_ref[:, cols].astype(F32) + mm(table, jnp.concatenate([rims, rims], axis=0))
         value, slope = slope_parts(pre)
         hidden = value.astype(BF)
         hidden_ref[:, cols] = hidden
-        slope_ref[:, cols] = slope
+        slope_ref[:, cols] = slope.astype(BF)
     return mm_nt(hidden_ref[...], onehot_ref[wide:])
 
 
@@ -125,7 +125,7 @@
         near = onehot_ref[:slab, cols]
         hit = onehot_ref[wide:, cols]
         stack = jnp.concatenate([near, near, hit, hit, edges_ref[:, cols]], axis=0)
-        base_ref[:, cols] = mm(table, stack) + bias[:, 0:1]
+        base_ref[:, cols] = (mm(table, stack) + bias[:, 0:1]).astype(BF)
 
 
 def node_base(state16, message, first_ref, bias):
@@ -263,7 +263,7 @@
             here = slice(rank * slots + cols.start, rank * slots + cols.stop)
             edges = pick([part[:, cols] for part in parts], rank)
             edges_ref[:, here] = edges
-            base_ref[:, here] = base_in[:, here] + mm(own, edges)
+            base_ref[:, here] = (base_in[:, here] + mm(own, edges)).astype(BF)
             message = add_to(message, mm_nt(edges, onehot_ref[wide:, here]))
     bias = bias_ref[...]
     message = message + bias[:, 1:2] * count_ref[0:1]
@@ -322,8 +322,8 @@
         hit = onehot_ref[wide:, cols]
         grad = mm(table, jnp.concatenate([hit, hit], axis=0))
         if extra_ref is not None:
-            grad = grad + extra_ref[:, cols]
-        low_ref[:, cols] = (grad * slope_ref[:, cols]).astype(BF)
+            grad = grad + extra_ref[:, cols].astype(F32)
+        low_ref[:, cols] = (grad * slope_ref[:, cols].astype(F32)).astype(BF)
     return mm_nt(low_ref[...], jnp.concatenate([onehot_ref[...], edges_ref[...]], axis=0))
 
 
@@ -367,7 +367,7 @@
     cross = None
     for cols in chunks_of(low_ref.shape[1]):
         low = low_ref[:, cols]
-        extra_ref[:, cols] = pair_mm(to_hidden[...], low)
+        extra_ref[:, cols] = pair_mm(to_hidden[...], low).astype(BF)
         cross = add_to(cross, mm_nt(low, hidden_zero_ref[:, cols]))
     slab16 = slab_ref[...]
     message = message_in[...] + wide_mm(second_ref[...], sums_ref[...])
@@ -470,55 +470,44 @@
     out_ref[...] = jnp.concatenate(pieces, axis=1).astype(BF)
 
 
-def pass_kernel(used, rim, mine_ref, other_ref, out_ref, near_ref):
+def add_kernel(used, rim, bit, mine_ref, other_ref, arrived_in, out_ref, arrived_ref):
     other = other_ref[...].astype(F32)
-    total = mine_ref[...].astype(F32)[:, :used] + other[:, :used]
     place = lax.axis_index("phi")
-    home = (lax.rem(place // 2, 2) == 1) == (lax.rem(place, 2) == 0)
+    home = (lax.rem(place // bit, 2) == 1) == (lax.rem(place, 2) == 0)
     held = other[:, used : used + 2 * rim]
-    near_ref[...] = jnp.where(home, held, 0.0)
-    pieces = [total, jnp.where(home, 0.0, held)]
-    spare = out_ref.shape[1] - used - 2 * rim
-    if spare:
-        pieces.append(jnp.zeros((total.shape[0], spare), F32))
-    block = jnp.concatenate(pieces, axis=1).astype(BF)
-    half = block.shape[0]
-    for first in range(0, out_ref.shape[0], half):
-        out_ref[first : first + half] = block
-
-
-def close_kernel(used, rim, count, all_ref, near_ref, half_ref, beta_ref):
-    half = half_ref.shape[0]
-    blocks = [all_ref[rank * half : (rank + 1) * half].astype(F32) for rank in range(count)]
-    total = blocks[0]
-    for block in blocks[1:]:
-        total = total + block
-    half_ref[...] = total
-    place = lax.axis_index("phi")
-    here = place // 4
-    step = jnp.where(lax.rem(place, 2) == 0, count - 1, 1)
-    source = lax.rem(here + step, count)
-    held = blocks[0]
-    for rank in range(1, count):
-        held = jnp.where(source == rank, blocks[rank], held)
-    beta_ref[...] = near_ref[...] + held[:, used : used + 2 * rim]
+    arrived = jnp.where(home, held, 0.0)
+    if arrived_in is not None:
+        arrived = arrived + arrived_in[...]
+    arrived_ref[...] = arrived
+    lane = lax.broadcasted_iota(jnp.int32, other.shape, 1)
+    mine = mine_ref[...].astype(F32)
+    passing = jnp.where(home, 0.0, other)
+    out_ref[...] = jnp.where(lane < used, mine + other, passing).astype(BF)
+
+
+def first_add(kernel, mine_ref, other_ref, out_ref, arrived_ref):
+    kernel(mine_ref, other_ref, None, out_ref, arrived_ref)
+
+
+def close_kernel(mine_ref, other_ref, half_ref):
+    half_ref[...] = (mine_ref[...].astype(F32) + other_ref[...].astype(F32)).astype(BF)
 
 
 def rims_of(value, used, rim):
     return jnp.concatenate([value[:, used : used + rim], value[:, used + rim : used + 2 * rim]], axis=0)
 
 
-def node_kernel(used, rim, first_ref, beta_ref, back_ref, upper_ref, lower_ref, node_grad):
+def node_kernel(used, rim, first_ref, other_ref, arrived_ref, back_ref, upper_ref, lower_ref, node_grad):
     alpha = rims_of(first_ref[...].astype(F32), used, rim)
-    beta = rims_of(beta_ref[...], 0, rim)
+    beta = rims_of(other_ref[...].astype(F32), used, rim) + rims_of(arrived_ref[...], 0, rim)
     grad = back_ref[...] + placed_rims(alpha, beta, upper_ref, lower_ref)
     node_grad[...] = own_rows(grad.T, node_grad.shape[0])
 
 
 def finish_kernel(used, half_ref, other_ref, edge_one, edge_two, node_one, node_two, bias_out):
     even = is_even()
-    mine = half_ref[...]
-    other = other_ref[...]
+    mine = half_ref[...].astype(F32)
+    other = other_ref[...].astype(F32)
     total = jnp.concatenate([jnp.where(even, mine, other), jnp.where(even, other, mine)], axis=0)
     cut = 0
     for ref in (edge_one, edge_two, node_one, node_two):
@@ -622,13 +611,13 @@
     )
     edges_zero, base, message, node_base_zero = call(
         functools.partial(start_kernel, groups),
-        [per_slot(BF), per_slot(F32), per_hit(F32), per_hit(F32)],
+        [per_slot(BF), per_slot(BF), per_hit(F32), per_hit(F32)],
         *parts, base, onehot, slab_zero, count, edge_first, node_first, bias, cost=1.0,
     )
     (hidden_zero, slope, rims_zero, sums_zero, node_pre_zero, node_hidden_zero, slab_one, table,
      alpha, beta) = call(
         forward_kernel,
-        [per_slot(BF), per_slot(F32), rim_shape, per_hit(F32), per_hit(F32), per_hit(BF), per_hit(BF), per_hit(F32),
+        [per_slot(BF), per_slot(BF), rim_shape, per_hit(F32), per_hit(F32), per_hit(BF), per_hit(BF), per_hit(F32),
          ((latent, 2 * room), BF), ((latent, 2 * room), BF)],
         base, onehot, slab_zero, beta, alpha, node_base_zero, table, edge_first, node_second, bias, to_node, to_table,
         alpha_place, beta_place, cost=2.0,
@@ -636,7 +625,7 @@
     beta = by_beta(beta)
     alpha = by_alpha(alpha)
     edges_one, base, message, joined_zero, node_base_one = call(
-        between_kernel, [per_slot(BF), per_slot(F32), per_hit(F32), per_hit(BF, 2), per_hit(F32)],
+        between_kernel, [per_slot(BF), per_slot(BF), per_hit(F32), per_hit(BF, 2), per_hit(F32)],
         edges_zero, hidden_zero, onehot, slab_zero, slab_one, table, sums_zero, message, count,
         edge_first, edge_second, node_first, bias, cost=2.0,
     )
@@ -646,13 +635,13 @@
         [per_slot(BF), per_slot(BF), per_hit(F32), per_hit(F32), per_hit(F32), per_hit(F32),
          ((hidden, wide + slab + latent), F32), rim_shape],
         base, onehot, edges_one, beta, alpha, node_base_one, cot, node_second_back, to_node, to_node_back,
-        scratch=[VM((hidden, total_slots), F32)], cost=3.0,
+        scratch=[VM((hidden, total_slots), BF)], cost=3.0,
     )
     beta = by_beta(rims)
     alpha = by_alpha(rims)
     extra, total, joined_one, back, back_node = call(
         functools.partial(carry_kernel, rim),
-        [per_slot(F32), ((latent, total_width), F32), per_hit(BF, 2), per_hit(F32), per_hit(F32)],
+        [per_slot(BF), ((latent, total_width), F32), per_hit(BF, 2), per_hit(F32), per_hit(F32)],
         low, hidden_zero, slab_one, sums_one, sums_zero, message, node_pre_one, node_grad_one, first_sums, count, cot,
         edge_second, first_back, node_first_back, node_second_back, to_hidden, cost=2.0,
     )
@@ -676,22 +665,23 @@
     mine = call(
         functools.partial(open_kernel, rim), [((half, width_now), BF)], keep, first, cost=0.1,
     )[0]
-    other = swap(mine, "phi", lambda index: index ^ 2)
-    mine, near = call(
-        functools.partial(pass_kernel, total_width, rim),
-        [((ring // 4 * half, width_now), BF), ((half, 2 * rim), F32)], mine, other, cost=0.1,
-    )
-    count = ring // 4
-    lines = [[place + 4 * rank for rank in range(count)] for place in range(4)]
-    every = lax.all_to_all(mine, "phi", 0, 0, axis_index_groups=lines, tiled=True)
-    mine, beta = call(
-        functools.partial(close_kernel, total_width, rim, count),
-        [((half, width_now), F32), ((half, 2 * rim), F32)], every, near, cost=0.1,
-    )
+    bit = 2
+    arrived = None
+    while True:
+        other = swap(mine, "phi", lambda index, bit=bit: index ^ bit)
+        if 2 * bit >= ring:
+            break
+        given = (mine, other) if arrived is None else (mine, other, arrived)
+        kernel = functools.partial(add_kernel, total_width, rim, bit)
+        if arrived is None:
+            kernel = functools.partial(first_add, kernel)
+        mine, arrived = call(kernel, [((half, width_now), BF), ((half, 2 * rim), F32)], *given, cost=0.1)
+        bit *= 2
+    mine = call(close_kernel, [((half, width_now), BF)], mine, other, cost=0.1)[0]
     whole = by_alpha(mine)
     node_grad = call(
         functools.partial(node_kernel, total_width, rim), [((width, latent), F32)],
-        first, beta, back, upper, lower, cost=1.0,
+        first, other, arrived, back, upper, lower, cost=1.0,
     )[0]
     edge_one, edge_two, node_one, node_two, bias_out = call(
         functools.partial(finish_kernel, total_width),

time: 48.5 us -> 47.6 us (0.981)
  starting transfers between devices: 15.6 us -> 12.4 us
  waiting for transfers between devices: 16.8 us -> 19.5 us
    ppermute x11 -> x13, waiting for transfers between devices: 12 us -> 19.5 us  [swap(): lax.ppermute(value, axis, [(source, pairing(source) % count) for source i...]
    all_to_all x1 -> x0, waiting for transfers between devices: 4.8 us -> none  [body(): lax.all_to_all(mine, 'phi', 0, 0, axis_index_groups=lines, tiled=True)]
    all_to_all x1 -> x0, starting transfers between devices: 3.32 us -> none  [body(): lax.all_to_all(mine, 'phi', 0, 0, axis_index_groups=lines, tiled=True)]
    pallas_call x16 -> x17, Pallas kernels: 14.4 us -> 14.1 us  [call(): pl.pallas_call(kernel, out_shape=[jax.ShapeDtypeStruct(shape, kind) for s...]
    ppermute x11 -> x13, starting transfers between devices: 12.3 us -> 12.4 us  [swap(): lax.ppermute(value, axis, [(source, pairing(source) % count) for source i...]
  transfers between devices with their start and end apart: 12 -> 13, of which waited for: 8 -> 9; matrix products, arithmetic and copies ran while one was open for 0% -> 0% of each run, Pallas kernels for 14% -> 14%
where the time goes in v6:
time: 47.6 us; the launch traced here: 47.4 us
  waiting for transfers between devices  19.5 us (41%)
  Pallas kernels  14.1 us (30%)
  starting transfers between devices  12.4 us (26%)
  between operations  1.44 us (3%)
    ppermute x13, waiting for transfers between devices, swap(): lax.ppermute(value, axis, [(source, pairing(source) % count) for source i...  19.5 us
    pallas_call x17, Pallas kernels, call(): pl.pallas_call(kernel, out_shape=[jax.ShapeDtypeStruct(shape, kind) for s...  14.1 us
    ppermute x13, starting transfers between devices, swap(): lax.ppermute(value, axis, [(source, pairing(source) % count) for source i...  12.4 us
  transfers between devices with their start and end apart: 13, of which 9 were waited for; matrix products, arithmetic and copies ran while one was open for 0% of the time, Pallas kernels for 14%

profile of v6, /device:TPU:0, one launch (start us, length us, event | category | flops | bytes accessed | tf_op | source)
XLA Modules:
  0.0 47.4 jit_solution(9078274619245476190)
XLA Ops:
  1.3 0.0 copy-start
  1.3 0.9 %shard_map.188 = (bf16[80,128]{1,0:T(8,128)(2,1)S(1)}, s32[1,24]{1,0:T(1,128)S(1)}, s32[1,24]{1,0:T(1,128)S(1)}) custom-call(s32[1,1]{1,0:T(1,128)S(6)} %copy.21.count_ref, s32[16,128]{1,0:T(8,128)} %bitcast.7, s32[16,128]{1,0:T(8,128)} %bitcast.8, bf16[32,64]{1,0:T(8,128)(2,1)} %bitcast.9, f32[32,64]{1,0:T(8,128)} %bitcast.6, s32[1,24]{1,0:T(1,128)} %upper_hbm.1, ...), custom_call_target="tpu_custom_call" | custom-call | flops 1000000000 | bytes 3600000 | tf_op jit(solution)/shard_map/pallas_call | solution.py:530
  2.2 3.0 %collective-permute-start.1 = (bf16[80,128]{1,0:T(8,128)(2,1)S(1)}, bf16[80,128]{1,0:T(8,128)(2,1)S(1)}, u32[]{:S(2)}, u32[]{:S(2)}) collective-permute-start(bf16[80,128]{1,0:T(8,128)(2,1)S(1)} %get-tuple-element.81.packed_ref.refs_0_), channel_id=1, source_target_pairs={{0,1},{1,0},{2,3},{3,2},{4,5},{5,4},{6,7},{7,6},{8,9},{9,8},{10,11... | collective-permute-start | bytes 61448 | tf_op jit(solution)/shard_map/ppermute | solution.py:545
  5.2 0.1 shard_map.189
  5.3 0.0 copy-done
  5.3 0.1 collective-permute-start
  5.4 1.6 %collective-permute-done.1.refs_1_ = bf16[80,128]{1,0:T(8,128)(2,1)S(1)} collective-permute-done((bf16[80,128]{1,0:T(8,128)(2,1)S(1)}, bf16[80,128]{1,0:T(8,128)(2,1)S(1)}, u32[]{:S(2)}, u32[]{:S(2)}) %collective-permute-start.1) | collective-permute-done | bytes 20512 | tf_op jit(solution)/shard_map/ppermute | solution.py:545
  7.0 0.0 copy-start.5
  7.0 0.2 shard_map.190
  7.2 3.4 %collective-permute-start.2 = (bf16[64,64]{1,0:T(8,128)(2,1)S(1)}, bf16[64,64]{1,0:T(8,128)(2,1)S(1)}, u32[]{:S(2)}, u32[]{:S(2)}) collective-permute-start(bf16[64,64]{1,0:T(8,128)(2,1)S(1)} %get-tuple-element.94), channel_id=1, source_target_pairs={{0,30},{2,4},{4,2},{6,8},{8,6},{10,12},{12,10},{14,16},{16,14},{18... | collective-permute-start | bytes 24584 | tf_op jit(solution)/shard_map/ppermute | solution.py:545
  10.6 0.0 collective-permute-start.3
  10.6 0.0 copy-done.1
  10.6 0.0 copy-done.2
  10.6 0.0 copy-done.3
  10.7 1.6 %shard_map.191 = (bf16[192,4096]{1,0:T(8,128)(2,1)S(1)}, f32[64,4096]{1,0:T(8,128)S(1)}, f32[8,64]{1,0:T(8,128)S(1)}, f32[64,64]{1,0:T(8,128)S(1)}, bf16[192,64]...) custom-call(bf16[80,128]{1,0:T(8,128)(2,1)S(1)} %get-tuple-element.8, ...), custom_call_target="tpu_custom_call" | custom-call | flops 2000000000 | bytes 7200000 | tf_op jit(solution)/shard_map/pallas_call | solution.py:530
  12.3 0.9 %collective-permute-done.refs_1_ = bf16[64,2048]{1,0:T(8,128)(2,1)S(1)} collective-permute-done((bf16[64,2048]{1,0:T(8,128)(2,1)S(1)}, bf16[64,2048]{1,0:T(8,128)(2,1)S(1)}, u32[]{:S(2)}, u32[]{:S(2)}) %collective-permute-start) | collective-permute-done | bytes 262176 | tf_op jit(solution)/shard_map/ppermute | solution.py:545
  13.2 0.6 %shard_map.192 = (bf16[64,4096]{1,0:T(8,128)(2,1)S(1)}, bf16[64,4096]{1,0:T(8,128)(2,1)S(1)}, f32[64,64]{1,0:T(8,128)S(1)}, f32[64,64]{1,0:T(8,128)S(1)}) custom-call(bf16[64,2048]{1,0:T(8,128)(2,1)S(1)} %copy-done, bf16[64,2048]{1,0:T(8,128)(2,1)S(1)} %collective-permute-done.refs_1_, f32[64,4096]{1,0:T(8,128)S(1)} %get-tuple-element.88.refs_2_, ...), custom_call_target="tpu_custom_call" | custom-call | flops 1000000000 | bytes 3600000 | tf_op jit(solution)/shard_map/pallas_call | solution.py:530
  13.8 0.0 collective-permute-done.2.beta_in
  13.8 0.0 collective-permute-done.3.alpha_in
  13.8 1.4 %shard_map.193 = (bf16[64,4096]{1,0:T(8,128)(2,1)S(1)}, bf16[64,4096]{1,0:T(8,128)(2,1)S(1)}, bf16[64,64]{1,0:T(8,128)(2,1)S(1)}, f32[64,64]{1,0:T(8,128)S(1)}, ...) custom-call(bf16[64,4096]{1,0:T(8,128)(2,1)S(1)} %get-tuple-element., ...), custom_call_target="tpu_custom_call" | custom-call | flops 2000000000 | bytes 7200000 | tf_op jit(solution)/shard_map/pallas_call | solution.py:530
  15.2 2.9 %collective-permute-start.4 = (bf16[64,128]{1,0:T(8,128)(2,1)S(1)}, bf16[64,128]{1,0:T(8,128)(2,1)S(1)}, u32[]{:S(2)}, u32[]{:S(2)}) collective-permute-start(bf16[64,128]{1,0:T(8,128)(2,1)S(1)} %get-tuple-element.109), channel_id=1, source_target_pairs={{0,30},{2,4},{4,2},{6,8},{8,6},{10,12},{12,10},{14,16},{16,14},{18... | collective-permute-start | bytes 49160 | tf_op jit(solution)/shard_map/ppermute | solution.py:545
  18.1 0.0 collective-permute-start.5
  18.1 1.1 %shard_map.194 = (bf16[64,4096]{1,0:T(8,128)(2,1)S(1)}, bf16[64,4096]{1,0:T(8,128)(2,1)S(1)}, f32[64,64]{1,0:T(8,128)S(1)}, bf16[128,64]{1,0:T(8,128)(2,1)S(1)}, f32[64,64]{1,0:T(8,128)S(1)}) custom-call(bf16[64,4096]{1,0:T(8,128)(2,1)S(1)} %get-tuple-element.92.edges_ref, bf16[64,4096]{1,0:T(8,128)(2,1)S(1)} %get-tuple-element.102.hidden_ref.hidden_zero_ref, ...), custom_call_target="tpu_custom_call" | custom-call | flops 2000000000 | bytes 7200000 | tf_op jit(solution)/shard_map/pallas_call | solution.py:530
  19.2 1.9 %collective-permute-done.4.beta_in = bf16[64,128]{1,0:T(8,128)(2,1)S(1)} collective-permute-done((bf16[64,128]{1,0:T(8,128)(2,1)S(1)}, bf16[64,128]{1,0:T(8,128)(2,1)S(1)}, u32[]{:S(2)}, u32[]{:S(2)}) %collective-permute-start.4) | collective-permute-done | bytes 16416 | tf_op jit(solution)/shard_map/ppermute | solution.py:545
  21.1 0.0 collective-permute-done.5.alpha_in
  21.2 2.1 %shard_map.195 = (bf16[64,4096]{1,0:T(8,128)(2,1)S(1)}, bf16[64,4096]{1,0:T(8,128)(2,1)S(1)}, f32[64,64]{1,0:T(8,128)S(1)}, f32[64,64]{1,0:T(8,128)S(1)}, f32[64...) custom-call(bf16[64,4096]{1,0:T(8,128)(2,1)S(1)} %get-tuple-element.108.base_ref, ...), custom_call_target="tpu_custom_call" | custom-call | flops 3000000000 | bytes 10800000 | tf_op jit(solution)/shard_map/pallas_call | solution.py:530
  23.3 2.8 %collective-permute-start.6 = (bf16[64,64]{1,0:T(8,128)(2,1)S(1)}, bf16[64,64]{1,0:T(8,128)(2,1)S(1)}, u32[]{:S(2)}, u32[]{:S(2)}) collective-permute-start(bf16[64,64]{1,0:T(8,128)(2,1)S(1)} %get-tuple-element.130), channel_id=1, source_target_pairs={{0,30},{2,4},{4,2},{6,8},{8,6},{10,12},{12,10},{14,16},{16,14},{18... | collective-permute-start | bytes 24584 | tf_op jit(solution)/shard_map/ppermute | solution.py:545
  26.1 0.0 collective-permute-start.7
  26.1 0.9 %shard_map.196 = (bf16[64,4096]{1,0:T(8,128)(2,1)S(1)}, f32[64,452]{1,0:T(8,128)S(1)}, bf16[128,64]{1,0:T(8,128)(2,1)S(1)}, f32[64,64]{1,0:T(8,128)S(1)}, f32[64,64]{1,0:T(8,128)S(1)}) custom-call(bf16[64,4096]{1,0:T(8,128)(2,1)S(1)} %get-tuple-element.116.low_ref, bf16[64,4096]{1,0:T(8,128)(2,1)S(1)} %get-tuple-element.102.hidden_ref.hidden_zero_ref, ...), custom_call_target="tpu_custom_call" | custom-call | flops 2000000000 | bytes 7200000 | tf_op jit(solution)/shard_map/pallas_call | solution.py:530
  27.0 2.2 %collective-permute-done.6.beta_in = bf16[64,64]{1,0:T(8,128)(2,1)S(1)} collective-permute-done((bf16[64,64]{1,0:T(8,128)(2,1)S(1)}, bf16[64,64]{1,0:T(8,128)(2,1)S(1)}, u32[]{:S(2)}, u32[]{:S(2)}) %collective-permute-start.6) | collective-permute-done | bytes 8224 | tf_op jit(solution)/shard_map/ppermute | solution.py:545
  29.2 0.0 collective-permute-done.7.alpha_in
  29.2 2.0 %shard_map.198 = (f32[32,452]{1,0:T(8,128)S(1)}, bf16[32,640]{1,0:T(8,128)(2,1)S(1)}, f32[64,64]{1,0:T(8,128)S(1)}) custom-call(f32[64,64]{1,0:T(8,128)S(1)} %get-tuple-element.128.back_in, f32[64,64]{1,0:T(8,128)S(1)} %get-tuple-element.129.back_node, bf16[64,64]{1,0:T(8,128)(2,1)S(1)} %collective-permute-done.6.beta_in, ...), custom_call_target="tpu_custom_call" | custom-call | flops 2000000000 | bytes 7200000 | tf_op jit(solution)/shard_map/pallas_call | solution.py:530
  31.2 0.1 collective-permute-start.8
  31.2 1.2 %collective-permute-done.8.other_ref.first_ref = bf16[32,640]{1,0:T(8,128)(2,1)S(1)} collective-permute-done((bf16[32,640]{1,0:T(8,128)(2,1)S(1)}, bf16[32,640]{1,0:T(8,128)(2,1)S(1)}, u32[]{:S(2)}, u32[]{:S(2)}) %collective-permute-start.8) | collective-permute-done | bytes 40992 | tf_op jit(solution)/shard_map/ppermute | solution.py:545
  32.4 0.1 shard_map.199.mine_ref
  32.5 0.0 collective-permute-start.9
  32.5 3.9 %collective-permute-done.9.other_ref = bf16[32,512]{1,0:T(8,128)(2,1)S(1)} collective-permute-done((bf16[32,512]{1,0:T(8,128)(2,1)S(1)}, bf16[32,512]{1,0:T(8,128)(2,1)S(1)}, u32[]{:S(2)}, u32[]{:S(2)}) %collective-permute-start.9) | collective-permute-done | bytes 32800 | tf_op jit(solution)/shard_map/ppermute | solution.py:545
  36.4 0.1 shard_map.200
  36.5 0.0 collective-permute-start.10
  36.6 3.9 %collective-permute-done.10.other_ref = bf16[32,512]{1,0:T(8,128)(2,1)S(1)} collective-permute-done((bf16[32,512]{1,0:T(8,128)(2,1)S(1)}, bf16[32,512]{1,0:T(8,128)(2,1)S(1)}, u32[]{:S(2)}, u32[]{:S(2)}) %collective-permute-start.10) | collective-permute-done | bytes 32800 | tf_op jit(solution)/shard_map/ppermute | solution.py:545
  40.5 0.1 shard_map.201
  40.6 0.0 collective-permute-start.11
  40.6 1.1 %shard_map.197 = (bf16[64,2048]{1,0:T(8,128)(2,1)}, bf16[32,64]{1,0:T(8,128)(2,1)}) custom-call(s32[1,1]{1,0:T(1,128)S(6)} %copy.21.count_ref, bf16[64,4096]{1,0:T(8,128)(2,1)S(1)} %get-tuple-element.107.edges_ref, bf16[64,4096]{1,0:T(8,128)(2,1)S(1)} %get-tuple-element.115.hidden_ref, bf16[128,64]{1,0:T(8,128)(2,1)S(1)} %get-tuple-element.125.joined_ref, ...), custom_call_target="tpu_custom_call" | custom-call | flops 2000000000 | bytes 7200000 | tf_op jit(solution)/shard_map/pallas_call | solution.py:530
  41.7 3.7 %collective-permute-done.11.other_ref = bf16[32,512]{1,0:T(8,128)(2,1)S(1)} collective-permute-done((bf16[32,512]{1,0:T(8,128)(2,1)S(1)}, bf16[32,512]{1,0:T(8,128)(2,1)S(1)}, u32[]{:S(2)}, u32[]{:S(2)}) %collective-permute-start.11) | collective-permute-done | bytes 32800 | tf_op jit(solution)/shard_map/ppermute | solution.py:545
  45.4 0.1 collective-permute-start.12
  45.5 1.0 %shard_map.202 = f32[32,64]{1,0:T(8,128)} custom-call(bf16[32,640]{1,0:T(8,128)(2,1)S(1)} %collective-permute-done.8.other_ref.first_ref, bf16[32,512]{1,0:T(8,128)(2,1)S(1)} %collective-permute-done.11.other_ref, f32[32,48]{1,0:T(8,128)S(1)} %get-tuple-element.145.arrived_ref, f32[64,64]{1,0:T(8,128)S(1)} %get-tuple-element.146.back_ref, ...), custom_call_target="tpu_custom_call" | custom-call | flops 1000000000 | bytes 3600000 | tf_op jit(solution)/shard_map/pallas_call | solution.py:530
  46.5 0.2 collective-permute-done.12.other_ref
  46.7 0.7 %shard_map.204 = (f32[64,192]{1,0:T(8,128)}, f32[64,64]{1,0:T(8,128)}, f32[64,128]{1,0:T(8,128)}, f32[64,64]{1,0:T(8,128)}, f32[4,64]{1,0:T(4,128)}) custom-call(bf16[32,512]{1,0:T(8,128)(2,1)S(1)} %shard_map.203.half_ref, bf16[32,512]{1,0:T(8,128)(2,1)S(1)} %collective-permute-done.12.other_ref), custom_call_target="tpu_custom_call" | custom-call | flops 1000000000 | bytes 3600000 | tf_op jit(solution)/shard_map/pallas_call | solution.py:530
  (7 shorter events, 0.0 us)
Async XLA Ops:
  1.3 4.0 %copy-start = (bf16[64,2048]{1,0:T(8,128)(2,1)S(1)}, bf16[64,2048]{1,0:T(8,128)(2,1)}, u32[]{:S(2)}) copy-start(bf16[64,2048]{1,0:T(8,128)(2,1)} %refs_0_.1) | copy-start | bytes 786436
  2.2 4.8 %collective-permute-start.1 = (bf16[80,128]{1,0:T(8,128)(2,1)S(1)}, bf16[80,128]{1,0:T(8,128)(2,1)S(1)}, u32[]{:S(2)}, u32[]{:S(2)}) collective-permute-start(bf16[80,128]{1,0:T(8,128)(2,1)S(1)} %get-tuple-element.81.packed_ref.refs_0_), channel_id=1, source_target_pairs={{0,1},{1,0},{2,3},{3,2},{4,5},{5,4},{6,7},{7,6},{8,9},{9,8},{10,11... | collective-permute-start | bytes 61448 | tf_op jit(solution)/shard_map/ppermute | solution.py:545
  5.3 7.8 %collective-permute-start = (bf16[64,2048]{1,0:T(8,128)(2,1)S(1)}, bf16[64,2048]{1,0:T(8,128)(2,1)S(1)}, u32[]{:S(2)}, u32[]{:S(2)}) collective-permute-start(bf16[64,2048]{1,0:T(8,128)(2,1)S(1)} %copy-done), channel_id=1, source_target_pairs={{0,1},{1,0},{2,3},{3,2},{4,5},{5,4},{6,7},{7,6},{8,9},{9,8},{10,11... | collective-permute-start | bytes 786440 | tf_op jit(solution)/shard_map/ppermute | solution.py:545
  7.0 3.6 %copy-start.1 = (bf16[64,192]{1,0:T(8,128)(2,1)S(1)}, bf16[64,192]{1,0:T(8,128)(2,1)}, u32[]{:S(2)}) copy-start(bf16[64,192]{1,0:T(8,128)(2,1)} %first_ref.3) | copy-start | bytes 73732
  7.0 3.6 %copy-start.2 = (bf16[64,128]{1,0:T(8,128)(2,1)S(1)}, bf16[64,128]{1,0:T(8,128)(2,1)}, u32[]{:S(2)}) copy-start(bf16[64,128]{1,0:T(8,128)(2,1)} %node_first_ref.1) | copy-start | bytes 49156
  7.0 3.6 %copy-start.3 = (bf16[64,64]{1,0:T(8,128)(2,1)S(1)}, bf16[64,64]{1,0:T(8,128)(2,1)}, u32[]{:S(2)}) copy-start(bf16[64,64]{1,0:T(8,128)(2,1)} %second_ref.5) | copy-start | bytes 24580
  7.0 3.6 %copy-start.4 = (bf16[64,64]{1,0:T(8,128)(2,1)S(1)}, bf16[64,64]{1,0:T(8,128)(2,1)}, u32[]{:S(2)}) copy-start(bf16[64,64]{1,0:T(8,128)(2,1)} %node_second_ref.3) | copy-start | bytes 24580
  7.0 3.6 %copy-start.5 = (f32[4,64]{1,0:T(4,128)S(1)}, f32[4,64]{1,0:T(4,128)}, u32[]{:S(2)}) copy-start(f32[4,64]{1,0:T(4,128)} %refs_7_.2) | copy-start | bytes 3076
  7.2 6.5 %collective-permute-start.2 = (bf16[64,64]{1,0:T(8,128)(2,1)S(1)}, bf16[64,64]{1,0:T(8,128)(2,1)S(1)}, u32[]{:S(2)}, u32[]{:S(2)}) collective-permute-start(bf16[64,64]{1,0:T(8,128)(2,1)S(1)} %get-tuple-element.94), channel_id=1, source_target_pairs={{0,30},{2,4},{4,2},{6,8},{8,6},{10,12},{12,10},{14,16},{16,14},{18... | collective-permute-start | bytes 24584 | tf_op jit(solution)/shard_map/ppermute | solution.py:545
  10.6 3.1 %collective-permute-start.3 = (bf16[64,64]{1,0:T(8,128)(2,1)S(1)}, bf16[64,64]{1,0:T(8,128)(2,1)S(1)}, u32[]{:S(2)}, u32[]{:S(2)}) collective-permute-start(bf16[64,64]{1,0:T(8,128)(2,1)S(1)} %get-tuple-element.95), channel_id=1, source_target_pairs={{0,2},{2,0},{4,6},{6,4},{8,10},{10,8},{12,14},{14,12},{16,18},{18,... | collective-permute-start | bytes 24584 | tf_op jit(solution)/shard_map/ppermute | solution.py:545
  15.2 5.9 %collective-permute-start.4 = (bf16[64,128]{1,0:T(8,128)(2,1)S(1)}, bf16[64,128]{1,0:T(8,128)(2,1)S(1)}, u32[]{:S(2)}, u32[]{:S(2)}) collective-permute-start(bf16[64,128]{1,0:T(8,128)(2,1)S(1)} %get-tuple-element.109), channel_id=1, source_target_pairs={{0,30},{2,4},{4,2},{6,8},{8,6},{10,12},{12,10},{14,16},{16,14},{18... | collective-permute-start | bytes 49160 | tf_op jit(solution)/shard_map/ppermute | solution.py:545
  18.1 3.1 %collective-permute-start.5 = (bf16[64,128]{1,0:T(8,128)(2,1)S(1)}, bf16[64,128]{1,0:T(8,128)(2,1)S(1)}, u32[]{:S(2)}, u32[]{:S(2)}) collective-permute-start(bf16[64,128]{1,0:T(8,128)(2,1)S(1)} %get-tuple-element.110), channel_id=1, source_target_pairs={{0,2},{2,0},{4,6},{6,4},{8,10},{10,8},{12,14},{14,12},{16,18},{18,... | collective-permute-start | bytes 49160 | tf_op jit(solution)/shard_map/ppermute | solution.py:545
  23.3 5.9 %collective-permute-start.6 = (bf16[64,64]{1,0:T(8,128)(2,1)S(1)}, bf16[64,64]{1,0:T(8,128)(2,1)S(1)}, u32[]{:S(2)}, u32[]{:S(2)}) collective-permute-start(bf16[64,64]{1,0:T(8,128)(2,1)S(1)} %get-tuple-element.130), channel_id=1, source_target_pairs={{0,30},{2,4},{4,2},{6,8},{8,6},{10,12},{12,10},{14,16},{16,14},{18... | collective-permute-start | bytes 24584 | tf_op jit(solution)/shard_map/ppermute | solution.py:545
  26.1 3.1 %collective-permute-start.7 = (bf16[64,64]{1,0:T(8,128)(2,1)S(1)}, bf16[64,64]{1,0:T(8,128)(2,1)S(1)}, u32[]{:S(2)}, u32[]{:S(2)}) collective-permute-start(bf16[64,64]{1,0:T(8,128)(2,1)S(1)} %get-tuple-element.130), channel_id=1, source_target_pairs={{0,2},{2,0},{4,6},{6,4},{8,10},{10,8},{12,14},{14,12},{16,18},{18,... | collective-permute-start | bytes 24584 | tf_op jit(solution)/shard_map/ppermute | solution.py:545
  31.2 1.3 %collective-permute-start.8 = (bf16[32,640]{1,0:T(8,128)(2,1)S(1)}, bf16[32,640]{1,0:T(8,128)(2,1)S(1)}, u32[]{:S(2)}, u32[]{:S(2)}) collective-permute-start(bf16[32,640]{1,0:T(8,128)(2,1)S(1)} %get-tuple-element.140), channel_id=1, source_target_pairs={{0,2},{2,0},{4,6},{6,4},{8,10},{10,8},{12,14},{14,12},{16,18},{18,... | collective-permute-start | bytes 122888 | tf_op jit(solution)/shard_map/ppermute | solution.py:545
  32.5 3.9 %collective-permute-start.9 = (bf16[32,512]{1,0:T(8,128)(2,1)S(1)}, bf16[32,512]{1,0:T(8,128)(2,1)S(1)}, u32[]{:S(2)}, u32[]{:S(2)}) collective-permute-start(bf16[32,512]{1,0:T(8,128)(2,1)S(1)} %shard_map.199.mine_ref), channel_id=1, source_target_pairs={{0,4},{2,6},{4,0},{6,2},{8,12},{10,14},{12,8},{14,10},{16,20},{18,... | collective-permute-start | bytes 98312 | tf_op jit(solution)/shard_map/ppermute | solution.py:545
  36.5 3.9 %collective-permute-start.10 = (bf16[32,512]{1,0:T(8,128)(2,1)S(1)}, bf16[32,512]{1,0:T(8,128)(2,1)S(1)}, u32[]{:S(2)}, u32[]{:S(2)}) collective-permute-start(bf16[32,512]{1,0:T(8,128)(2,1)S(1)} %get-tuple-element.142.mine_ref), channel_id=1, source_target_pairs={{0,8},{2,10},{4,12},{6,14},{8,0},{10,2},{12,4},{14,6},{16,24},{18,... | collective-permute-start | bytes 98312 | tf_op jit(solution)/shard_map/ppermute | solution.py:545
  40.6 4.8 %collective-permute-start.11 = (bf16[32,512]{1,0:T(8,128)(2,1)S(1)}, bf16[32,512]{1,0:T(8,128)(2,1)S(1)}, u32[]{:S(2)}, u32[]{:S(2)}) collective-permute-start(bf16[32,512]{1,0:T(8,128)(2,1)S(1)} %get-tuple-element.144.mine_ref), channel_id=1, source_target_pairs={{0,16},{2,18},{4,20},{6,22},{8,24},{10,26},{12,28},{14,30},{16,0},... | collective-permute-start | bytes 98312 | tf_op jit(solution)/shard_map/ppermute | solution.py:545
  45.4 1.3 %collective-permute-start.12 = (bf16[32,512]{1,0:T(8,128)(2,1)S(1)}, bf16[32,512]{1,0:T(8,128)(2,1)S(1)}, u32[]{:S(2)}, u32[]{:S(2)}) collective-permute-start(bf16[32,512]{1,0:T(8,128)(2,1)S(1)} %shard_map.203.half_ref), channel_id=1, source_target_pairs={{0,2},{2,0},{4,6},{6,4},{8,10},{10,8},{12,14},{14,12},{16,18},{18,... | collective-permute-start | bytes 98312 | tf_op jit(solution)/shard_map/ppermute | solution.py:545

commit v7 on v6

--- a/solution.py
+++ b/solution.py
@@ -52,6 +52,16 @@
 
 def is_even():
     return lax.rem(lax.axis_index("phi"), 2) == 0
+
+
+def lower_rows(ring):
+    place = lax.axis_index("phi")
+    total = place
+    bit = 2
+    while bit < ring:
+        total = total + place // bit
+        bit *= 2
+    return lax.rem(total, 2) == 0
 
 
 def pick(parts, natural):
@@ -105,16 +115,25 @@
     return value, logistic + value * (1.0 - logistic)
 
 
-def activate(base_ref, table, onehot_ref, slab, hidden_ref, slope_ref):
+def activate(base_ref, table, onehot_ref, slab, edges_ref, second_ref, bias, hidden_ref, slope_ref, new_ref):
     wide = onehot_ref.shape[0] - slab
+    second = second_ref[...]
+    latent = second.shape[0]
+    same = lax.broadcasted_iota(jnp.int32, (latent, latent), 0) == lax.broadcasted_iota(
+        jnp.int32, (latent, latent), 1
+    )
+    update = jnp.concatenate([second.astype(F32), same.astype(F32)], axis=1).astype(BF)
     for cols in chunks_of(base_ref.shape[1]):
         rims = onehot_ref[slab:wide, cols]
-        pre = base_ref[:, cols].astype(F32) + mm(table, jnp.concatenate([rims, rims], axis=0))
-        value, slope = slope_parts(pre)
-        hidden = value.astype(BF)
-        hidden_ref[:, cols] = hidden
-        slope_ref[:, cols] = slope.astype(BF)
-    return mm_nt(hidden_ref[...], onehot_ref[wide:])
+        slope_ref[:, cols] = base_ref[:, cols] + mm(table, jnp.concatenate([rims, rims], axis=0))
+    for cols in chunks_of(base_ref.shape[1]):
+        value, slope = slope_parts(slope_ref[:, cols])
+        hidden_ref[:, cols] = value.astype(BF)
+        slope_ref[:, cols] = slope
+    for cols in chunks_of(base_ref.shape[1]):
+        both = jnp.concatenate([hidden_ref[:, cols], edges_ref[:, cols]], axis=0)
+        new_ref[:, cols] = (mm(update, both) + bias[:, 1:2]).astype(BF)
+    return mm_nt(new_ref[...], onehot_ref[wide:])
 
 
 def slab_base(source, target, own, bias, onehot_ref, edges_ref, base_ref):
@@ -125,16 +144,7 @@
         near = onehot_ref[:slab, cols]
         hit = onehot_ref[wide:, cols]
         stack = jnp.concatenate([near, near, hit, hit, edges_ref[:, cols]], axis=0)
-        base_ref[:, cols] = (mm(table, stack) + bias[:, 0:1]).astype(BF)
-
-
-def node_base(state16, message, first_ref, bias):
-    latent = state16.shape[0]
-    return (
-        mm(first_ref[:, :latent], state16)
-        + wide_mm(first_ref[:, latent:], message)
-        + bias[:, 2:3]
-    )
+        base_ref[:, cols] = mm(table, stack) + bias[:, 0:1]
 
 
 def node_sums(grad, pre_grad, joined, hidden):
@@ -198,8 +208,8 @@
 def onehot_kernel(groups, rows, rim, *refs):
     packs = [ref[: 3 * rows].astype(F32) for ref in refs[:groups]]
     (slab_ref, first_ref, second_ref, node_first_ref, node_second_ref, bias_ref, alpha_pick, beta_pick,
-     onehot_ref, base_ref, count_ref, table_ref, first_back, second_back, node_first_back, node_second_back, bias_out,
-     to_node, to_node_back, to_table, to_table_back, to_hidden, alpha_place, beta_place) = refs[groups:]
+     onehot_ref, base_ref, count_ref, first_back, second_back, node_first_back, node_second_back, bias_out,
+     to_node_back, to_table_back, to_hidden, alpha_place, beta_place) = refs[groups:]
     latent = first_ref.shape[0]
     slab, room = alpha_pick.shape
     wide = slab + room
@@ -220,8 +230,6 @@
     slab16 = slab_ref[...]
     source = mm(first_ref[:, :latent], slab16)
     target = mm(first_ref[:, latent : 2 * latent], slab16)
-    shift = wide_mm(first_ref[:, :latent], jnp.broadcast_to(bias[:, 3:4], (latent, LANES)))
-    table_ref[...] = source + shift[:, :1]
     table = jnp.concatenate([*halves(source), *halves(target)], axis=1)
     count = None
     for cols in chunks_of(base_ref.shape[1]):
@@ -235,10 +243,8 @@
     node_first_back[...] = flip(node_first_ref[...])
     node_second_back[...] = flip(node_second_ref[...])
     forward = mm(node_first_ref[:, latent:], second_ref[...])
-    to_node[...] = split(forward)
     to_node_back[...] = split(forward.T)
     table = mm(first_ref[:, :latent], node_second_ref[...])
-    to_table[...] = split(table)
     to_table_back[...] = split(table.T)
     to_hidden[...] = split(mm(first_ref[:, 2 * latent :], second_ref[...]).T)
     for choose, place in ((alpha_pick, alpha_place), (beta_pick, beta_place)):
@@ -251,106 +257,100 @@
 
 def start_kernel(groups, *refs):
     parts = refs[:groups]
-    (base_in, onehot_ref, slab_ref, count_ref, first_ref, node_first_ref, bias_ref,
-     edges_ref, base_ref, message_ref, node_base_ref) = refs[groups:]
-    latent, slab = slab_ref.shape
-    wide = onehot_ref.shape[0] - slab
+    base_in, first_ref, edges_ref, base_ref = refs[groups:]
+    latent = first_ref.shape[1] // 3
     slots = parts[0].shape[1]
     own = first_ref[:, 2 * latent :]
-    message = None
     for rank in range(groups):
         for cols in chunks_of(slots):
             here = slice(rank * slots + cols.start, rank * slots + cols.stop)
             edges = pick([part[:, cols] for part in parts], rank)
             edges_ref[:, here] = edges
-            base_ref[:, here] = (base_in[:, here] + mm(own, edges)).astype(BF)
-            message = add_to(message, mm_nt(edges, onehot_ref[wide:, here]))
-    bias = bias_ref[...]
-    message = message + bias[:, 1:2] * count_ref[0:1]
-    message_ref[...] = message
-    node_base_ref[...] = node_base(slab_ref[...], message, node_first_ref, bias)
-
-
-def forward_kernel(base_ref, onehot_ref, slab_ref, beta_in, alpha_in, node_base_ref, table_in,
-                   first_ref, node_second_ref, bias_ref, to_node, to_table, alpha_place, beta_place,
-                   hidden_ref, slope_ref, rims_ref, sums_ref, node_pre_ref, node_hidden_ref, state_ref, table_ref,
-                   alpha_ref, beta_ref):
+            base_ref[:, here] = base_in[:, here] + mm(own, edges)
+
+
+def node_forward(slab16, message, node_first_ref, bias):
+    joined = jnp.concatenate([slab16, message.astype(BF)], axis=0)
+    return joined, mm(node_first_ref[...], joined) + bias[:, 2:3]
+
+
+def forward_kernel(base_ref, onehot_ref, edges_ref, slab_ref, beta_in, alpha_in,
+                   first_ref, second_ref, node_first_ref, node_second_ref, bias_ref, alpha_place, beta_place,
+                   hidden_ref, slope_ref, new_ref, rims_ref, joined_ref, node_pre_ref, node_hidden_ref, state_ref,
+                   table_ref, alpha_ref, beta_ref):
     latent, slab = slab_ref.shape
     rims16 = alpha_in[...] + beta_in[...]
     rims_ref[...] = rims16
+    bias = bias_ref[...]
     table = jnp.concatenate(halves(mm(first_ref[:, :latent], rims16)), axis=1)
-    sums = activate(base_ref, table, onehot_ref, slab, hidden_ref, slope_ref)
-    sums_ref[...] = sums
-    node_pre = node_base_ref[...] + split_mm(to_node[...], sums)
+    message = activate(
+        base_ref, table, onehot_ref, slab, edges_ref, second_ref, bias, hidden_ref, slope_ref, new_ref
+    )
+    slab16 = slab_ref[...]
+    joined, node_pre = node_forward(slab16, message, node_first_ref, bias)
+    joined_ref[...] = joined
     node_pre_ref[...] = node_pre
     node_hidden = slope_parts(node_pre)[0].astype(BF)
     node_hidden_ref[...] = node_hidden
-    table = table_in[...] + pair_mm(to_table[...], node_hidden)
+    state = (slab16.astype(F32) + mm(node_second_ref[...], node_hidden) + bias[:, 3:4]).astype(BF)
+    state_ref[...] = state
+    table = mm(first_ref[:, :latent], state)
     table_ref[...] = table
     both = jnp.concatenate(halves(table), axis=1)
     alpha_ref[...] = mm(both, alpha_place[...]).astype(BF)
     beta_ref[...] = mm(both, beta_place[...]).astype(BF)
-    state = slab_ref[...].astype(F32) + mm(node_second_ref[...], node_hidden) + bias_ref[:, 3:4]
-    state_ref[...] = state.astype(BF)
-
-
-def between_kernel(edges_ref, hidden_ref, onehot_ref, slab_in, state_ref, table_ref, sums_ref, message_in, count_ref,
-                   first_ref, second_ref, node_first_ref, bias_ref,
-                   new_ref, base_ref, message_ref, joined_ref, node_base_ref):
-    latent = edges_ref.shape[0]
-    bias = bias_ref[...]
-    second = second_ref[...]
-    for cols in chunks_of(edges_ref.shape[1]):
-        new_ref[:, cols] = (
-            edges_ref[:, cols].astype(F32) + mm(second, hidden_ref[:, cols]) + bias[:, 1:2]
-        ).astype(BF)
-    state16 = state_ref[...]
-    target = mm(first_ref[:, latent : 2 * latent], state16)
-    slab_base(table_ref[...], target, first_ref[:, 2 * latent :], bias, onehot_ref, new_ref, base_ref)
-    message = message_in[...] + wide_mm(second, sums_ref[...])
-    joined_ref[...] = jnp.concatenate([slab_in[...], message.astype(BF)], axis=0)
-    message = message + bias[:, 1:2] * count_ref[0:1]
-    message_ref[...] = message
-    node_base_ref[...] = node_base(state16, message, node_first_ref, bias)
+
+
+def between_kernel(edges_ref, hidden_ref, onehot_ref, state_ref, table_ref, first_ref, bias_ref, base_ref, sums_ref):
+    latent, slab = state_ref.shape
+    wide = onehot_ref.shape[0] - slab
+    target = mm(first_ref[:, latent : 2 * latent], state_ref[...])
+    slab_base(
+        table_ref[...], target, first_ref[:, 2 * latent :], bias_ref[...], onehot_ref, edges_ref, base_ref
+    )
+    sums_ref[...] = mm_nt(hidden_ref[...], onehot_ref[wide:])
 
 
 def edge_gradient(wanted, extra_ref, slope_ref, onehot_ref, edges_ref, low_ref):
     slab = wanted.shape[1]
     wide = onehot_ref.shape[0] - slab
-    table = jnp.concatenate(halves(wanted), axis=1)
+    table = wanted.astype(BF)
     for cols in chunks_of(edges_ref.shape[1]):
-        hit = onehot_ref[wide:, cols]
-        grad = mm(table, jnp.concatenate([hit, hit], axis=0))
+        grad = mm(table, onehot_ref[wide:, cols])
         if extra_ref is not None:
-            grad = grad + extra_ref[:, cols].astype(F32)
-        low_ref[:, cols] = (grad * slope_ref[:, cols].astype(F32)).astype(BF)
+            grad = grad + extra_ref[:, cols]
+        low_ref[:, cols] = (grad * slope_ref[:, cols]).astype(BF)
     return mm_nt(low_ref[...], jnp.concatenate([onehot_ref[...], edges_ref[...]], axis=0))
 
 
-def middle_kernel(base_ref, onehot_ref, edges_ref, beta_in, alpha_in, node_base_ref, cot_ref,
-                  node_second_back, to_node, to_node_back,
-                  hidden_ref, low_ref, sums_ref, node_pre_ref, node_grad_ref, wanted_ref, first_sums_ref, rims_ref,
-                  slope_ref):
+def middle_kernel(base_ref, onehot_ref, edges_ref, slab_ref, beta_in, alpha_in, cot_ref,
+                  second_ref, node_first_ref, bias_ref, node_second_back, to_node_back,
+                  hidden_ref, new_ref, low_ref, joined_ref, node_pre_ref, node_grad_ref, wanted_ref, first_sums_ref,
+                  rims_ref, slope_ref):
     slab = cot_ref.shape[1]
     wide = onehot_ref.shape[0] - slab
+    bias = bias_ref[...]
     cot_grad = mm(node_second_back[...], cot_ref[...].astype(BF))
-    sums = activate(base_ref, alpha_in[...] + beta_in[...], onehot_ref, slab, hidden_ref, slope_ref)
-    sums_ref[...] = sums
-    node_pre = node_base_ref[...] + split_mm(to_node[...], sums)
+    message = activate(
+        base_ref, alpha_in[...] + beta_in[...], onehot_ref, slab, edges_ref, second_ref, bias, hidden_ref,
+        slope_ref, new_ref,
+    )
+    joined, node_pre = node_forward(slab_ref[...], message, node_first_ref, bias)
+    joined_ref[...] = joined
     node_pre_ref[...] = node_pre
     pre_grad = cot_grad * slope_parts(node_pre)[1]
     node_grad_ref[...] = pre_grad
-    wanted = split_mm(to_node_back[...], pre_grad)
+    wanted = pair_mm(to_node_back[...], pre_grad.astype(BF))
     wanted_ref[...] = wanted
     first_sums = edge_gradient(wanted, None, slope_ref, onehot_ref, edges_ref, low_ref)
     rims_ref[...] = first_sums[:, slab:wide].astype(BF)
     first_sums_ref[...] = first_sums
 
 
-def carry_kernel(rim, low_ref, hidden_zero_ref, slab_ref, sums_ref, sums_zero_ref, message_in,
+def carry_kernel(rim, low_ref, hidden_zero_ref, hidden_ref, onehot_ref, slab_ref, sums_zero_ref, joined_ref,
                  node_pre_ref, node_grad_ref, first_sums_ref, count_ref, cot_ref,
-                 second_ref, first_back, node_first_back, node_second_back, to_hidden,
-                 extra_ref, total_ref, joined_ref, back_ref, back_node_ref):
+                 first_back, node_first_back, node_second_back, to_hidden,
+                 extra_ref, total_ref, back_ref, back_node_ref):
     latent, slab = slab_ref.shape
     wide = first_sums_ref.shape[1] - slab - latent
     sums = first_sums_ref[...]
@@ -367,15 +367,14 @@
     cross = None
     for cols in chunks_of(low_ref.shape[1]):
         low = low_ref[:, cols]
-        extra_ref[:, cols] = pair_mm(to_hidden[...], low).astype(BF)
+        extra_ref[:, cols] = pair_mm(to_hidden[...], low)
         cross = add_to(cross, mm_nt(low, hidden_zero_ref[:, cols]))
     slab16 = slab_ref[...]
-    message = message_in[...] + wide_mm(second_ref[...], sums_ref[...])
-    joined = jnp.concatenate([slab16, message.astype(BF)], axis=0)
-    joined_ref[...] = joined
+    joined = joined_ref[...]
+    hidden_sums = mm_nt(hidden_ref[...], onehot_ref[wide:])
     pre_sum = sums[:, slab + 2 * rim : slab + 2 * rim + 1]
     edge_two = (
-        mm_nt(gm, sums_ref[...].astype(BF))
+        mm_nt(gm, hidden_sums.astype(BF))
         + mm_nt(gm, sums_zero_ref[...].astype(BF))
         + mm(self_back, cross.astype(BF))
     )
@@ -393,15 +392,10 @@
     )
 
 
-def output_kernel(count_ref, edges_ref, hidden_ref, joined_ref, node_pre_ref, second_ref, node_second_ref, bias_ref,
-                  edge_out, node_out, new_ref):
+def output_kernel(count_ref, new_ref, joined_ref, node_pre_ref, node_second_ref, bias_ref,
+                  edge_out, node_out):
     bias = bias_ref[...]
-    latent = edges_ref.shape[0]
-    second = second_ref[...]
-    for cols in chunks_of(edges_ref.shape[1]):
-        new_ref[:, cols] = (
-            edges_ref[:, cols].astype(F32) + mm(second, hidden_ref[:, cols]) + bias[:, 1:2]
-        ).astype(BF)
+    latent = new_ref.shape[0]
     slots = edge_out.shape[1]
     begin = lax.axis_index("layer") * slots
     for cols in chunks_of(slots):
@@ -413,15 +407,15 @@
     node_out[...] = own_rows(state.T, node_out.shape[0]).astype(BF)
 
 
-def last_kernel(rim, back_in, back_node, beta_in, alpha_in, alpha_pick, beta_pick, joined_ref, node_pre_ref,
+def last_kernel(rim, ring, back_in, back_node, beta_in, alpha_in, alpha_pick, beta_pick, joined_ref, node_pre_ref,
                 node_hidden_ref, wanted_in, sums_ref, count_ref, extra_ref, slope_ref, onehot_ref, edges_ref,
                 slab_ref, rims_ref, slab_one_ref, total_in, first_back, node_first_back, to_node_back, to_table_back,
                 keep_ref, send_ref, back_ref, low_ref):
     latent, slab = slab_ref.shape
     wide = onehot_ref.shape[0] - slab
     placed = mm_nt(alpha_in[...], alpha_pick[...]) + mm_nt(beta_in[...], beta_pick[...])
-    pre_grad = (back_node[...] + split_mm(to_table_back[...], placed)) * slope_parts(node_pre_ref[...])[1]
-    wanted = wanted_in[...] + split_mm(to_node_back[...], pre_grad)
+    pre_grad = (back_node[...] + pair_mm(to_table_back[...], placed.astype(BF))) * slope_parts(node_pre_ref[...])[1]
+    wanted = wanted_in[...] + pair_mm(to_node_back[...], pre_grad.astype(BF))
     sums = edge_gradient(wanted, extra_ref, slope_ref, onehot_ref, edges_ref, low_ref)
     source = sums[:, :wide].astype(BF)
     target = sums[:, wide : wide + slab].astype(BF)
@@ -450,10 +444,10 @@
     total = total_in[...] + jnp.concatenate(
         [edge_one, edge_two, node_one, node_two, pre_sum, gm_sum, node_pre_sum, grad_sum], axis=1
     )
-    even = is_even()
+    lower = lower_rows(ring)
     half, used = keep_ref.shape
-    keep_ref[...] = jnp.where(even, total[:half], total[half:])
-    pieces = [jnp.where(even, total[half:], total[:half]), alpha[:half], alpha[half:], beta[:half], beta[half:]]
+    keep_ref[...] = jnp.where(lower, total[:half], total[half:])
+    pieces = [jnp.where(lower, total[half:], total[:half]), alpha[:half], alpha[half:], beta[:half], beta[half:]]
     spare = send_ref.shape[1] - used - 4 * rim
     if spare:
         pieces.append(jnp.zeros((half, spare), F32))
@@ -470,45 +464,43 @@
     out_ref[...] = jnp.concatenate(pieces, axis=1).astype(BF)
 
 
-def add_kernel(used, rim, bit, mine_ref, other_ref, arrived_in, out_ref, arrived_ref):
+def add_kernel(used, rim, bit, turn, mine_ref, other_ref, out_ref, arrived_ref):
     other = other_ref[...].astype(F32)
     place = lax.axis_index("phi")
-    home = (lax.rem(place // bit, 2) == 1) == (lax.rem(place, 2) == 0)
-    held = other[:, used : used + 2 * rim]
-    arrived = jnp.where(home, held, 0.0)
-    if arrived_in is not None:
-        arrived = arrived + arrived_in[...]
-    arrived_ref[...] = arrived
+    upward = lax.rem(place, 2) == turn % 2
+    home = (lax.rem(place // bit, 2) == 1) == upward
+    arrived_ref[...] = jnp.where(home, other[:, used : used + 2 * rim], 0.0)
     lane = lax.broadcasted_iota(jnp.int32, other.shape, 1)
     mine = mine_ref[...].astype(F32)
     passing = jnp.where(home, 0.0, other)
     out_ref[...] = jnp.where(lane < used, mine + other, passing).astype(BF)
 
 
-def first_add(kernel, mine_ref, other_ref, out_ref, arrived_ref):
-    kernel(mine_ref, other_ref, None, out_ref, arrived_ref)
-
-
-def close_kernel(mine_ref, other_ref, half_ref):
-    half_ref[...] = (mine_ref[...].astype(F32) + other_ref[...].astype(F32)).astype(BF)
+def close_kernel(used, rim, turns, mine_ref, other_ref, *refs):
+    mine = mine_ref[...].astype(F32)
+    other = other_ref[...].astype(F32)
+    arrived = [ref[...] for ref in refs[:-2]] + [other[:, used : used + 2 * rim]]
+    half_ref, stay_ref = refs[-2:]
+    crossed = sum(arrived[2::2], arrived[0])
+    stay = sum(arrived[3::2], arrived[1])
+    stay_ref[...] = stay
+    pieces = [(mine + other)[:, :used], crossed]
+    spare = half_ref.shape[1] - used - 2 * rim
+    if spare:
+        pieces.append(jnp.zeros((mine.shape[0], spare), F32))
+    half_ref[...] = jnp.concatenate(pieces, axis=1)
 
 
 def rims_of(value, used, rim):
     return jnp.concatenate([value[:, used : used + rim], value[:, used + rim : used + 2 * rim]], axis=0)
 
 
-def node_kernel(used, rim, first_ref, other_ref, arrived_ref, back_ref, upper_ref, lower_ref, node_grad):
-    alpha = rims_of(first_ref[...].astype(F32), used, rim)
-    beta = rims_of(other_ref[...].astype(F32), used, rim) + rims_of(arrived_ref[...], 0, rim)
-    grad = back_ref[...] + placed_rims(alpha, beta, upper_ref, lower_ref)
-    node_grad[...] = own_rows(grad.T, node_grad.shape[0])
-
-
-def finish_kernel(used, half_ref, other_ref, edge_one, edge_two, node_one, node_two, bias_out):
-    even = is_even()
-    mine = half_ref[...].astype(F32)
-    other = other_ref[...].astype(F32)
-    total = jnp.concatenate([jnp.where(even, mine, other), jnp.where(even, other, mine)], axis=0)
+def finish_kernel(used, rim, ring, half_ref, other_ref, stay_ref, first_ref, back_ref, upper_ref, lower_ref,
+                  node_grad, edge_one, edge_two, node_one, node_two, bias_out):
+    lower = lower_rows(ring)
+    mine = half_ref[...]
+    other = other_ref[...]
+    total = jnp.concatenate([jnp.where(lower, mine, other), jnp.where(lower, other, mine)], axis=0)
     cut = 0
     for ref in (edge_one, edge_two, node_one, node_two):
         ref[...] = total[:, cut : cut + ref.shape[1]]
@@ -516,6 +508,10 @@
     block = used - 4 - (used - 4) % LANES
     turned = total[:, block : block + LANES].T
     bias_out[...] = turned[used - 4 - block : used - block]
+    alpha = rims_of(first_ref[...].astype(F32), used, rim)
+    beta = rims_of(other, used, rim) + rims_of(stay_ref[...], 0, rim)
+    grad = back_ref[...] + placed_rims(alpha, beta, upper_ref, lower_ref)
+    node_grad[...] = own_rows(grad.T, node_grad.shape[0])
 
 
 def call(kernel, outs, *args, scratch=(), smem=0, hbm=(), cost=1.0):
@@ -600,60 +596,56 @@
     )
     beta = by_beta(beta)
     alpha = by_alpha(alpha)
-    (onehot, base, count, table, first_back, second_back, node_first_back, node_second_back, bias,
-     to_node, to_node_back, to_table, to_table_back, to_hidden, alpha_place, beta_place) = call(
+    (onehot, base, count, first_back, second_back, node_first_back, node_second_back, bias,
+     to_node_back, to_table_back, to_hidden, alpha_place, beta_place) = call(
         functools.partial(onehot_kernel, groups, rows, rim),
-        [((wide + slab, total_slots), BF), per_slot(F32), ((8, slab), F32), per_hit(F32),
+        [((wide + slab, total_slots), BF), per_slot(F32), ((8, slab), F32),
          (edge_first.shape[::-1], BF), (edge_second.shape[::-1], BF),
          (node_first.shape[::-1], BF), (node_second.shape[::-1], BF), (biases.shape[::-1], F32)]
-        + [((hidden, 3 * hidden), BF)] * 5 + [((2 * slab, 2 * room), BF)] * 2,
+        + [((hidden, 3 * hidden), BF)] * 3 + [((2 * slab, 2 * room), BF)] * 2,
         *packs, slab_zero, edge_first, edge_second, node_first, node_second, biases, alpha_pick, beta_pick, cost=2.0,
     )
-    edges_zero, base, message, node_base_zero = call(
-        functools.partial(start_kernel, groups),
-        [per_slot(BF), per_slot(BF), per_hit(F32), per_hit(F32)],
-        *parts, base, onehot, slab_zero, count, edge_first, node_first, bias, cost=1.0,
-    )
-    (hidden_zero, slope, rims_zero, sums_zero, node_pre_zero, node_hidden_zero, slab_one, table,
+    edges_zero, base = call(
+        functools.partial(start_kernel, groups), [per_slot(BF), per_slot(F32)], *parts, base, edge_first, cost=1.0,
+    )
+    (hidden_zero, slope, edges_one, rims_zero, joined_zero, node_pre_zero, node_hidden_zero, slab_one, table,
      alpha, beta) = call(
         forward_kernel,
-        [per_slot(BF), per_slot(BF), rim_shape, per_hit(F32), per_hit(F32), per_hit(BF), per_hit(BF), per_hit(F32),
-         ((latent, 2 * room), BF), ((latent, 2 * room), BF)],
-        base, onehot, slab_zero, beta, alpha, node_base_zero, table, edge_first, node_second, bias, to_node, to_table,
+        [per_slot(BF), per_slot(F32), per_slot(BF), rim_shape, per_hit(BF, 2), per_hit(F32), per_hit(BF), per_hit(BF),
+         per_hit(F32), ((latent, 2 * room), BF), ((latent, 2 * room), BF)],
+        base, onehot, edges_zero, slab_zero, beta, alpha, edge_first, edge_second, node_first, node_second, bias,
         alpha_place, beta_place, cost=2.0,
     )
     beta = by_beta(beta)
     alpha = by_alpha(alpha)
-    edges_one, base, message, joined_zero, node_base_one = call(
-        between_kernel, [per_slot(BF), per_slot(BF), per_hit(F32), per_hit(BF, 2), per_hit(F32)],
-        edges_zero, hidden_zero, onehot, slab_zero, slab_one, table, sums_zero, message, count,
-        edge_first, edge_second, node_first, bias, cost=2.0,
+    base, sums_zero = call(
+        between_kernel, [per_slot(F32), per_hit(F32)],
+        edges_one, hidden_zero, onehot, slab_one, table, edge_first, bias, cost=2.0,
     )
     total_width = edge_first.shape[1] + hidden + node_first.shape[1] + node_second.shape[1] + 4
-    hidden_one, low, sums_one, node_pre_one, node_grad_one, wanted, first_sums, rims = call(
+    hidden_one, edges_two, low, joined_one, node_pre_one, node_grad_one, wanted, first_sums, rims = call(
         middle_kernel,
-        [per_slot(BF), per_slot(BF), per_hit(F32), per_hit(F32), per_hit(F32), per_hit(F32),
+        [per_slot(BF), per_slot(BF), per_slot(BF), per_hit(BF, 2), per_hit(F32), per_hit(F32), per_hit(F32),
          ((hidden, wide + slab + latent), F32), rim_shape],
-        base, onehot, edges_one, beta, alpha, node_base_one, cot, node_second_back, to_node, to_node_back,
-        scratch=[VM((hidden, total_slots), BF)], cost=3.0,
+        base, onehot, edges_one, slab_one, beta, alpha, cot, edge_second, node_first, bias, node_second_back,
+        to_node_back, scratch=[VM((hidden, total_slots), F32)], cost=3.0,
     )
     beta = by_beta(rims)
     alpha = by_alpha(rims)
-    extra, total, joined_one, back, back_node = call(
+    extra, total, back, back_node = call(
         functools.partial(carry_kernel, rim),
-        [per_slot(BF), ((latent, total_width), F32), per_hit(BF, 2), per_hit(F32), per_hit(F32)],
-        low, hidden_zero, slab_one, sums_one, sums_zero, message, node_pre_one, node_grad_one, first_sums, count, cot,
-        edge_second, first_back, node_first_back, node_second_back, to_hidden, cost=2.0,
+        [per_slot(F32), ((latent, total_width), F32), per_hit(F32), per_hit(F32)],
+        low, hidden_zero, hidden_one, onehot, slab_one, sums_zero, joined_one, node_pre_one, node_grad_one, first_sums,
+        count, cot, first_back, node_first_back, node_second_back, to_hidden, cost=2.0,
     )
     edge_out, node_out = call(
         output_kernel, [((latent, slots), BF), ((width, latent), BF)],
-        edge_counts, edges_one, hidden_one, joined_one, node_pre_one, edge_second, node_second, bias,
-        scratch=[VM((latent, total_slots), BF)], smem=1, cost=2.0,
+        edge_counts, edges_two, joined_one, node_pre_one, node_second, bias, smem=1, cost=2.0,
     )
     half = hidden // 2
     up = lambda count: -(-count // LANES) * LANES
     keep, send, back = call(
-        functools.partial(last_kernel, rim),
+        functools.partial(last_kernel, rim, ring),
         [((half, total_width), F32), ((half, up(total_width + 4 * rim)), BF), per_hit(F32)],
         back, back_node, beta, alpha, alpha_pick, beta_pick, joined_zero, node_pre_zero, node_hidden_zero, wanted,
         sums_zero, count, extra, slope, onehot, edges_zero, slab_zero, rims_zero, slab_one, total,
@@ -665,29 +657,30 @@
     mine = call(
         functools.partial(open_kernel, rim), [((half, width_now), BF)], keep, first, cost=0.1,
     )[0]
+    arrived = []
     bit = 2
-    arrived = None
+    turn = 1
     while True:
-        other = swap(mine, "phi", lambda index, bit=bit: index ^ bit)
+        other = swap(mine, "phi", lambda index, bit=bit: index ^ (bit + 1))
         if 2 * bit >= ring:
             break
-        given = (mine, other) if arrived is None else (mine, other, arrived)
-        kernel = functools.partial(add_kernel, total_width, rim, bit)
-        if arrived is None:
-            kernel = functools.partial(first_add, kernel)
-        mine, arrived = call(kernel, [((half, width_now), BF), ((half, 2 * rim), F32)], *given, cost=0.1)
+        mine, block = call(
+            functools.partial(add_kernel, total_width, rim, bit, turn),
+            [((half, width_now), BF), ((half, 2 * rim), F32)], mine, other, cost=0.1,
+        )
+        arrived.append(block)
         bit *= 2
-    mine = call(close_kernel, [((half, width_now), BF)], mine, other, cost=0.1)[0]
+        turn += 1
+    mine, stay = call(
+        functools.partial(close_kernel, total_width, rim, turn),
+        [((half, width_now), F32), ((half, 2 * rim), F32)], mine, other, *arrived, cost=0.1,
+    )
     whole = by_alpha(mine)
-    node_grad = call(
-        functools.partial(node_kernel, total_width, rim), [((width, latent), F32)],
-        first, other, arrived, back, upper, lower, cost=1.0,
-    )[0]
-    edge_one, edge_two, node_one, node_two, bias_out = call(
-        functools.partial(finish_kernel, total_width),
-        [(edge_first.shape, F32), (edge_second.shape, F32), (node_first.shape, F32), (node_second.shape, F32),
-         (biases.shape, F32)],
-        mine, whole,
+    node_grad, edge_one, edge_two, node_one, node_two, bias_out = call(
+        functools.partial(finish_kernel, total_width, rim, ring),
+        [((width, latent), F32), (edge_first.shape, F32), (edge_second.shape, F32), (node_first.shape, F32),
+         (node_second.shape, F32), (biases.shape, F32)],
+        mine, whole, stay, first, back, upper, lower,
     )
     return node_out.T, edge_out, node_grad.T, edge_one, edge_two, node_one, node_two, bias_out
 

time: 47.6 us -> 46.8 us (0.983)
  Pallas kernels: 14.1 us -> 13 us
  starting transfers between devices: 12.4 us -> 13.1 us
  waiting for transfers between devices: 19.5 us -> 19 us
    pallas_call x17 -> x16, Pallas kernels: 14.1 us -> 13 us  [call(): pl.pallas_call(kernel, out_shape=[jax.ShapeDtypeStruct(shape, kind) for s...]
    ppermute x13, starting transfers between devices: 12.4 us -> 13.1 us  [swap(): lax.ppermute(value, axis, [(source, pairing(source) % count) for source i...]
    ppermute x13, waiting for transfers between devices: 19.5 us -> 19 us  [swap(): lax.ppermute(value, axis, [(source, pairing(source) % count) for source i...]
  transfers between devices with their start and end apart: 13 -> 13, of which waited for: 9 -> 9; matrix products, arithmetic and copies ran while one was open for 0% -> 0% of each run, Pallas kernels for 14% -> 11%
where the time goes in v7:
time: 46.8 us; the launch traced here: 46.6 us
  waiting for transfers between devices  19 us (41%)
  starting transfers between devices  13.1 us (28%)
  Pallas kernels  13 us (28%)
  between operations  1.45 us (3%)
    ppermute x13, waiting for transfers between devices, swap(): lax.ppermute(value, axis, [(source, pairing(source) % count) for source i...  19 us
    ppermute x13, starting transfers between devices, swap(): lax.ppermute(value, axis, [(source, pairing(source) % count) for source i...  13.1 us
    pallas_call x16, Pallas kernels, call(): pl.pallas_call(kernel, out_shape=[jax.ShapeDtypeStruct(shape, kind) for s...  13 us
  transfers between devices with their start and end apart: 13, of which 9 were waited for; matrix products, arithmetic and copies ran while one was open for 0% of the time, Pallas kernels for 11%

profile of v7, /device:TPU:0, one launch (start us, length us, event | category | flops | bytes accessed | tf_op | source)
XLA Modules:
  0.0 46.6 jit_solution(10147345672542220030)
XLA Ops:
  1.3 0.0 copy-start
  1.3 0.9 %shard_map.188 = (bf16[80,128]{1,0:T(8,128)(2,1)S(1)}, s32[1,24]{1,0:T(1,128)S(1)}, s32[1,24]{1,0:T(1,128)S(1)}) custom-call(s32[1,1]{1,0:T(1,128)S(6)} %copy.21.count_ref, s32[16,128]{1,0:T(8,128)} %bitcast.7, s32[16,128]{1,0:T(8,128)} %bitcast.8, bf16[32,64]{1,0:T(8,128)(2,1)} %bitcast.9, f32[32,64]{1,0:T(8,128)} %bitcast.6, s32[1,24]{1,0:T(1,128)} %upper_hbm.1, ...), custom_call_target="tpu_custom_call" | custom-call | flops 1000000000 | bytes 3600000 | tf_op jit(solution)/shard_map/pallas_call | solution.py:526
  2.2 3.0 %collective-permute-start.1 = (bf16[80,128]{1,0:T(8,128)(2,1)S(1)}, bf16[80,128]{1,0:T(8,128)(2,1)S(1)}, u32[]{:S(2)}, u32[]{:S(2)}) collective-permute-start(bf16[80,128]{1,0:T(8,128)(2,1)S(1)} %get-tuple-element.77.packed_ref.refs_0_), channel_id=1, source_target_pairs={{0,1},{1,0},{2,3},{3,2},{4,5},{5,4},{6,7},{7,6},{8,9},{9,8},{10,11... | collective-permute-start | bytes 61448 | tf_op jit(solution)/shard_map/ppermute | solution.py:541
  5.2 0.1 shard_map.189
  5.3 0.0 copy-done
  5.3 0.1 collective-permute-start
  5.4 1.6 %collective-permute-done.1.refs_1_ = bf16[80,128]{1,0:T(8,128)(2,1)S(1)} collective-permute-done((bf16[80,128]{1,0:T(8,128)(2,1)S(1)}, bf16[80,128]{1,0:T(8,128)(2,1)S(1)}, u32[]{:S(2)}, u32[]{:S(2)}) %collective-permute-start.1) | collective-permute-done | bytes 20512 | tf_op jit(solution)/shard_map/ppermute | solution.py:541
  7.0 0.0 copy-start.5
  7.0 0.2 shard_map.190
  7.2 3.4 %collective-permute-start.2 = (bf16[64,64]{1,0:T(8,128)(2,1)S(1)}, bf16[64,64]{1,0:T(8,128)(2,1)S(1)}, u32[]{:S(2)}, u32[]{:S(2)}) collective-permute-start(bf16[64,64]{1,0:T(8,128)(2,1)S(1)} %get-tuple-element.88), channel_id=1, source_target_pairs={{0,30},{2,4},{4,2},{6,8},{8,6},{10,12},{12,10},{14,16},{16,14},{18... | collective-permute-start | bytes 24584 | tf_op jit(solution)/shard_map/ppermute | solution.py:541
  10.6 0.0 collective-permute-start.3
  10.6 0.0 copy-done.1
  10.6 0.0 copy-done.2
  10.6 0.0 copy-done.3
  10.7 1.5 %shard_map.191 = (bf16[192,4096]{1,0:T(8,128)(2,1)S(1)}, f32[64,4096]{1,0:T(8,128)S(1)}, f32[8,64]{1,0:T(8,128)S(1)}, bf16[192,64]{1,0:T(8,128)(2,1)S(1)}, bf16[...) custom-call(bf16[80,128]{1,0:T(8,128)(2,1)S(1)} %get-tuple-element.7, ...), custom_call_target="tpu_custom_call" | custom-call | flops 2000000000 | bytes 7200000 | tf_op jit(solution)/shard_map/pallas_call | solution.py:526
  12.2 1.0 %collective-permute-done.refs_1_ = bf16[64,2048]{1,0:T(8,128)(2,1)S(1)} collective-permute-done((bf16[64,2048]{1,0:T(8,128)(2,1)S(1)}, bf16[64,2048]{1,0:T(8,128)(2,1)S(1)}, u32[]{:S(2)}, u32[]{:S(2)}) %collective-permute-start) | collective-permute-done | bytes 262176 | tf_op jit(solution)/shard_map/ppermute | solution.py:541
  13.2 0.3 shard_map.192
  13.5 0.0 collective-permute-done.2.beta_in
  13.5 0.0 collective-permute-done.3.alpha_in
  13.5 1.8 %shard_map.193 = (bf16[64,4096]{1,0:T(8,128)(2,1)S(1)}, f32[64,4096]{1,0:T(8,128)S(1)}, bf16[64,4096]{1,0:T(8,128)(2,1)S(1)}, bf16[64,64]{1,0:T(8,128)(2,1)S(1)}...) custom-call(f32[64,4096]{1,0:T(8,128)S(1)} %get-tuple-element.85.bas, ...), custom_call_target="tpu_custom_call" | custom-call | flops 2000000000 | bytes 7200000 | tf_op jit(solution)/shard_map/pallas_call | solution.py:526
  15.3 3.0 %collective-permute-start.4 = (bf16[64,128]{1,0:T(8,128)(2,1)S(1)}, bf16[64,128]{1,0:T(8,128)(2,1)S(1)}, u32[]{:S(2)}, u32[]{:S(2)}) collective-permute-start(bf16[64,128]{1,0:T(8,128)(2,1)S(1)} %get-tuple-element.98), channel_id=1, source_target_pairs={{0,30},{2,4},{4,2},{6,8},{8,6},{10,12},{12,10},{14,16},{16,14},{18... | collective-permute-start | bytes 49160 | tf_op jit(solution)/shard_map/ppermute | solution.py:541
  18.3 0.0 collective-permute-start.5
  18.3 1.0 %shard_map.194 = (f32[64,4096]{1,0:T(8,128)S(1)}, f32[64,64]{1,0:T(8,128)S(1)}) custom-call(bf16[64,4096]{1,0:T(8,128)(2,1)S(1)} %get-tuple-element.93.edges_ref, bf16[64,4096]{1,0:T(8,128)(2,1)S(1)} %get-tuple-element.94.hidden_ref.hidden_zero_ref, bf16[192,4096]{1,0:T(8,128)(2,1)S(1)} %get-tuple-element.86.onehot_ref, ...), custom_call_target="tpu_custom_call" | custom-call | flops 2000000000 | bytes 7200000 | tf_op jit(solution)/shard_map/pallas_call | solution.py:526
  19.3 1.9 %collective-permute-done.4.beta_in = bf16[64,128]{1,0:T(8,128)(2,1)S(1)} collective-permute-done((bf16[64,128]{1,0:T(8,128)(2,1)S(1)}, bf16[64,128]{1,0:T(8,128)(2,1)S(1)}, u32[]{:S(2)}, u32[]{:S(2)}) %collective-permute-start.4) | collective-permute-done | bytes 16416 | tf_op jit(solution)/shard_map/ppermute | solution.py:541
  21.2 0.0 collective-permute-done.5.alpha_in
  21.2 2.2 %shard_map.195 = (bf16[64,4096]{1,0:T(8,128)(2,1)S(1)}, bf16[64,4096]{1,0:T(8,128)(2,1)S(1)}, bf16[64,4096]{1,0:T(8,128)(2,1)S(1)}, bf16[128,64]{1,0:T(8,128)(2,...) custom-call(f32[64,4096]{1,0:T(8,128)S(1)} %get-tuple-element.97.bas, ...), custom_call_target="tpu_custom_call" | custom-call | flops 3000000000 | bytes 10800000 | tf_op jit(solution)/shard_map/pallas_call | solution.py:526
  23.4 0.0 collective-permute-start.7
  23.4 3.0 %collective-permute-start.6 = (bf16[64,64]{1,0:T(8,128)(2,1)S(1)}, bf16[64,64]{1,0:T(8,128)(2,1)S(1)}, u32[]{:S(2)}, u32[]{:S(2)}) collective-permute-start(bf16[64,64]{1,0:T(8,128)(2,1)S(1)} %get-tuple-element.119), channel_id=1, source_target_pairs={{0,30},{2,4},{4,2},{6,8},{8,6},{10,12},{12,10},{14,16},{16,14},{18... | collective-permute-start | bytes 24584 | tf_op jit(solution)/shard_map/ppermute | solution.py:541
  26.5 1.0 %shard_map.197 = (f32[64,4096]{1,0:T(8,128)S(1)}, f32[64,452]{1,0:T(8,128)S(1)}, f32[64,64]{1,0:T(8,128)S(1)}, f32[64,64]{1,0:T(8,128)S(1)}) custom-call(bf16[64,4096]{1,0:T(8,128)(2,1)S(1)} %get-tuple-element.108.low_ref, bf16[64,4096]{1,0:T(8,128)(2,1)S(1)} %get-tuple-element.94.hidden_ref.hidden_zero_ref, ...), custom_call_target="tpu_custom_call" | custom-call | flops 2000000000 | bytes 7200000 | tf_op jit(solution)/shard_map/pallas_call | solution.py:526
  27.5 0.0 collective-permute-done.7.alpha_in
  27.5 1.9 %collective-permute-done.6.beta_in = bf16[64,64]{1,0:T(8,128)(2,1)S(1)} collective-permute-done((bf16[64,64]{1,0:T(8,128)(2,1)S(1)}, bf16[64,64]{1,0:T(8,128)(2,1)S(1)}, u32[]{:S(2)}, u32[]{:S(2)}) %collective-permute-start.6) | collective-permute-done | bytes 8224 | tf_op jit(solution)/shard_map/ppermute | solution.py:541
  29.4 1.7 %shard_map.198 = (f32[32,452]{1,0:T(8,128)S(1)}, bf16[32,640]{1,0:T(8,128)(2,1)S(1)}, f32[64,64]{1,0:T(8,128)S(1)}) custom-call(f32[64,64]{1,0:T(8,128)S(1)} %get-tuple-element.117.back_in, f32[64,64]{1,0:T(8,128)S(1)} %get-tuple-element.118.back_node, bf16[64,64]{1,0:T(8,128)(2,1)S(1)} %collective-permute-done.6.beta_in, ...), custom_call_target="tpu_custom_call" | custom-call | flops 2000000000 | bytes 7200000 | tf_op jit(solution)/shard_map/pallas_call | solution.py:526
  31.1 0.1 collective-permute-start.8
  31.2 1.2 %collective-permute-done.8.other_ref.first_ref = bf16[32,640]{1,0:T(8,128)(2,1)S(1)} collective-permute-done((bf16[32,640]{1,0:T(8,128)(2,1)S(1)}, bf16[32,640]{1,0:T(8,128)(2,1)S(1)}, u32[]{:S(2)}, u32[]{:S(2)}) %collective-permute-start.8) | collective-permute-done | bytes 40992 | tf_op jit(solution)/shard_map/ppermute | solution.py:541
  32.4 0.1 shard_map.199.mine_ref
  32.5 0.0 collective-permute-start.9
  32.5 3.3 %collective-permute-done.9.other_ref = bf16[32,512]{1,0:T(8,128)(2,1)S(1)} collective-permute-done((bf16[32,512]{1,0:T(8,128)(2,1)S(1)}, bf16[32,512]{1,0:T(8,128)(2,1)S(1)}, u32[]{:S(2)}, u32[]{:S(2)}) %collective-permute-start.9) | collective-permute-done | bytes 32800 | tf_op jit(solution)/shard_map/ppermute | solution.py:541
  35.8 0.1 shard_map.200
  35.9 0.0 collective-permute-start.10
  35.9 3.3 %collective-permute-done.10.other_ref = bf16[32,512]{1,0:T(8,128)(2,1)S(1)} collective-permute-done((bf16[32,512]{1,0:T(8,128)(2,1)S(1)}, bf16[32,512]{1,0:T(8,128)(2,1)S(1)}, u32[]{:S(2)}, u32[]{:S(2)}) %collective-permute-start.10) | collective-permute-done | bytes 32800 | tf_op jit(solution)/shard_map/ppermute | solution.py:541
  39.3 0.1 shard_map.201
  39.4 0.3 collective-permute-start.11
  39.7 4.5 %collective-permute-done.11.other_ref = bf16[32,512]{1,0:T(8,128)(2,1)S(1)} collective-permute-done((bf16[32,512]{1,0:T(8,128)(2,1)S(1)}, bf16[32,512]{1,0:T(8,128)(2,1)S(1)}, u32[]{:S(2)}, u32[]{:S(2)}) %collective-permute-start.11) | collective-permute-done | bytes 32800 | tf_op jit(solution)/shard_map/ppermute | solution.py:541
  44.2 0.1 shard_map.202
  44.3 0.1 collective-permute-start.12
  44.5 0.9 %shard_map.196 = (bf16[64,2048]{1,0:T(8,128)(2,1)}, bf16[32,64]{1,0:T(8,128)(2,1)}) custom-call(s32[1,1]{1,0:T(1,128)S(6)} %copy.21.count_ref, bf16[64,4096]{1,0:T(8,128)(2,1)S(1)} %get-tuple-element.103.new_ref, bf16[128,64]{1,0:T(8,128)(2,1)S(1)} %get-tuple-element.104.joined_ref, f32[64,64]{1,0:T(8,128)S(1)} %get-tuple-element.105.node_pre_ref, ...), custom_call_target="tpu_custom_call" | custom-call | flops 2000000000 | bytes 7200000 | tf_op jit(solution)/shard_map/pallas_call | solution.py:526
  45.3 0.3 collective-permute-done.12.other_ref
  45.6 1.0 %shard_map.203 = (f32[32,64]{1,0:T(8,128)}, f32[64,192]{1,0:T(8,128)}, f32[64,64]{1,0:T(8,128)}, f32[64,128]{1,0:T(8,128)}, f32[64,64]{1,0:T(8,128)}, /*index=5*/f32[4,64]{1,0:T(4,128)}) custom-call(f32[32,512]{1,0:T(8,128)S(1)} %get-tuple-element.135.half_ref, f32[32,512]{1,0:T(8,128)S(1)} %collective-permute-done.12.other_ref, ...), custom_call_target="tpu_custom_call" | custom-call | flops 1000000000 | bytes 3600000 | tf_op jit(solution)/shard_map/pallas_call | solution.py:526
  (6 shorter events, 0.0 us)
Async XLA Ops:
  1.3 4.0 %copy-start = (bf16[64,2048]{1,0:T(8,128)(2,1)S(1)}, bf16[64,2048]{1,0:T(8,128)(2,1)}, u32[]{:S(2)}) copy-start(bf16[64,2048]{1,0:T(8,128)(2,1)} %refs_0_.1) | copy-start | bytes 786436
  2.2 4.8 %collective-permute-start.1 = (bf16[80,128]{1,0:T(8,128)(2,1)S(1)}, bf16[80,128]{1,0:T(8,128)(2,1)S(1)}, u32[]{:S(2)}, u32[]{:S(2)}) collective-permute-start(bf16[80,128]{1,0:T(8,128)(2,1)S(1)} %get-tuple-element.77.packed_ref.refs_0_), channel_id=1, source_target_pairs={{0,1},{1,0},{2,3},{3,2},{4,5},{5,4},{6,7},{7,6},{8,9},{9,8},{10,11... | collective-permute-start | bytes 61448 | tf_op jit(solution)/shard_map/ppermute | solution.py:541
  5.3 7.8 %collective-permute-start = (bf16[64,2048]{1,0:T(8,128)(2,1)S(1)}, bf16[64,2048]{1,0:T(8,128)(2,1)S(1)}, u32[]{:S(2)}, u32[]{:S(2)}) collective-permute-start(bf16[64,2048]{1,0:T(8,128)(2,1)S(1)} %copy-done), channel_id=1, source_target_pairs={{0,1},{1,0},{2,3},{3,2},{4,5},{5,4},{6,7},{7,6},{8,9},{9,8},{10,11... | collective-permute-start | bytes 786440 | tf_op jit(solution)/shard_map/ppermute | solution.py:541
  7.0 3.6 %copy-start.1 = (bf16[64,192]{1,0:T(8,128)(2,1)S(1)}, bf16[64,192]{1,0:T(8,128)(2,1)}, u32[]{:S(2)}) copy-start(bf16[64,192]{1,0:T(8,128)(2,1)} %first_ref.3) | copy-start | bytes 73732
  7.0 3.6 %copy-start.2 = (bf16[64,64]{1,0:T(8,128)(2,1)S(1)}, bf16[64,64]{1,0:T(8,128)(2,1)}, u32[]{:S(2)}) copy-start(bf16[64,64]{1,0:T(8,128)(2,1)} %second_ref.3) | copy-start | bytes 24580
  7.0 3.6 %copy-start.3 = (bf16[64,128]{1,0:T(8,128)(2,1)S(1)}, bf16[64,128]{1,0:T(8,128)(2,1)}, u32[]{:S(2)}) copy-start(bf16[64,128]{1,0:T(8,128)(2,1)} %node_first_ref.3) | copy-start | bytes 49156
  7.0 3.6 %copy-start.4 = (bf16[64,64]{1,0:T(8,128)(2,1)S(1)}, bf16[64,64]{1,0:T(8,128)(2,1)}, u32[]{:S(2)}) copy-start(bf16[64,64]{1,0:T(8,128)(2,1)} %node_second_ref.3) | copy-start | bytes 24580
  7.0 3.6 %copy-start.5 = (f32[4,64]{1,0:T(4,128)S(1)}, f32[4,64]{1,0:T(4,128)}, u32[]{:S(2)}) copy-start(f32[4,64]{1,0:T(4,128)} %refs_7_.1) | copy-start | bytes 3076
  7.2 6.3 %collective-permute-start.2 = (bf16[64,64]{1,0:T(8,128)(2,1)S(1)}, bf16[64,64]{1,0:T(8,128)(2,1)S(1)}, u32[]{:S(2)}, u32[]{:S(2)}) collective-permute-start(bf16[64,64]{1,0:T(8,128)(2,1)S(1)} %get-tuple-element.88), channel_id=1, source_target_pairs={{0,30},{2,4},{4,2},{6,8},{8,6},{10,12},{12,10},{14,16},{16,14},{18... | collective-permute-start | bytes 24584 | tf_op jit(solution)/shard_map/ppermute | solution.py:541
  10.6 2.9 %collective-permute-start.3 = (bf16[64,64]{1,0:T(8,128)(2,1)S(1)}, bf16[64,64]{1,0:T(8,128)(2,1)S(1)}, u32[]{:S(2)}, u32[]{:S(2)}) collective-permute-start(bf16[64,64]{1,0:T(8,128)(2,1)S(1)} %get-tuple-element.89), channel_id=1, source_target_pairs={{0,2},{2,0},{4,6},{6,4},{8,10},{10,8},{12,14},{14,12},{16,18},{18,... | collective-permute-start | bytes 24584 | tf_op jit(solution)/shard_map/ppermute | solution.py:541
  15.3 5.9 %collective-permute-start.4 = (bf16[64,128]{1,0:T(8,128)(2,1)S(1)}, bf16[64,128]{1,0:T(8,128)(2,1)S(1)}, u32[]{:S(2)}, u32[]{:S(2)}) collective-permute-start(bf16[64,128]{1,0:T(8,128)(2,1)S(1)} %get-tuple-element.98), channel_id=1, source_target_pairs={{0,30},{2,4},{4,2},{6,8},{8,6},{10,12},{12,10},{14,16},{16,14},{18... | collective-permute-start | bytes 49160 | tf_op jit(solution)/shard_map/ppermute | solution.py:541
  18.3 2.9 %collective-permute-start.5 = (bf16[64,128]{1,0:T(8,128)(2,1)S(1)}, bf16[64,128]{1,0:T(8,128)(2,1)S(1)}, u32[]{:S(2)}, u32[]{:S(2)}) collective-permute-start(bf16[64,128]{1,0:T(8,128)(2,1)S(1)} %get-tuple-element.99), channel_id=1, source_target_pairs={{0,2},{2,0},{4,6},{6,4},{8,10},{10,8},{12,14},{14,12},{16,18},{18,... | collective-permute-start | bytes 49160 | tf_op jit(solution)/shard_map/ppermute | solution.py:541
  23.4 4.1 %collective-permute-start.7 = (bf16[64,64]{1,0:T(8,128)(2,1)S(1)}, bf16[64,64]{1,0:T(8,128)(2,1)S(1)}, u32[]{:S(2)}, u32[]{:S(2)}) collective-permute-start(bf16[64,64]{1,0:T(8,128)(2,1)S(1)} %get-tuple-element.119), channel_id=1, source_target_pairs={{0,2},{2,0},{4,6},{6,4},{8,10},{10,8},{12,14},{14,12},{16,18},{18,... | collective-permute-start | bytes 24584 | tf_op jit(solution)/shard_map/ppermute | solution.py:541
  23.4 5.9 %collective-permute-start.6 = (bf16[64,64]{1,0:T(8,128)(2,1)S(1)}, bf16[64,64]{1,0:T(8,128)(2,1)S(1)}, u32[]{:S(2)}, u32[]{:S(2)}) collective-permute-start(bf16[64,64]{1,0:T(8,128)(2,1)S(1)} %get-tuple-element.119), channel_id=1, source_target_pairs={{0,30},{2,4},{4,2},{6,8},{8,6},{10,12},{12,10},{14,16},{16,14},{18... | collective-permute-start | bytes 24584 | tf_op jit(solution)/shard_map/ppermute | solution.py:541
  31.1 1.3 %collective-permute-start.8 = (bf16[32,640]{1,0:T(8,128)(2,1)S(1)}, bf16[32,640]{1,0:T(8,128)(2,1)S(1)}, u32[]{:S(2)}, u32[]{:S(2)}) collective-permute-start(bf16[32,640]{1,0:T(8,128)(2,1)S(1)} %get-tuple-element.130), channel_id=1, source_target_pairs={{0,2},{2,0},{4,6},{6,4},{8,10},{10,8},{12,14},{14,12},{16,18},{18,... | collective-permute-start | bytes 122888 | tf_op jit(solution)/shard_map/ppermute | solution.py:541
  32.5 3.4 %collective-permute-start.9 = (bf16[32,512]{1,0:T(8,128)(2,1)S(1)}, bf16[32,512]{1,0:T(8,128)(2,1)S(1)}, u32[]{:S(2)}, u32[]{:S(2)}) collective-permute-start(bf16[32,512]{1,0:T(8,128)(2,1)S(1)} %shard_map.199.mine_ref), channel_id=1, source_target_pairs={{0,6},{2,4},{4,2},{6,0},{8,14},{10,12},{12,10},{14,8},{16,22},{18,... | collective-permute-start | bytes 98312 | tf_op jit(solution)/shard_map/ppermute | solution.py:541
  35.9 3.3 %collective-permute-start.10 = (bf16[32,512]{1,0:T(8,128)(2,1)S(1)}, bf16[32,512]{1,0:T(8,128)(2,1)S(1)}, u32[]{:S(2)}, u32[]{:S(2)}) collective-permute-start(bf16[32,512]{1,0:T(8,128)(2,1)S(1)} %get-tuple-element.131.mine_ref), channel_id=1, source_target_pairs={{0,10},{2,8},{4,14},{6,12},{8,2},{10,0},{12,6},{14,4},{16,26},{18,... | collective-permute-start | bytes 98312 | tf_op jit(solution)/shard_map/ppermute | solution.py:541
  39.4 4.8 %collective-permute-start.11 = (bf16[32,512]{1,0:T(8,128)(2,1)S(1)}, bf16[32,512]{1,0:T(8,128)(2,1)S(1)}, u32[]{:S(2)}, u32[]{:S(2)}) collective-permute-start(bf16[32,512]{1,0:T(8,128)(2,1)S(1)} %get-tuple-element.132.mine_ref), channel_id=1, source_target_pairs={{0,18},{2,16},{4,22},{6,20},{8,26},{10,24},{12,30},{14,28},{16,2},... | collective-permute-start | bytes 98312 | tf_op jit(solution)/shard_map/ppermute | solution.py:541
  44.3 1.3 %collective-permute-start.12 = (f32[32,512]{1,0:T(8,128)S(1)}, f32[32,512]{1,0:T(8,128)S(1)}, u32[]{:S(2)}, u32[]{:S(2)}) collective-permute-start(f32[32,512]{1,0:T(8,128)S(1)} %get-tuple-element.135.half_ref), channel_id=1, source_target_pairs={{0,2},{2,0},{4,6},{6,4},{8,10},{10,8},{12,14},{14,12},{16,18},{18,... | collective-permute-start | bytes 196616 | tf_op jit(solution)/shard_map/ppermute | solution.py:541
